TPU v7x, 32 devices: a whole 2x2x4 slice. The times are simulated.
32 devices in a mesh: parts: 2 (over y), aux: 8 (over z, x), pair: 2 (over core).
Axes of the slice: x: 2, y: 2, z: 4, core: 2. Of those that a mesh axis runs over, the one named last changes fastest.
Arguments:
- pair_tensor: float32 [2016, 800], P(('parts', 'aux'), 'pair'), parts along dimension 0, may hold values from -0.625 to 0.625
- occ_energy: float32 [8], P(('parts', 'pair')), parts along dimension 0, may hold values from -1.2 to -0.3
- vir_energy: float32 [400], P('parts'), parts along dimension 0, may hold values from 0.1 to 3
- frequency: float32 [2], P('parts'), parts along dimension 0, may hold values from 0.1 to 4
Outputs:
- response: float32 [2016, 630], P(('parts', 'aux'), 'pair'), parts along dimension 0
There are 2 independent parts, one for each index of `parts`. A program takes and returns all parts, laid end to end along the dimension named above; each array names one. Nothing has to cross between parts.
All inputs are finite; a program needn't handle non-finite values.
Results may differ from a plain program's by a relative error of at most 0.0003.
Values sent between devices are 32-bit elements; how exact they have to be, the bound alone decides.
No kernel may reach another device: no remote copies, remote signals or barrier semaphores. Data moves between devices by JAX's collectives and lax.ppermute only.
A program may use at most 64 MiB of HBM per device.

v0:
```python
import jax
import jax.numpy as jnp
from jax import lax
from jax.sharding import PartitionSpec as P


def passed_along(value, axis, by):
    peers = lax.axis_size(axis)
    return lax.ppermute(value, axis, [(i, (i + by) % peers) for i in range(peers)])


def pair_weights(occ_energy, vir_energy, frequency):
    energy_gap = vir_energy[None, :] - occ_energy[:, None]
    return (4.0 * energy_gap / (energy_gap * energy_gap + frequency[0] * frequency[0])).reshape(-1)


def product_tile(scaled_rows, block_rows):
    return lax.dot_general(
        scaled_rows,
        block_rows,
        (((1,), (1,)), ((), ())),
        precision=lax.Precision.HIGHEST,
        preferred_element_type=jnp.float32,
    )


def write_block(collected, values, column):
    return lax.dynamic_update_slice_in_dim(collected, values, column, 1)


def half_turn(scaled_rows, first_block, half_span):
    row_count = scaled_rows.shape[0]
    collected = jnp.zeros((row_count, (half_span + 1) * row_count), jnp.float32)
    collected = write_block(collected, product_tile(scaled_rows, first_block), 0)
    opposite = passed_along(first_block, "aux", -half_span)
    collected = write_block(collected, product_tile(scaled_rows, opposite), half_span * row_count)

    def advance(turn_index, loop_state):
        collected, forward, backward = loop_state
        forward = passed_along(forward, "aux", -1)
        backward = passed_along(backward, "aux", 1)
        collected = write_block(
            collected, product_tile(scaled_rows, forward), turn_index * row_count
        )
        collected = write_block(
            collected, product_tile(scaled_rows, backward), (half_span - turn_index) * row_count
        )
        return (collected, forward, backward)

    collected, forward, backward = lax.fori_loop(
        1, half_span // 2, advance, (collected, first_block, opposite)
    )
    middle = passed_along(forward, "aux", -1)
    return write_block(collected, product_tile(scaled_rows, middle), half_span // 2 * row_count)


def shards(pair_tensor, occ_energy, vir_energy, frequency):
    n_aux = lax.axis_size("aux")
    scaled_rows = pair_tensor * pair_weights(occ_energy, vir_energy, frequency)[None, :]
    collected = half_turn(scaled_rows, pair_tensor, n_aux // 2)
    return lax.psum_scatter(collected, "pair", scatter_dimension=1, tiled=True)


def solution(mesh):
    in_specs = (P(("parts", "aux"), "pair"), P(("parts", "pair")), P("parts"), P("parts"))
    out_specs = P(("parts", "aux"), "pair")
    return jax.shard_map(shards, mesh=mesh, in_specs=in_specs, out_specs=out_specs, check_vma=False)
```

profile of v0, /device:TPU:0, one launch (start us, length us, event | category | flops | bytes accessed | tf_op | source)
XLA Modules:
  0.0 40.8 jit_solution(4964654855928829054)
XLA Ops:
  0.0 6.0 %collective-permute-start.1 = (f32[126,400]{0,1:T(8,128)}, f32[126,400]{0,1:T(8,128)S(1)}, u32[]{:S(2)}, u32[]{:S(2)}) collective-permute-start(f32[126,400]{0,1:T(8,128)} %param.4), channel_id=1, source_target_pairs={{0,14},{2,0},{4,2},{6,4},{8,6},{10,8},{12,10},{14,12},{1,15},{3,1}... | collective-permute-start | bytes 604808 | tf_op jit(solution)/shard_map/while/body/eval_jaxpr/ppermute | solution.py:9
  6.0 0.0 collective-permute-start
  6.6 0.0 copy-start.1
  6.6 0.0 copy-start.3
  6.7 0.7 %copy-done.1 = f32[200]{0:T(256)S(1)} copy-done((f32[200]{0:T(256)S(1)}, f32[200]{0:T(256)}, u32[]{:S(2)}) %copy-start.1) | copy-done | bytes 824
  7.3 0.0 copy-done.3
  7.3 0.1 fusion.15
  7.4 0.1 div.11
  7.5 1.8 %fusion.8 = f32[126,126]{0,1:T(8,128)S(1)} fusion(f32[126,400]{0,1:T(8,128)} %param.4, f32[400]{0:T(512)S(1)} %div.11), kind=kOutput, calls=%fused_computation.8 | convolution fusion | flops 76255200 | bytes 266704 | tf_op jit(solution)/shard_map/dot_general | solution.py:18
  9.2 0.0 copy-start
  9.3 2.5 %collective-permute-done.1 = f32[126,400]{0,1:T(8,128)S(1)} collective-permute-done((f32[126,400]{0,1:T(8,128)}, f32[126,400]{0,1:T(8,128)S(1)}, u32[]{:S(2)}, u32[]{:S(2)}) %collective-permute-start.1) | collective-permute-done | bytes 201632 | tf_op jit(solution)/shard_map/while/body/eval_jaxpr/ppermute | solution.py:9
  11.8 0.0 copy-done
  11.8 0.7 %fusion.5 = f32[126,126]{0,1:T(8,128)S(1)} fusion(f32[126,400]{0,1:T(8,128)S(1)} %collective-permute-done.1, f32[126,400]{0,1:T(8,128)S(1)} %copy-done, f32[400]{0:T(512)S(1)} %div.11), kind=kOutput, calls=%fused_computation.5 | convolution fusion | flops 76255200 | bytes 468304 | tf_op jit(solution)/shard_map/while/body/eval_jaxpr/dot_general | solution.py:18
  12.5 6.7 %collective-permute-done = f32[126,400]{0,1:T(8,128)S(1)} collective-permute-done((f32[126,400]{0,1:T(8,128)}, f32[126,400]{0,1:T(8,128)S(1)}, u32[]{:S(2)}, u32[]{:S(2)}) %collective-permute-start) | collective-permute-done | bytes 201632 | tf_op jit(solution)/shard_map/ppermute | solution.py:9
  19.2 0.0 collective-permute-start.2
  19.2 0.7 %convolution_dynamic-update-slice_fusion = f32[126,630]{0,1:T(8,128)S(1)} fusion(f32[126,630]{0,1:T(8,128)S(1)} %dynamic_update_slice.17, f32[126,400]{0,1:T(8,128)S(1)} %collective-permute-done, f32[126,400]{0,1:T(8,128)S(1)} %copy-done, f32[400]{0:T(512)S(1)} %div.11), kind=kOutput, calls=%fused_computation | convolution fusion | flops 76255200 | bytes 477184 | tf_op jit(solution)/shard_map/dot_general | solution.py:18
  19.9 0.6 %dynamic_update_slice.19 = f32[126,630]{0,1:T(8,128)S(1)} dynamic-update-slice(f32[126,630]{0,1:T(8,128)S(1)} %convolution_dynamic-update-slice_fusion, f32[126,126]{0,1:T(8,128)S(1)} %fusion.5, s32[]{:T(128)} %constant.25.clone.1, s32[]{:T(128)} %constant.27.clone.1) | dynamic-update-slice | bytes 127012 | tf_op jit(solution)/shard_map/while/body/eval_jaxpr/dynamic_update_slice | solution.py:28
  20.5 4.8 %collective-permute-start.3 = (f32[126,400]{0,1:T(8,128)S(1)}, f32[126,400]{0,1:T(8,128)S(1)}, u32[]{:S(2)}, u32[]{:S(2)}) collective-permute-start(f32[126,400]{0,1:T(8,128)S(1)} %collective-permute-done.1), channel_id=1, source_target_pairs={{0,14},{2,0},{4,2},{6,4},{8,6},{10,8},{12,10},{14,12},{1,15},{3,1}... | collective-permute-start | bytes 604808 | tf_op jit(solution)/shard_map/ppermute | solution.py:9
  25.3 2.7 %collective-permute-done.2 = f32[126,400]{0,1:T(8,128)S(1)} collective-permute-done((f32[126,400]{0,1:T(8,128)S(1)}, f32[126,400]{0,1:T(8,128)S(1)}, u32[]{:S(2)}, u32[]{:S(2)}) %collective-permute-start.2) | collective-permute-done | bytes 201632 | tf_op jit(solution)/shard_map/while/body/eval_jaxpr/ppermute | solution.py:9
  27.9 0.7 %fusion.3 = f32[126,126]{0,1:T(8,128)S(1)} fusion(f32[126,400]{0,1:T(8,128)S(1)} %collective-permute-done.2, f32[126,400]{0,1:T(8,128)S(1)} %copy-done, f32[400]{0:T(512)S(1)} %div.11), kind=kOutput, calls=%fused_computation.3 | convolution fusion | flops 76255200 | bytes 468304 | tf_op jit(solution)/shard_map/while/body/eval_jaxpr/dot_general | solution.py:18
  28.7 0.6 %dynamic_update_slice.20 = f32[126,630]{0,1:T(8,128)S(1)} dynamic-update-slice(f32[126,630]{0,1:T(8,128)S(1)} %dynamic_update_slice.19, f32[126,126]{0,1:T(8,128)S(1)} %fusion.3, s32[]{:T(128)} %constant.25.clone.1, s32[]{:T(128)} %constant.28.clone.1) | dynamic-update-slice | bytes 127012 | tf_op jit(solution)/shard_map/while/body/eval_jaxpr/dynamic_update_slice | solution.py:28
  29.3 2.3 %collective-permute-done.3 = f32[126,400]{0,1:T(8,128)S(1)} collective-permute-done((f32[126,400]{0,1:T(8,128)S(1)}, f32[126,400]{0,1:T(8,128)S(1)}, u32[]{:S(2)}, u32[]{:S(2)}) %collective-permute-start.3) | collective-permute-done | bytes 201632 | tf_op jit(solution)/shard_map/ppermute | solution.py:9
  31.5 0.7 %fusion.1 = f32[126,126]{0,1:T(8,128)S(1)} fusion(f32[126,400]{0,1:T(8,128)S(1)} %collective-permute-done.3, f32[126,400]{0,1:T(8,128)S(1)} %copy-done, f32[400]{0:T(512)S(1)} %div.11), kind=kOutput, calls=%fused_computation.1 | convolution fusion | flops 76255200 | bytes 468304 | tf_op jit(solution)/shard_map/dot_general | solution.py:18
  32.3 0.6 %dynamic_update_slice.21 = f32[126,630]{0,1:T(8,128)S(1)} dynamic-update-slice(f32[126,630]{0,1:T(8,128)S(1)} %dynamic_update_slice.20, f32[126,126]{0,1:T(8,128)S(1)} %fusion.1, s32[]{:T(128)} %constant.25.clone.1, s32[]{:T(128)} %constant.29.clone.1) | dynamic-update-slice | bytes 127012 | tf_op jit(solution)/shard_map/dynamic_update_slice | solution.py:28
  32.9 3.2 %fusion = f32[126,320]{0,1:T(8,128)S(1)} fusion(f32[126,630]{0,1:T(8,128)S(1)} %dynamic_update_slice.21), kind=kCustom, calls=%all-reduce-scatter | all-reduce-scatter fusion | flops 80641 | bytes 479312
  36.0 0.0 copy-start.2
  36.1 2.3 %collective-permute-start.4 = (f32[126,5]{0,1:T(8,128)S(1)}, f32[126,5]{0,1:T(8,128)S(1)}, u32[]{:S(2)}, u32[]{:S(2)}) collective-permute-start(f32[126,5]{0,1:T(8,128)S(1)} %slice), channel_id=1, source_target_pairs={{0,1},{2,3},{4,5},{6,7},{8,9},{10,11},{12,13},{14,15},{16,17},{18,... | collective-permute-start | bytes 7568
  38.3 0.0 copy-done.2
  38.3 0.6 %dynamic-slice.4 = u32[1]{0:T(128)} dynamic-slice(u32[32]{0:T(128)S(1)} %copy-done.2, u32[]{:S(6)} %partition-id.2), dynamic_slice_sizes={1} | dynamic-slice | bytes 12
  39.6 0.0 collective-permute-done.4
  39.6 0.5 %concatenate = f32[126,325]{0,1:T(8,128)S(1)} concatenate(f32[126,5]{0,1:T(8,128)S(1)} %collective-permute-done.4, f32[126,320]{0,1:T(8,128)S(1)} %fusion), dimensions={1} | concatenate | bytes 327600
  40.1 0.7 %constant_dynamic-slice_fusion = f32[126,315]{0,1:T(8,128)} fusion(f32[126,325]{0,1:T(8,128)S(1)} %concatenate, u32[]{:S(6)} %subtract), kind=kLoop, calls=%fused_computation.15 | loop fusion | bytes 317524
  (2 shorter events, 0.0 us)
Async XLA Ops:
  0.0 11.8 %collective-permute-start.1 = (f32[126,400]{0,1:T(8,128)}, f32[126,400]{0,1:T(8,128)S(1)}, u32[]{:S(2)}, u32[]{:S(2)}) collective-permute-start(f32[126,400]{0,1:T(8,128)} %param.4), channel_id=1, source_target_pairs={{0,14},{2,0},{4,2},{6,4},{8,6},{10,8},{12,10},{14,12},{1,15},{3,1}... | collective-permute-start | bytes 604808 | tf_op jit(solution)/shard_map/while/body/eval_jaxpr/ppermute | solution.py:9
  6.0 13.2 %collective-permute-start = (f32[126,400]{0,1:T(8,128)}, f32[126,400]{0,1:T(8,128)S(1)}, u32[]{:S(2)}, u32[]{:S(2)}) collective-permute-start(f32[126,400]{0,1:T(8,128)} %param.4), channel_id=1, source_target_pairs={{0,8},{2,10},{4,12},{6,14},{8,0},{10,2},{12,4},{14,6},{1,9},{3,11}... | collective-permute-start | bytes 604808 | tf_op jit(solution)/shard_map/ppermute | solution.py:9
  6.6 0.7 %copy-start.1 = (f32[200]{0:T(256)S(1)}, f32[200]{0:T(256)}, u32[]{:S(2)}) copy-start(f32[200]{0:T(256)} %param.6) | copy-start | bytes 2404
  6.6 0.7 %copy-start.3 = (f32[2]{0:T(128)S(1)}, f32[2]{0:T(128)}, u32[]{:S(2)}) copy-start(f32[2]{0:T(128)} %param.5) | copy-start | bytes 28
  9.2 2.5 %copy-start = (f32[126,400]{0,1:T(8,128)S(1)}, f32[126,400]{0,1:T(8,128)}, u32[]{:S(2)}) copy-start(f32[126,400]{0,1:T(8,128)} %param.4) | copy-start | bytes 604804
  19.2 8.8 %collective-permute-start.2 = (f32[126,400]{0,1:T(8,128)S(1)}, f32[126,400]{0,1:T(8,128)S(1)}, u32[]{:S(2)}, u32[]{:S(2)}) collective-permute-start(f32[126,400]{0,1:T(8,128)S(1)} %collective-permute-done), channel_id=1, source_target_pairs={{0,2},{2,4},{4,6},{6,8},{8,10},{10,12},{12,14},{14,0},{1,3},{3,5},... | collective-permute-start | bytes 604808 | tf_op jit(solution)/shard_map/while/body/eval_jaxpr/ppermute | solution.py:9
  20.5 11.0 %collective-permute-start.3 = (f32[126,400]{0,1:T(8,128)S(1)}, f32[126,400]{0,1:T(8,128)S(1)}, u32[]{:S(2)}, u32[]{:S(2)}) collective-permute-start(f32[126,400]{0,1:T(8,128)S(1)} %collective-permute-done.1), channel_id=1, source_target_pairs={{0,14},{2,0},{4,2},{6,4},{8,6},{10,8},{12,10},{14,12},{1,15},{3,1}... | collective-permute-start | bytes 604808 | tf_op jit(solution)/shard_map/ppermute | solution.py:9
  36.0 2.3 %copy-start.2 = (u32[32]{0:T(128)S(1)}, u32[32]{0:T(128)}, u32[]{:S(2)}) copy-start(u32[32]{0:T(128)} %constant.37) | copy-start | bytes 388
  36.1 3.5 %collective-permute-start.4 = (f32[126,5]{0,1:T(8,128)S(1)}, f32[126,5]{0,1:T(8,128)S(1)}, u32[]{:S(2)}, u32[]{:S(2)}) collective-permute-start(f32[126,5]{0,1:T(8,128)S(1)} %slice), channel_id=1, source_target_pairs={{0,1},{2,3},{4,5},{6,7},{8,9},{10,11},{12,13},{14,15},{16,17},{18,... | collective-permute-start | bytes 7568
where the time goes:
time: 41 us; the launch traced here: 40.8 us
  waiting for transfers between devices  14.1 us (34%)
  starting transfers between devices  13 us (32%)
  matrix products  4.67 us (11%)
  local copies, waits for them, and re-layouts  4.26 us (10%)
  blocking collectives  3.17 us (8%)
  between operations  1.44 us (4%)
    ppermute x4, waiting for transfers between devices, passed_along(): lax.ppermute(value, axis, [(i, (i + by) % peers) for i in range(peers)])  14.1 us
    ppermute x4, starting transfers between devices, passed_along(): lax.ppermute(value, axis, [(i, (i + by) % peers) for i in range(peers)])  10.8 us
    dot_general x5, matrix products, product_tile(): lax.dot_general(scaled_rows, block_rows, (((1,), (1,)), ((), ())), precis...  4.67 us
    unnamed x1, blocking collectives  3.17 us
    unnamed x12, local copies, waits for them, and re-layouts  2.45 us
    unnamed x1, starting transfers between devices  2.27 us
    dynamic_update_slice x4, local copies, waits for them, and re-layouts, write_block(): return lax.dynamic_update_slice_in_dim(collected, values, column, 1)  1.73 us
  transfers between devices with their start and end apart: 5, of which 4 were waited for; matrix products, arithmetic and copies ran while one was open for 14% of the time, Pallas kernels for 0%

commit v1 on v0

--- a/solution.py
+++ b/solution.py
@@ -1,6 +1,8 @@
 import jax
 import jax.numpy as jnp
 from jax import lax
+from jax.experimental import pallas as pl
+from jax.experimental.pallas import tpu as pltpu
 from jax.sharding import PartitionSpec as P
 
 
@@ -54,14 +56,236 @@
     return write_block(collected, product_tile(scaled_rows, middle), half_span // 2 * row_count)
 
 
-def shards(pair_tensor, occ_energy, vir_energy, frequency):
+def ring_shards(pair_tensor, occ_energy, vir_energy, frequency):
     n_aux = lax.axis_size("aux")
     scaled_rows = pair_tensor * pair_weights(occ_energy, vir_energy, frequency)[None, :]
     collected = half_turn(scaled_rows, pair_tensor, n_aux // 2)
     return lax.psum_scatter(collected, "pair", scatter_dimension=1, tiled=True)
 
 
+def sent(value, target_of):
+    pairs = []
+    for z in range(4):
+        for x in range(2):
+            for c in range(2):
+                target = target_of(z, x, c)
+                if target is not None:
+                    tz, tx, tc = target
+                    pairs.append(((z * 2 + x) * 2 + c, (tz * 2 + tx) * 2 + tc))
+    return lax.ppermute(value, ("aux", "pair"), pairs)
+
+
+def to_other_core(z, x, c):
+    return (z, x, 1 - c)
+
+
+def far_of_odd_xp_of_even(z, x, c):
+    return (z ^ 2, x, c) if z % 2 else (z, 1 - x, c)
+
+
+def far_of_even_xp_of_odd(z, x, c):
+    return (z, 1 - x, c) if z % 2 else (z ^ 2, 1 - x, c)
+
+
+def neighbour(z, x, c):
+    return (z ^ 1, x, c)
+
+
+def early_tile(z, x, c):
+    if z % 2:
+        return (z ^ 2, x, c)
+    return (z, 1 - x, c) if x == c else None
+
+
+def late_tile(z, x, c):
+    if z % 2:
+        return (z, 1, 1) if (x, c) == (0, 1) else None
+    return (z, 1 - x, 1) if x == c else (z ^ 1, x, 1 - x)
+
+
+def place():
+    block = lax.axis_index("aux")
+    return lax.rem(block // 2, 2) == 0, lax.rem(block, 2), lax.axis_index("pair")
+
+
+def halves(value):
+    high = value.astype(jnp.bfloat16)
+    return high, (value - high.astype(jnp.float32)).astype(jnp.bfloat16)
+
+
+def summed_over_pairs(left, right):
+    left_high, left_low = left
+    right_high, right_low = right
+    return lax.dot_general(
+        jnp.concatenate([left_high, left_low, left_high], 0),
+        jnp.concatenate([right_high, right_high, right_low], 0),
+        (((0,), (0,)), ((), ())),
+        preferred_element_type=jnp.float32,
+    )
+
+
+def tile_of(left_blocks, right_blocks):
+    total = None
+    for left, right in zip(left_blocks, right_blocks):
+        part = summed_over_pairs(halves(left), halves(right))
+        total = part if total is None else total + part
+    return total
+
+
+def early_kernel(weight, weight2, zn, zn2, a, a2, tile):
+    tile[...] = tile_of(
+        (zn[...], zn2[...]), (a[...] * weight[...], a2[...] * weight2[...])
+    )
+
+
+def local_kernel(weight, weight2, own, own2, zn, zn2, a, a2, own_own, a_own, zn_own):
+    scaled = (own[...] * weight[...], own2[...] * weight2[...])
+    own_own[...] = tile_of((own[...], own2[...]), scaled)
+    a_own[...] = tile_of((a[...], a2[...]), scaled)
+    zn_own[...] = tile_of((zn[...], zn2[...]), scaled)
+
+
+def late_kernel(weight, weight2, zn, zn2, a, a2, b, b2, tile):
+    even, x, c = place()
+    b_blocks = (b[...], b2[...])
+
+    @pl.when(even & (x == c))
+    def _():
+        tile[...] = tile_of(b_blocks, (a[...] * weight[...], a2[...] * weight2[...]))
+
+    @pl.when(even & (x != c))
+    def _():
+        tile[...] = tile_of(b_blocks, (zn[...] * weight[...], zn2[...] * weight2[...]))
+
+    @pl.when(~even)
+    def _():
+        tile[...] = tile_of((a[...] * weight[...], a2[...] * weight2[...]), b_blocks)
+
+
+def gather_kernel(weight, weight2, own, own2, b, b2, own_own, a_own, zn_own, early, kept):
+    even, x, c = place()
+    rows = own_own.shape[0]
+    half = rows // 2
+
+    @pl.when(c == 0)
+    def _():
+        kept[pl.ds(0, rows), :] = own_own[...]
+
+        @pl.when(even & (x == 0))
+        def _():
+            kept[pl.ds(rows, rows), :] = a_own[...]
+
+        @pl.when(even & (x == 1))
+        def _():
+            kept[pl.ds(rows, rows), :] = early[...]
+
+        @pl.when(~even)
+        def _():
+            kept[pl.ds(rows, rows), :] = tile_of(
+                (b[...], b2[...]), (own[...] * weight[...], own2[...] * weight2[...])
+            )
+
+        @pl.when(even)
+        def _():
+            kept[pl.ds(2 * rows, half), :] = zn_own[pl.ds(0, half), :]
+
+        @pl.when(~even)
+        def _():
+            kept[pl.ds(2 * rows, half), :] = early[pl.ds(0, half), :]
+
+    @pl.when(c == 1)
+    def _():
+        @pl.when(even)
+        def _():
+            kept[pl.ds(0, half), :] = zn_own[pl.ds(half, half), :]
+
+        @pl.when(~even)
+        def _():
+            kept[pl.ds(0, half), :] = early[pl.ds(half, half), :]
+
+        @pl.when(even & (x == 0))
+        def _():
+            kept[pl.ds(half, rows), :] = early[...]
+
+        @pl.when(even & (x == 1))
+        def _():
+            kept[pl.ds(half, rows), :] = tile_of(
+                (b[...], b2[...]), (own[...] * weight[...], own2[...] * weight2[...])
+            )
+
+        @pl.when(~even)
+        def _():
+            kept[pl.ds(half, rows), :] = a_own[...]
+
+        kept[pl.ds(half + rows, rows), :] = a_own[...]
+
+
+def finish_kernel(kept, late, response):
+    even, x, c = place()
+    rows = late.shape[0]
+    half = rows // 2
+    response[...] = kept[...]
+
+    @pl.when((c == 0) & ~even & (x == 1))
+    def _():
+        response[pl.ds(rows, rows), :] = late[...]
+
+    @pl.when((c == 1) & even)
+    def _():
+        response[pl.ds(half + rows, rows), :] = late[...]
+
+    @pl.when((c == 1) & ~even)
+    def _():
+        response[pl.ds(half, rows), :] = late[...]
+
+
+def in_vmem(kernel, shapes, *operands):
+    whole = pl.BlockSpec(memory_space=pltpu.VMEM)
+    out_shape = [jax.ShapeDtypeStruct(shape, jnp.float32) for shape in shapes]
+    return pl.pallas_call(
+        kernel,
+        out_shape=out_shape,
+        in_specs=[whole] * len(operands),
+        out_specs=[whole] * len(shapes),
+        compiler_params=pltpu.CompilerParams(vmem_limit_bytes=32 * 1024 * 1024),
+    )(*operands)
+
+
+def octet_shards(pair_tensor, occ_energy, vir_energy, frequency):
+    own = pair_tensor.T
+    pairs, rows = own.shape
+    a = sent(own, far_of_odd_xp_of_even)
+    b = sent(own, far_of_even_xp_of_odd)
+    zn = sent(own, neighbour)
+    own2 = sent(own, to_other_core)
+    occ_energy2 = sent(occ_energy, to_other_core)
+    weight, weight2 = (
+        jnp.broadcast_to(pair_weights(e, vir_energy, frequency)[:, None], (pairs, rows))
+        for e in (occ_energy, occ_energy2)
+    )
+    weights = (weight, weight2)
+    a_both = (a, sent(a, to_other_core))
+    zn_both = (zn, sent(zn, to_other_core))
+    square = (rows, rows)
+    (early,) = in_vmem(early_kernel, [square], *weights, *zn_both, *a_both)
+    early = sent(early, early_tile)
+    own_own, a_own, zn_own = in_vmem(
+        local_kernel, [square] * 3, *weights, own, own2, *zn_both, *a_both
+    )
+    b_both = (b, sent(b, to_other_core))
+    (late,) = in_vmem(late_kernel, [square], *weights, *zn_both, *a_both, *b_both)
+    late = sent(late, late_tile)
+    kept_shape = (5 * rows // 2, rows)
+    (kept,) = in_vmem(
+        gather_kernel, [kept_shape], *weights, own, own2, *b_both, own_own, a_own, zn_own, early
+    )
+    (response,) = in_vmem(finish_kernel, [kept_shape], kept, late)
+    return response.T
+
+
 def solution(mesh):
     in_specs = (P(("parts", "aux"), "pair"), P(("parts", "pair")), P("parts"), P("parts"))
     out_specs = P(("parts", "aux"), "pair")
+    octet = mesh.shape["aux"] == 8 and mesh.shape["pair"] == 2
+    shards = octet_shards if octet else ring_shards
     return jax.shard_map(shards, mesh=mesh, in_specs=in_specs, out_specs=out_specs, check_vma=False)

time: 41 us -> 27.1 us (0.66)
  matrix products: 4.67 us -> 0 us
  waiting for transfers between devices: 14.1 us -> 9.98 us
  local copies, waits for them, and re-layouts: 4.26 us -> 0.4 us
  blocking collectives: 3.17 us -> 0 us
  Pallas kernels: 0 us -> 2.32 us
  between operations: 1.44 us -> 0.77 us
    dot_general x5 -> x0, matrix products: 4.67 us -> none  [product_tile(): lax.dot_general(scaled_rows, block_rows, (((1,), (1,)), ((), ())), precis...]
    ppermute x4 -> x10, waiting for transfers between devices: 14.1 us -> 9.98 us  [sent(): return lax.ppermute(value, ('aux', 'pair'), pairs)]
    unnamed x1 -> x0, blocking collectives: 3.17 us -> none
    ppermute x4 -> x10, starting transfers between devices: 10.8 us -> 13.4 us  [sent(): return lax.ppermute(value, ('aux', 'pair'), pairs)]
    unnamed x12 -> x6, local copies, waits for them, and re-layouts: 2.45 us -> 0.01 us
    pallas_call x0 -> x5, Pallas kernels: none -> 2.32 us  [in_vmem(): pl.pallas_call(kernel, out_shape=out_shape, in_specs=[whole] * len(operan...]
    unnamed x1 -> x0, starting transfers between devices: 2.27 us -> none
    dynamic_update_slice x4 -> x0, local copies, waits for them, and re-layouts: 1.73 us -> none  [write_block(): return lax.dynamic_update_slice_in_dim(collected, values, column, 1)]
  transfers between devices with their start and end apart: 5 -> 10, of which waited for: 4 -> 4; matrix products, arithmetic and copies ran while one was open for 14% -> 2% of each run, Pallas kernels for 0% -> 6%
where the time goes in v1:
time: 27.1 us; the launch traced here: 27 us
  starting transfers between devices  13.4 us (49%)
  waiting for transfers between devices  9.98 us (37%)
  Pallas kernels  2.32 us (9%)
  between operations  0.77 us (3%)
  local copies, waits for them, and re-layouts  0.4 us (1%)
    ppermute x10, starting transfers between devices, sent(): return lax.ppermute(value, ('aux', 'pair'), pairs)  13.4 us
    ppermute x10, waiting for transfers between devices, sent(): return lax.ppermute(value, ('aux', 'pair'), pairs)  9.98 us
    pallas_call x5, Pallas kernels, in_vmem(): pl.pallas_call(kernel, out_shape=out_shape, in_specs=[whole] * len(operan...  2.32 us
  transfers between devices with their start and end apart: 10, of which 4 were waited for; matrix products, arithmetic and copies ran while one was open for 2% of the time, Pallas kernels for 6%

profile of v1, /device:TPU:0, one launch (start us, length us, event | category | flops | bytes accessed | tf_op | source)
XLA Modules:
  0.0 27.0 jit_solution(8821608343361126003)
XLA Ops:
  0.0 3.0 %collective-permute-start.4 = (f32[400,126]{1,0:T(8,128)}, f32[400,126]{1,0:T(8,128)S(1)}, u32[]{:S(2)}, u32[]{:S(2)}) collective-permute-start(f32[400,126]{1,0:T(8,128)} %bitcast.3), channel_id=1, source_target_pairs={{0,4},{1,5},{2,6},{3,7},{4,0},{5,1},{6,2},{7,3},{8,12},{9,13},{10,... | collective-permute-start | bytes 604808 | tf_op jit(solution)/shard_map/ppermute | solution.py:75
  3.0 1.5 %collective-permute-start.6 = (f32[400,126]{1,0:T(8,128)}, f32[400,126]{1,0:T(8,128)S(1)}, u32[]{:S(2)}, u32[]{:S(2)}) collective-permute-start(f32[400,126]{1,0:T(8,128)} %bitcast.4), channel_id=1, source_target_pairs={{0,2},{1,3},{2,0},{3,1},{4,12},{5,13},{6,14},{7,15},{8,10},{9,11},... | collective-permute-start | bytes 604808 | tf_op jit(solution)/shard_map/ppermute | solution.py:75
  4.5 2.6 %collective-permute-start.2 = (f32[400,126]{1,0:T(8,128)}, f32[400,126]{1,0:T(8,128)S(1)}, u32[]{:S(2)}, u32[]{:S(2)}) collective-permute-start(f32[400,126]{1,0:T(8,128)} %bitcast.5), channel_id=1, source_target_pairs={{0,10},{1,11},{2,8},{3,9},{4,6},{5,7},{6,4},{7,5},{8,2},{9,3},{10,... | collective-permute-start | bytes 604808 | tf_op jit(solution)/shard_map/ppermute | solution.py:75
  7.1 0.0 collective-permute-start.1
  7.1 0.5 %collective-permute-start = (f32[2]{0:T(128)S(1)}, f32[2]{0:T(128)S(1)}, u32[]{:S(2)}, u32[]{:S(2)}) collective-permute-start(f32[2]{0:T(128)S(1)} %copy-done.2), channel_id=1, source_target_pairs={{0,1},{1,0},{2,3},{3,2},{4,5},{5,4},{6,7},{7,6},{8,9},{9,8},{10,11... | collective-permute-start | bytes 32 | tf_op jit(solution)/shard_map/ppermute | solution.py:75
  8.2 0.0 copy-start.1
  8.3 2.7 %collective-permute-done.4.zn = f32[400,126]{1,0:T(8,128)S(1)} collective-permute-done((f32[400,126]{1,0:T(8,128)}, f32[400,126]{1,0:T(8,128)S(1)}, u32[]{:S(2)}, u32[]{:S(2)}) %collective-permute-start.4) | collective-permute-done | bytes 201632 | tf_op jit(solution)/shard_map/ppermute | solution.py:75
  10.9 0.0 collective-permute-start.5
  10.9 1.9 %collective-permute-done.6.a = f32[400,126]{1,0:T(8,128)S(1)} collective-permute-done((f32[400,126]{1,0:T(8,128)}, f32[400,126]{1,0:T(8,128)S(1)}, u32[]{:S(2)}, u32[]{:S(2)}) %collective-permute-start.6) | collective-permute-done | bytes 201632 | tf_op jit(solution)/shard_map/ppermute | solution.py:75
  12.9 0.0 collective-permute-start.7
  12.9 4.3 %collective-permute-done.2.b = f32[400,126]{1,0:T(8,128)S(1)} collective-permute-done((f32[400,126]{1,0:T(8,128)}, f32[400,126]{1,0:T(8,128)S(1)}, u32[]{:S(2)}, u32[]{:S(2)}) %collective-permute-start.2) | collective-permute-done | bytes 201632 | tf_op jit(solution)/shard_map/ppermute | solution.py:75
  17.2 0.0 collective-permute-start.3
  17.2 0.0 collective-permute-done
  17.2 0.1 fusion.2
  17.3 0.1 div.21
  17.4 0.1 div.23
  17.5 0.0 collective-permute-done.5.zn2
  17.5 0.0 collective-permute-done.7.a2
  17.5 0.1 broadcast_in_dim.4.weight
  17.6 0.1 broadcast_in_dim.5.weight2
  17.7 0.4 %shard_map.47 = f32[126,126]{1,0:T(8,128)S(1)} custom-call(f32[400,126]{1,0:T(8,128)S(1)} %broadcast_in_dim.4.weight, f32[400,126]{1,0:T(8,128)S(1)} %broadcast_in_dim.5.weight2, f32[400,126]{1,0:T(8,128)S(1)} %collective-permute-done.4.zn, f32[400,126]{1,0:T(8,128)S(1)} %collective-permute-done.5.zn2, f32[400,126]{1,0:T(8,128)S(1)} %collective-permute-done.6.a, ...), custom_call_target="tpu_custom_call" | custom-call | tf_op jit(solution)/shard_map/pallas_call | solution.py:245
  18.1 0.0 copy-start
  18.1 2.6 %collective-permute-start.8 = (f32[126,126]{1,0:T(8,128)S(1)}, f32[126,126]{1,0:T(8,128)S(1)}, u32[]{:S(2)}, u32[]{:S(2)}) collective-permute-start(f32[126,126]{1,0:T(8,128)S(1)} %shard_map.47), channel_id=1, source_target_pairs={{0,2},{3,1},{4,12},{5,13},{6,14},{7,15},{8,10},{11,9},{12,4},{13,5... | collective-permute-start | bytes 190520 | tf_op jit(solution)/shard_map/ppermute | solution.py:75
  20.7 0.0 collective-permute-done.3.b2
  20.7 0.4 %shard_map.49 = f32[126,126]{1,0:T(8,128)S(1)} custom-call(f32[400,126]{1,0:T(8,128)S(1)} %broadcast_in_dim.4.weight, f32[400,126]{1,0:T(8,128)S(1)} %broadcast_in_dim.5.weight2, f32[400,126]{1,0:T(8,128)S(1)} %collective-permute-done.4.zn, f32[400,126]{1,0:T(8,128)S(1)} %collective-permute-done.5.zn2, f32[400,126]{1,0:T(8,128)S(1)} %collective-permute-done.6.a, ...), custom_call_target="tpu_custom_call" | custom-call | tf_op jit(solution)/shard_map/pallas_call | solution.py:245
  21.1 3.2 %collective-permute-start.9 = (f32[126,126]{1,0:T(8,128)S(1)}, f32[126,126]{1,0:T(8,128)S(1)}, u32[]{:S(2)}, u32[]{:S(2)}) collective-permute-start(f32[126,126]{1,0:T(8,128)S(1)} %shard_map.49), channel_id=1, source_target_pairs={{0,3},{1,5},{2,6},{3,1},{5,7},{8,11},{9,13},{10,14},{11,9},{13,15}... | collective-permute-start | bytes 190520 | tf_op jit(solution)/shard_map/ppermute | solution.py:75
  24.4 0.0 collective-permute-done.1.own2
  24.4 0.8 %shard_map.46 = (f32[126,126]{1,0:T(8,128)S(1)}, f32[126,126]{1,0:T(8,128)S(1)}, f32[126,126]{1,0:T(8,128)S(1)}) custom-call(f32[400,126]{1,0:T(8,128)S(1)} %broadcast_in_dim.4.weight, f32[400,126]{1,0:T(8,128)S(1)} %broadcast_in_dim.5.weight2, f32[400,126]{1,0:T(8,128)S(1)} %bitcast.7, f32[400,126]{1,0:T(8,128)S(1)} %collective-permute-done.1.own2, ...), custom_call_target="tpu_custom_call" | custom-call | tf_op jit(solution)/shard_map/pallas_call | solution.py:245
  25.2 0.0 collective-permute-done.8.early
  25.2 0.1 shard_map.48.kept
  25.2 1.0 %collective-permute-done.9.late = f32[126,126]{1,0:T(8,128)S(1)} collective-permute-done((f32[126,126]{1,0:T(8,128)S(1)}, f32[126,126]{1,0:T(8,128)S(1)}, u32[]{:S(2)}, u32[]{:S(2)}) %collective-permute-start.9) | collective-permute-done | bytes 63536 | tf_op jit(solution)/shard_map/ppermute | solution.py:75
  26.3 0.7 %shard_map.50 = f32[315,126]{1,0:T(8,128)} custom-call(f32[315,126]{1,0:T(8,128)S(1)} %shard_map.48.kept, f32[126,126]{1,0:T(8,128)S(1)} %collective-permute-done.9.late), custom_call_target="tpu_custom_call" | custom-call | tf_op jit(solution)/shard_map/pallas_call | solution.py:245
  (4 shorter events, 0.0 us)
Async XLA Ops:
  0.0 7.1 %copy-start.2 = (f32[2]{0:T(128)S(1)}, f32[2]{0:T(128)}, u32[]{:S(2)}) copy-start(f32[2]{0:T(128)} %param.5) | copy-start | bytes 28
  0.0 10.9 %collective-permute-start.4 = (f32[400,126]{1,0:T(8,128)}, f32[400,126]{1,0:T(8,128)S(1)}, u32[]{:S(2)}, u32[]{:S(2)}) collective-permute-start(f32[400,126]{1,0:T(8,128)} %bitcast.3), channel_id=1, source_target_pairs={{0,4},{1,5},{2,6},{3,7},{4,0},{5,1},{6,2},{7,3},{8,12},{9,13},{10,... | collective-permute-start | bytes 604808 | tf_op jit(solution)/shard_map/ppermute | solution.py:75
  3.0 9.8 %collective-permute-start.6 = (f32[400,126]{1,0:T(8,128)}, f32[400,126]{1,0:T(8,128)S(1)}, u32[]{:S(2)}, u32[]{:S(2)}) collective-permute-start(f32[400,126]{1,0:T(8,128)} %bitcast.4), channel_id=1, source_target_pairs={{0,2},{1,3},{2,0},{3,1},{4,12},{5,13},{6,14},{7,15},{8,10},{9,11},... | collective-permute-start | bytes 604808 | tf_op jit(solution)/shard_map/ppermute | solution.py:75
  4.5 12.7 %collective-permute-start.2 = (f32[400,126]{1,0:T(8,128)}, f32[400,126]{1,0:T(8,128)S(1)}, u32[]{:S(2)}, u32[]{:S(2)}) collective-permute-start(f32[400,126]{1,0:T(8,128)} %bitcast.5), channel_id=1, source_target_pairs={{0,10},{1,11},{2,8},{3,9},{4,6},{5,7},{6,4},{7,5},{8,2},{9,3},{10,... | collective-permute-start | bytes 604808 | tf_op jit(solution)/shard_map/ppermute | solution.py:75
  7.1 17.3 %collective-permute-start.1 = (f32[400,126]{1,0:T(8,128)}, f32[400,126]{1,0:T(8,128)S(1)}, u32[]{:S(2)}, u32[]{:S(2)}) collective-permute-start(f32[400,126]{1,0:T(8,128)} %bitcast.6), channel_id=1, source_target_pairs={{0,1},{1,0},{2,3},{3,2},{4,5},{5,4},{6,7},{7,6},{8,9},{9,8},{10,11... | collective-permute-start | bytes 604808 | tf_op jit(solution)/shard_map/ppermute | solution.py:75
  7.1 10.1 %collective-permute-start = (f32[2]{0:T(128)S(1)}, f32[2]{0:T(128)S(1)}, u32[]{:S(2)}, u32[]{:S(2)}) collective-permute-start(f32[2]{0:T(128)S(1)} %copy-done.2), channel_id=1, source_target_pairs={{0,1},{1,0},{2,3},{3,2},{4,5},{5,4},{6,7},{7,6},{8,9},{9,8},{10,11... | collective-permute-start | bytes 32 | tf_op jit(solution)/shard_map/ppermute | solution.py:75
  8.2 9.0 %copy-start.1 = (f32[200]{0:T(256)S(1)}, f32[200]{0:T(256)}, u32[]{:S(2)}) copy-start(f32[200]{0:T(256)} %param.6) | copy-start | bytes 2404
  10.9 6.5 %collective-permute-start.5 = (f32[400,126]{1,0:T(8,128)S(1)}, f32[400,126]{1,0:T(8,128)S(1)}, u32[]{:S(2)}, u32[]{:S(2)}) collective-permute-start(f32[400,126]{1,0:T(8,128)S(1)} %collective-permute-done.4.zn), channel_id=1, source_target_pairs={{0,1},{1,0},{2,3},{3,2},{4,5},{5,4},{6,7},{7,6},{8,9},{9,8},{10,11... | collective-permute-start | bytes 604808 | tf_op jit(solution)/shard_map/ppermute | solution.py:75
  12.9 4.6 %collective-permute-start.7 = (f32[400,126]{1,0:T(8,128)S(1)}, f32[400,126]{1,0:T(8,128)S(1)}, u32[]{:S(2)}, u32[]{:S(2)}) collective-permute-start(f32[400,126]{1,0:T(8,128)S(1)} %collective-permute-done.6.a), channel_id=1, source_target_pairs={{0,1},{1,0},{2,3},{3,2},{4,5},{5,4},{6,7},{7,6},{8,9},{9,8},{10,11... | collective-permute-start | bytes 604808 | tf_op jit(solution)/shard_map/ppermute | solution.py:75
  17.2 3.5 %collective-permute-start.3 = (f32[400,126]{1,0:T(8,128)S(1)}, f32[400,126]{1,0:T(8,128)S(1)}, u32[]{:S(2)}, u32[]{:S(2)}) collective-permute-start(f32[400,126]{1,0:T(8,128)S(1)} %collective-permute-done.2.b), channel_id=1, source_target_pairs={{0,1},{1,0},{2,3},{3,2},{4,5},{5,4},{6,7},{7,6},{8,9},{9,8},{10,11... | collective-permute-start | bytes 604808 | tf_op jit(solution)/shard_map/ppermute | solution.py:75
  18.1 6.3 %copy-start = (f32[126,400]{0,1:T(8,128)S(1)}, f32[126,400]{0,1:T(8,128)}, u32[]{:S(2)}) copy-start(f32[126,400]{0,1:T(8,128)} %param.4) | copy-start | bytes 604804
  18.1 7.1 %collective-permute-start.8 = (f32[126,126]{1,0:T(8,128)S(1)}, f32[126,126]{1,0:T(8,128)S(1)}, u32[]{:S(2)}, u32[]{:S(2)}) collective-permute-start(f32[126,126]{1,0:T(8,128)S(1)} %shard_map.47), channel_id=1, source_target_pairs={{0,2},{3,1},{4,12},{5,13},{6,14},{7,15},{8,10},{11,9},{12,4},{13,5... | collective-permute-start | bytes 190520 | tf_op jit(solution)/shard_map/ppermute | solution.py:75
  21.1 5.1 %collective-permute-start.9 = (f32[126,126]{1,0:T(8,128)S(1)}, f32[126,126]{1,0:T(8,128)S(1)}, u32[]{:S(2)}, u32[]{:S(2)}) collective-permute-start(f32[126,126]{1,0:T(8,128)S(1)} %shard_map.49), channel_id=1, source_target_pairs={{0,3},{1,5},{2,6},{3,1},{5,7},{8,11},{9,13},{10,14},{11,9},{13,15}... | collective-permute-start | bytes 190520 | tf_op jit(solution)/shard_map/ppermute | solution.py:75

commit v2 on v0

--- a/solution.py
+++ b/solution.py
@@ -1,6 +1,8 @@
 import jax
 import jax.numpy as jnp
 from jax import lax
+from jax.experimental import pallas as pl
+from jax.experimental.pallas import tpu as pltpu
 from jax.sharding import PartitionSpec as P
 
 
@@ -54,14 +56,219 @@
     return write_block(collected, product_tile(scaled_rows, middle), half_span // 2 * row_count)
 
 
-def shards(pair_tensor, occ_energy, vir_energy, frequency):
+def ring_shards(pair_tensor, occ_energy, vir_energy, frequency):
     n_aux = lax.axis_size("aux")
     scaled_rows = pair_tensor * pair_weights(occ_energy, vir_energy, frequency)[None, :]
     collected = half_turn(scaled_rows, pair_tensor, n_aux // 2)
     return lax.psum_scatter(collected, "pair", scatter_dimension=1, tiled=True)
 
 
+def sent(value, target_of):
+    pairs = []
+    for z in range(4):
+        for x in range(2):
+            for c in range(2):
+                tz, tx, tc = target_of(z, x, c)
+                pairs.append(((z * 2 + x) * 2 + c, (tz * 2 + tx) * 2 + tc))
+    return lax.ppermute(value, ("aux", "pair"), pairs)
+
+
+def other_core(z, x, c):
+    return (z, x, 1 - c)
+
+
+def far_chip(z, x, c):
+    return (z ^ 2, x, c)
+
+
+def other_x(z, x, c):
+    return (z, 1 - x, c)
+
+
+def next_chip(z, x, c):
+    return (z ^ 1, x if z % 2 else 1 - x, c)
+
+
+def tile_chip(z, x, c):
+    if z % 2 == 0:
+        return (z, 1 - x, c)
+    return (z ^ 2, x, c) if x != c else (z, 1 - x, 1 - c)
+
+
+def half_tile_chip(z, x, c):
+    return (z ^ 1, x, c)
+
+
+def place():
+    block = lax.axis_index("aux")
+    return lax.rem(block // 2, 2) == 0, lax.rem(block, 2), lax.axis_index("pair")
+
+
+def halves(value):
+    high = value.astype(jnp.bfloat16)
+    return high, (value - high.astype(jnp.float32)).astype(jnp.bfloat16)
+
+
+def summed_over_pairs(left, right):
+    left_high, left_low = left
+    right_high, right_low = right
+    return lax.dot_general(
+        jnp.concatenate([left_high, left_low, left_high], 0),
+        jnp.concatenate([right_high, right_high, right_low], 0),
+        (((0,), (0,)), ((), ())),
+        preferred_element_type=jnp.float32,
+    )
+
+
+def tile_of(left_blocks, right_blocks):
+    total = None
+    for left, right in zip(left_blocks, right_blocks):
+        part = summed_over_pairs(halves(left), halves(right))
+        total = part if total is None else total + part
+    return total
+
+
+def scale_kernel(weight, weight2, xp, xp2, zn, zn2, xp_scaled, zn_scaled):
+    xp_scaled[0] = xp[...] * weight[...]
+    xp_scaled[1] = xp2[...] * weight2[...]
+    zn_scaled[0] = zn[...] * weight[...]
+    zn_scaled[1] = zn2[...] * weight2[...]
+
+
+def tile_kernel(zn, zn2, xp_scaled, zn_scaled, far, far2, tile):
+    even, x, c = place()
+    far_blocks = (far[...], far2[...])
+
+    def far_xp():
+        tile[...] = tile_of(far_blocks, (xp_scaled[0], xp_scaled[1]))
+
+    @pl.when(even & (x == 0) & (c == 1))
+    def _():
+        far_xp()
+
+    @pl.when(~even & (x == 0) & (c == 0))
+    def _():
+        far_xp()
+
+    @pl.when(even & ((x == 1) | (c == 0)))
+    def _():
+        tile[...] = tile_of((zn[...], zn2[...]), (xp_scaled[0], xp_scaled[1]))
+
+    @pl.when(~even & ((x == 1) | (c == 1)))
+    def _():
+        tile[...] = tile_of((zn_scaled[0], zn_scaled[1]), far_blocks)
+
+
+def half_tile_kernel(zn_scaled, far, far2, half_tile):
+    _, _, c = place()
+    half = half_tile.shape[0]
+    tile = tile_of((far[...], far2[...]), (zn_scaled[0], zn_scaled[1]))
+
+    @pl.when(c == 0)
+    def _():
+        half_tile[...] = tile[:half]
+
+    @pl.when(c == 1)
+    def _():
+        half_tile[...] = tile[half:]
+
+
+def local_kernel(weight, weight2, own, own2, xp, xp2, zn, zn2, far, far2, kept):
+    even, x, c = place()
+    rows = own.shape[1]
+    half = rows // 2
+    scaled = (own[...] * weight[...], own2[...] * weight2[...])
+
+    @pl.when(c == 0)
+    def _():
+        kept[pl.ds(0, rows), :] = tile_of((own[...], own2[...]), scaled)
+        kept[pl.ds(rows, rows), :] = tile_of((xp[...], xp2[...]), scaled)
+
+    @pl.when(c == 1)
+    def _():
+        kept[pl.ds(half, rows), :] = jnp.zeros((rows, rows), jnp.float32)
+        kept[pl.ds(half + rows, rows), :] = tile_of((far[...], far2[...]), scaled)
+
+    zn_own = tile_of((zn[...], zn2[...]), scaled)
+
+    @pl.when(c == 0)
+    def _():
+        kept[pl.ds(2 * rows, half), :] = zn_own[:half]
+
+    @pl.when(c == 1)
+    def _():
+        kept[pl.ds(0, half), :] = zn_own[half:]
+
+
+def finish_kernel(kept, tile, half_tile, response):
+    even, x, c = place()
+    rows = tile.shape[0]
+    half = rows // 2
+    response[...] = kept[...]
+
+    @pl.when((c == 0) & (x == 1))
+    def _():
+        response[pl.ds(rows, rows), :] = tile[...]
+
+    @pl.when(c == 1)
+    def _():
+        response[pl.ds(half, rows), :] = tile[...]
+
+    @pl.when((c == 0) & ~even)
+    def _():
+        response[pl.ds(2 * rows, half), :] = half_tile[...]
+
+    @pl.when((c == 1) & ~even)
+    def _():
+        response[pl.ds(0, half), :] = half_tile[...]
+
+
+def in_vmem(kernel, shapes, *operands):
+    whole = pl.BlockSpec(memory_space=pltpu.VMEM)
+    out_shape = [jax.ShapeDtypeStruct(shape, jnp.float32) for shape in shapes]
+    return pl.pallas_call(
+        kernel,
+        out_shape=out_shape,
+        in_specs=[whole] * len(operands),
+        out_specs=[whole] * len(shapes),
+        compiler_params=pltpu.CompilerParams(vmem_limit_bytes=32 * 1024 * 1024),
+        cost_estimate=pl.CostEstimate(flops=1000, bytes_accessed=1000, transcendentals=0),
+    )(*operands)
+
+
+def octet_shards(pair_tensor, occ_energy, vir_energy, frequency):
+    own = pair_tensor.T
+    pairs, rows = own.shape
+    far = sent(own, far_chip)
+    xp = sent(own, other_x)
+    zn = sent(own, next_chip)
+    own2 = sent(own, other_core)
+    occ_energy2 = sent(occ_energy, other_core)
+    weights = tuple(
+        jnp.broadcast_to(pair_weights(e, vir_energy, frequency)[:, None], (pairs, rows))
+        for e in (occ_energy, occ_energy2)
+    )
+    far2, xp2, zn2 = (sent(v, other_core) for v in (far, xp, zn))
+    xp_scaled, zn_scaled = in_vmem(
+        scale_kernel, [(2, pairs, rows)] * 2, *weights, xp, xp2, zn, zn2
+    )
+    (tile,) = in_vmem(
+        tile_kernel, [(rows, rows)], zn, zn2, xp_scaled, zn_scaled, far, far2
+    )
+    tile = sent(tile, tile_chip)
+    (half_tile,) = in_vmem(half_tile_kernel, [(rows // 2, rows)], zn_scaled, far, far2)
+    half_tile = sent(half_tile, half_tile_chip)
+    kept_shape = (5 * rows // 2, rows)
+    (kept,) = in_vmem(
+        local_kernel, [kept_shape], *weights, own, own2, xp, xp2, zn, zn2, far, far2
+    )
+    (response,) = in_vmem(finish_kernel, [kept_shape], kept, tile, half_tile)
+    return response.T
+
+
 def solution(mesh):
     in_specs = (P(("parts", "aux"), "pair"), P(("parts", "pair")), P("parts"), P("parts"))
     out_specs = P(("parts", "aux"), "pair")
+    octet = mesh.shape["aux"] == 8 and mesh.shape["pair"] == 2
+    shards = octet_shards if octet else ring_shards
     return jax.shard_map(shards, mesh=mesh, in_specs=in_specs, out_specs=out_specs, check_vma=False)

time: 41 us -> 24.9 us (0.61)
  matrix products: 4.67 us -> 0 us
  local copies, waits for them, and re-layouts: 4.26 us -> 0.4 us
  starting transfers between devices: 13 us -> 9.73 us
  blocking collectives: 3.17 us -> 0 us
  waiting for transfers between devices: 14.1 us -> 11.3 us
  Pallas kernels: 0 us -> 2.5 us
  between operations: 1.44 us -> 0.76 us
    dot_general x5 -> x0, matrix products: 4.67 us -> none  [product_tile(): lax.dot_general(scaled_rows, block_rows, (((1,), (1,)), ((), ())), precis...]
    unnamed x1 -> x0, blocking collectives: 3.17 us -> none
    ppermute x4 -> x10, waiting for transfers between devices: 14.1 us -> 11.3 us  [sent(): return lax.ppermute(value, ('aux', 'pair'), pairs)]
    pallas_call x0 -> x5, Pallas kernels: none -> 2.5 us  [in_vmem(): pl.pallas_call(kernel, out_shape=out_shape, in_specs=[whole] * len(operan...]
    unnamed x12 -> x6, local copies, waits for them, and re-layouts: 2.45 us -> 0.01 us
    unnamed x1 -> x0, starting transfers between devices: 2.27 us -> none
    dynamic_update_slice x4 -> x0, local copies, waits for them, and re-layouts: 1.73 us -> none  [write_block(): return lax.dynamic_update_slice_in_dim(collected, values, column, 1)]
    ppermute x4 -> x10, starting transfers between devices: 10.8 us -> 9.73 us  [sent(): return lax.ppermute(value, ('aux', 'pair'), pairs)]
  transfers between devices with their start and end apart: 5 -> 10, of which waited for: 4 -> 4; matrix products, arithmetic and copies ran while one was open for 14% -> 2% of each run, Pallas kernels for 0% -> 7%
where the time goes in v2:
time: 24.9 us; the launch traced here: 24.8 us
  waiting for transfers between devices  11.3 us (45%)
  starting transfers between devices  9.73 us (39%)
  Pallas kernels  2.5 us (10%)
  between operations  0.76 us (3%)
  local copies, waits for them, and re-layouts  0.4 us (2%)
    ppermute x10, waiting for transfers between devices, sent(): return lax.ppermute(value, ('aux', 'pair'), pairs)  11.3 us
    ppermute x10, starting transfers between devices, sent(): return lax.ppermute(value, ('aux', 'pair'), pairs)  9.73 us
    pallas_call x5, Pallas kernels, in_vmem(): pl.pallas_call(kernel, out_shape=out_shape, in_specs=[whole] * len(operan...  2.5 us
  transfers between devices with their start and end apart: 10, of which 4 were waited for; matrix products, arithmetic and copies ran while one was open for 2% of the time, Pallas kernels for 7%

profile of v2, /device:TPU:0, one launch (start us, length us, event | category | flops | bytes accessed | tf_op | source)
XLA Modules:
  0.0 24.8 jit_solution(3674651592157314698)
XLA Ops:
  0.0 4.0 %collective-permute-start.4 = (f32[400,126]{1,0:T(8,128)}, f32[400,126]{1,0:T(8,128)S(1)}, u32[]{:S(2)}, u32[]{:S(2)}) collective-permute-start(f32[400,126]{1,0:T(8,128)} %bitcast.3), channel_id=1, source_target_pairs={{0,6},{1,7},{2,4},{3,5},{4,0},{5,1},{6,2},{7,3},{8,14},{9,15},{10,... | collective-permute-start | bytes 604808 | tf_op jit(solution)/shard_map/ppermute | solution.py:73
  4.0 0.5 %collective-permute-start.2 = (f32[400,126]{1,0:T(8,128)}, f32[400,126]{1,0:T(8,128)S(1)}, u32[]{:S(2)}, u32[]{:S(2)}) collective-permute-start(f32[400,126]{1,0:T(8,128)} %bitcast.4), channel_id=1, source_target_pairs={{0,2},{1,3},{2,0},{3,1},{4,6},{5,7},{6,4},{7,5},{8,10},{9,11},{10,... | collective-permute-start | bytes 604808 | tf_op jit(solution)/shard_map/ppermute | solution.py:73
  4.5 2.6 %collective-permute-start.6 = (f32[400,126]{1,0:T(8,128)}, f32[400,126]{1,0:T(8,128)S(1)}, u32[]{:S(2)}, u32[]{:S(2)}) collective-permute-start(f32[400,126]{1,0:T(8,128)} %bitcast.5), channel_id=1, source_target_pairs={{0,8},{1,9},{2,10},{3,11},{4,12},{5,13},{6,14},{7,15},{8,0},{9,1},... | collective-permute-start | bytes 604808 | tf_op jit(solution)/shard_map/ppermute | solution.py:73
  7.1 0.0 collective-permute-start.1
  7.1 0.0 copy-done.2
  7.1 0.5 %collective-permute-start = (f32[2]{0:T(128)S(1)}, f32[2]{0:T(128)S(1)}, u32[]{:S(2)}, u32[]{:S(2)}) collective-permute-start(f32[2]{0:T(128)S(1)} %copy-done.2), channel_id=1, source_target_pairs={{0,1},{1,0},{2,3},{3,2},{4,5},{5,4},{6,7},{7,6},{8,9},{9,8},{10,11... | collective-permute-start | bytes 32 | tf_op jit(solution)/shard_map/ppermute | solution.py:73
  8.3 2.7 %collective-permute-done.4.zn = f32[400,126]{1,0:T(8,128)S(1)} collective-permute-done((f32[400,126]{1,0:T(8,128)}, f32[400,126]{1,0:T(8,128)S(1)}, u32[]{:S(2)}, u32[]{:S(2)}) %collective-permute-start.4) | collective-permute-done | bytes 201632 | tf_op jit(solution)/shard_map/ppermute | solution.py:73
  10.9 0.0 collective-permute-start.5
  10.9 0.0 collective-permute-done.2.xp
  10.9 0.5 %collective-permute-start.3 = (f32[400,126]{1,0:T(8,128)S(1)}, f32[400,126]{1,0:T(8,128)S(1)}, u32[]{:S(2)}, u32[]{:S(2)}) collective-permute-start(f32[400,126]{1,0:T(8,128)S(1)} %collective-permute-done.2.xp), channel_id=1, source_target_pairs={{0,1},{1,0},{2,3},{3,2},{4,5},{5,4},{6,7},{7,6},{8,9},{9,8},{10,11... | collective-permute-start | bytes 604808 | tf_op jit(solution)/shard_map/ppermute | solution.py:73
  11.4 4.9 %collective-permute-done.6.far = f32[400,126]{1,0:T(8,128)S(1)} collective-permute-done((f32[400,126]{1,0:T(8,128)}, f32[400,126]{1,0:T(8,128)S(1)}, u32[]{:S(2)}, u32[]{:S(2)}) %collective-permute-start.6) | collective-permute-done | bytes 201632 | tf_op jit(solution)/shard_map/ppermute | solution.py:73
  16.3 0.0 collective-permute-start.7
  16.3 0.0 collective-permute-done
  16.3 0.1 fusion.2
  16.4 0.1 div.21
  16.5 0.1 div.23
  16.6 0.0 collective-permute-done.5.zn2
  16.6 0.0 collective-permute-done.3.xp2
  16.6 0.1 broadcast_in_dim.4.weight
  16.7 0.1 broadcast_in_dim.5.weight2
  16.8 0.1 shard_map.47
  16.9 0.8 %collective-permute-done.7.far2 = f32[400,126]{1,0:T(8,128)S(1)} collective-permute-done((f32[400,126]{1,0:T(8,128)S(1)}, f32[400,126]{1,0:T(8,128)S(1)}, u32[]{:S(2)}, u32[]{:S(2)}) %collective-permute-start.7) | collective-permute-done | bytes 201632 | tf_op jit(solution)/shard_map/ppermute | solution.py:73
  17.8 0.4 %shard_map.48 = f32[126,126]{1,0:T(8,128)S(1)} custom-call(f32[400,126]{1,0:T(8,128)S(1)} %collective-permute-done.4.zn, f32[400,126]{1,0:T(8,128)S(1)} %collective-permute-done.5.zn2, f32[2,400,126]{2,1,0:T(8,128)S(1)} %get-tuple-element.7.xp_scaled, f32[2,400,126]{2,1,0:T(8,128)S(1)} %get-tuple-element.8.zn_scaled, ...), custom_call_target="tpu_custom_call" | custom-call | flops 1000 | bytes 1000 | tf_op jit(solution)/shard_map/pallas_call | solution.py:229
  18.2 0.0 copy-start
  18.2 1.6 %collective-permute-start.8 = (f32[126,126]{1,0:T(8,128)S(1)}, f32[126,126]{1,0:T(8,128)S(1)}, u32[]{:S(2)}, u32[]{:S(2)}) collective-permute-start(f32[126,126]{1,0:T(8,128)S(1)} %shard_map.48), channel_id=1, source_target_pairs={{0,2},{1,3},{2,0},{3,1},{4,7},{5,13},{6,14},{7,4},{8,10},{9,11},{1... | collective-permute-start | bytes 190520 | tf_op jit(solution)/shard_map/ppermute | solution.py:73
  19.7 0.4 %shard_map.49 = f32[63,126]{1,0:T(8,128)S(1)} custom-call(f32[2,400,126]{2,1,0:T(8,128)S(1)} %get-tuple-element.8.zn_scaled, f32[400,126]{1,0:T(8,128)S(1)} %collective-permute-done.6.far, f32[400,126]{1,0:T(8,128)S(1)} %collective-permute-done.7.far2), custom_call_target="tpu_custom_call" | custom-call | flops 1000 | bytes 1000 | tf_op jit(solution)/shard_map/pallas_call | solution.py:229
  20.1 0.1 collective-permute-start.9
  20.2 0.0 collective-permute-done.1.own2
  20.2 1.0 %shard_map.46.kept = f32[315,126]{1,0:T(8,128)S(1)} custom-call(f32[400,126]{1,0:T(8,128)S(1)} %broadcast_in_dim.4.weight, f32[400,126]{1,0:T(8,128)S(1)} %broadcast_in_dim.5.weight2, f32[400,126]{1,0:T(8,128)S(1)} %bitcast.7, f32[400,126]{1,0:T(8,128)S(1)} %collective-permute-done.1.own2, f32[400,126]{1,0:T(8,128)S(1)} %collective-permute-done.2.xp, ...), custom_call_target="tpu_custom_call" | custom-call | flops 1000 | bytes 1000 | tf_op jit(solution)/shard_map/pallas_call | solution.py:229
  21.2 2.9 %collective-permute-done.9.half_tile = f32[63,126]{1,0:T(8,128)S(1)} collective-permute-done((f32[63,126]{1,0:T(8,128)S(1)}, f32[63,126]{1,0:T(8,128)S(1)}, u32[]{:S(2)}, u32[]{:S(2)}) %collective-permute-start.9) | collective-permute-done | bytes 31784 | tf_op jit(solution)/shard_map/ppermute | solution.py:73
  24.1 0.0 collective-permute-done.8.tile
  24.1 0.7 %shard_map.50 = f32[315,126]{1,0:T(8,128)} custom-call(f32[315,126]{1,0:T(8,128)S(1)} %shard_map.46.kept, f32[126,126]{1,0:T(8,128)S(1)} %collective-permute-done.8.tile, f32[63,126]{1,0:T(8,128)S(1)} %collective-permute-done.9.half_tile), custom_call_target="tpu_custom_call" | custom-call | flops 1000 | bytes 1000 | tf_op jit(solution)/shard_map/pallas_call | solution.py:229
  (4 shorter events, 0.0 us)
Async XLA Ops:
  0.0 7.1 %copy-start.2 = (f32[2]{0:T(128)S(1)}, f32[2]{0:T(128)}, u32[]{:S(2)}) copy-start(f32[2]{0:T(128)} %param.5) | copy-start | bytes 28
  0.0 10.9 %collective-permute-start.4 = (f32[400,126]{1,0:T(8,128)}, f32[400,126]{1,0:T(8,128)S(1)}, u32[]{:S(2)}, u32[]{:S(2)}) collective-permute-start(f32[400,126]{1,0:T(8,128)} %bitcast.3), channel_id=1, source_target_pairs={{0,6},{1,7},{2,4},{3,5},{4,0},{5,1},{6,2},{7,3},{8,14},{9,15},{10,... | collective-permute-start | bytes 604808 | tf_op jit(solution)/shard_map/ppermute | solution.py:73
  4.0 7.0 %collective-permute-start.2 = (f32[400,126]{1,0:T(8,128)}, f32[400,126]{1,0:T(8,128)S(1)}, u32[]{:S(2)}, u32[]{:S(2)}) collective-permute-start(f32[400,126]{1,0:T(8,128)} %bitcast.4), channel_id=1, source_target_pairs={{0,2},{1,3},{2,0},{3,1},{4,6},{5,7},{6,4},{7,5},{8,10},{9,11},{10,... | collective-permute-start | bytes 604808 | tf_op jit(solution)/shard_map/ppermute | solution.py:73
  4.5 11.8 %collective-permute-start.6 = (f32[400,126]{1,0:T(8,128)}, f32[400,126]{1,0:T(8,128)S(1)}, u32[]{:S(2)}, u32[]{:S(2)}) collective-permute-start(f32[400,126]{1,0:T(8,128)} %bitcast.5), channel_id=1, source_target_pairs={{0,8},{1,9},{2,10},{3,11},{4,12},{5,13},{6,14},{7,15},{8,0},{9,1},... | collective-permute-start | bytes 604808 | tf_op jit(solution)/shard_map/ppermute | solution.py:73
  7.1 13.1 %collective-permute-start.1 = (f32[400,126]{1,0:T(8,128)}, f32[400,126]{1,0:T(8,128)S(1)}, u32[]{:S(2)}, u32[]{:S(2)}) collective-permute-start(f32[400,126]{1,0:T(8,128)} %bitcast.6), channel_id=1, source_target_pairs={{0,1},{1,0},{2,3},{3,2},{4,5},{5,4},{6,7},{7,6},{8,9},{9,8},{10,11... | collective-permute-start | bytes 604808 | tf_op jit(solution)/shard_map/ppermute | solution.py:73
  7.1 9.2 %collective-permute-start = (f32[2]{0:T(128)S(1)}, f32[2]{0:T(128)S(1)}, u32[]{:S(2)}, u32[]{:S(2)}) collective-permute-start(f32[2]{0:T(128)S(1)} %copy-done.2), channel_id=1, source_target_pairs={{0,1},{1,0},{2,3},{3,2},{4,5},{5,4},{6,7},{7,6},{8,9},{9,8},{10,11... | collective-permute-start | bytes 32 | tf_op jit(solution)/shard_map/ppermute | solution.py:73
  8.2 8.1 %copy-start.1 = (f32[200]{0:T(256)S(1)}, f32[200]{0:T(256)}, u32[]{:S(2)}) copy-start(f32[200]{0:T(256)} %param.6) | copy-start | bytes 2404
  10.9 5.7 %collective-permute-start.5 = (f32[400,126]{1,0:T(8,128)S(1)}, f32[400,126]{1,0:T(8,128)S(1)}, u32[]{:S(2)}, u32[]{:S(2)}) collective-permute-start(f32[400,126]{1,0:T(8,128)S(1)} %collective-permute-done.4.zn), channel_id=1, source_target_pairs={{0,1},{1,0},{2,3},{3,2},{4,5},{5,4},{6,7},{7,6},{8,9},{9,8},{10,11... | collective-permute-start | bytes 604808 | tf_op jit(solution)/shard_map/ppermute | solution.py:73
  10.9 5.7 %collective-permute-start.3 = (f32[400,126]{1,0:T(8,128)S(1)}, f32[400,126]{1,0:T(8,128)S(1)}, u32[]{:S(2)}, u32[]{:S(2)}) collective-permute-start(f32[400,126]{1,0:T(8,128)S(1)} %collective-permute-done.2.xp), channel_id=1, source_target_pairs={{0,1},{1,0},{2,3},{3,2},{4,5},{5,4},{6,7},{7,6},{8,9},{9,8},{10,11... | collective-permute-start | bytes 604808 | tf_op jit(solution)/shard_map/ppermute | solution.py:73
  16.3 1.5 %collective-permute-start.7 = (f32[400,126]{1,0:T(8,128)S(1)}, f32[400,126]{1,0:T(8,128)S(1)}, u32[]{:S(2)}, u32[]{:S(2)}) collective-permute-start(f32[400,126]{1,0:T(8,128)S(1)} %collective-permute-done.6.far), channel_id=1, source_target_pairs={{0,1},{1,0},{2,3},{3,2},{4,5},{5,4},{6,7},{7,6},{8,9},{9,8},{10,11... | collective-permute-start | bytes 604808 | tf_op jit(solution)/shard_map/ppermute | solution.py:73
  18.2 2.0 %copy-start = (f32[126,400]{0,1:T(8,128)S(1)}, f32[126,400]{0,1:T(8,128)}, u32[]{:S(2)}) copy-start(f32[126,400]{0,1:T(8,128)} %param.4) | copy-start | bytes 604804
  18.2 5.9 %collective-permute-start.8 = (f32[126,126]{1,0:T(8,128)S(1)}, f32[126,126]{1,0:T(8,128)S(1)}, u32[]{:S(2)}, u32[]{:S(2)}) collective-permute-start(f32[126,126]{1,0:T(8,128)S(1)} %shard_map.48), channel_id=1, source_target_pairs={{0,2},{1,3},{2,0},{3,1},{4,7},{5,13},{6,14},{7,4},{8,10},{9,11},{1... | collective-permute-start | bytes 190520 | tf_op jit(solution)/shard_map/ppermute | solution.py:73
  20.1 4.0 %collective-permute-start.9 = (f32[63,126]{1,0:T(8,128)S(1)}, f32[63,126]{1,0:T(8,128)S(1)}, u32[]{:S(2)}, u32[]{:S(2)}) collective-permute-start(f32[63,126]{1,0:T(8,128)S(1)} %shard_map.49), channel_id=1, source_target_pairs={{0,4},{1,5},{2,6},{3,7},{4,0},{5,1},{6,2},{7,3},{8,12},{9,13},{10,... | collective-permute-start | bytes 95264 | tf_op jit(solution)/shard_map/ppermute | solution.py:73

commit v3 on v0

--- a/solution.py
+++ b/solution.py
@@ -1,6 +1,10 @@
+import functools
+
 import jax
 import jax.numpy as jnp
 from jax import lax
+from jax.experimental import pallas as pl
+from jax.experimental.pallas import tpu as pltpu
 from jax.sharding import PartitionSpec as P
 
 
@@ -54,14 +58,260 @@
     return write_block(collected, product_tile(scaled_rows, middle), half_span // 2 * row_count)
 
 
-def shards(pair_tensor, occ_energy, vir_energy, frequency):
+def ring_shards(pair_tensor, occ_energy, vir_energy, frequency):
     n_aux = lax.axis_size("aux")
     scaled_rows = pair_tensor * pair_weights(occ_energy, vir_energy, frequency)[None, :]
     collected = half_turn(scaled_rows, pair_tensor, n_aux // 2)
     return lax.psum_scatter(collected, "pair", scatter_dimension=1, tiled=True)
 
 
+def sent(value, target_of):
+    pairs = []
+    for z in range(4):
+        for x in range(2):
+            for c in range(2):
+                tz, tx, tc = target_of(z, x, c)
+                pairs.append(((z * 2 + x) * 2 + c, (tz * 2 + tx) * 2 + tc))
+    return lax.ppermute(value, ("aux", "pair"), pairs)
+
+
+def other_core(z, x, c):
+    return (z, x, 1 - c)
+
+
+def far_chip(z, x, c):
+    return (z ^ 2, x, c)
+
+
+def other_x(z, x, c):
+    return (z, 1 - x, c)
+
+
+def next_chip(z, x, c):
+    return (z ^ 1, x if z % 2 else 1 - x, c)
+
+
+def tile_chip(z, x, c):
+    if z % 2 == 0:
+        return (z, 1 - x, c)
+    return (z ^ 2, x, c) if x != c else (z, 1 - x, 1 - c)
+
+
+def half_tile_chip(z, x, c):
+    return (z ^ 1, x, c)
+
+
+def place():
+    block = lax.axis_index("aux")
+    return lax.rem(block // 2, 2) == 0, lax.rem(block, 2), lax.axis_index("pair")
+
+
+def halves(value):
+    high = value.astype(jnp.bfloat16)
+    return high, (value - high.astype(jnp.float32)).astype(jnp.bfloat16)
+
+
+def stack_kernel(order, block, stack):
+    pairs, rows = block.shape
+    parts = halves(block[...])
+    for i, part in enumerate(order):
+        stack[pl.ds(i * pairs, pairs), pl.ds(0, rows)] = parts[part]
+
+
+def scaled_kernel(weight, block, stack):
+    pairs, rows = block.shape
+    parts = halves(block[...] * weight[...])
+    for i, part in enumerate((0, 0, 1)):
+        stack[pl.ds(i * pairs, pairs), pl.ds(0, rows)] = parts[part]
+
+
+def meet_kernel(far, xp, xp_scaled, zn_scaled, mine, theirs):
+    even, x, c = place()
+    rows = mine.shape[1]
+    half = rows // 2
+    tiles = lax.dot_general(
+        jnp.concatenate([far[...], xp[...]], 1),
+        jnp.concatenate([zn_scaled[...], xp_scaled[...]], 1),
+        (((0,), (0,)), ((), ())),
+        preferred_element_type=jnp.float32,
+    )
+    far_zn, far_xp = tiles[:rows, :rows], tiles[:rows, 128 : 128 + rows]
+    xp_zn = tiles[128 : 128 + rows, :rows]
+
+    def put(core, row, values):
+        @pl.when(c == core)
+        def _():
+            mine[pl.ds(row, values.shape[0]), :] = values
+
+        @pl.when(c != core)
+        def _():
+            theirs[pl.ds(row, values.shape[0]), :] = values
+
+    put(0, rows, far_zn[:half])
+    put(1, rows, far_zn[half:])
+
+    @pl.when(even)
+    def _():
+        zn_xp = xp_zn.T
+        put(0, 0, zn_xp)
+
+        @pl.when(x == 0)
+        def _():
+            put(1, 0, far_xp)
+
+        @pl.when(x == 1)
+        def _():
+            put(1, 0, zn_xp)
+
+    @pl.when(~even)
+    def _():
+        zn_far = far_zn.T
+        put(1, 0, zn_far)
+
+        @pl.when(x == 0)
+        def _():
+            put(0, 0, far_xp)
+
+        @pl.when(x == 1)
+        def _():
+            put(0, 0, zn_far)
+
+
+def sum_kernel(mine, theirs, tile, half_tile):
+    rows, half = tile.shape[0], half_tile.shape[0]
+    tile[...] = mine[pl.ds(0, rows), :] + theirs[pl.ds(0, rows), :]
+    half_tile[...] = mine[pl.ds(rows, half), :] + theirs[pl.ds(rows, half), :]
+
+
+def dot_over_pairs(left, right):
+    return lax.dot_general(
+        left, right, (((0,), (0,)), ((), ())), preferred_element_type=jnp.float32
+    )
+
+
+def local_kernel(own, own_scaled, xp, zn_scaled, mine, theirs):
+    even, x, c = place()
+    rows = mine.shape[1]
+    half = rows // 2
+    own_stack = own[...]
+    by_own = dot_over_pairs(jnp.concatenate([own_stack, xp[...]], 1), own_scaled[...])
+    own_own, xp_own = by_own[:rows, :rows], by_own[128 : 128 + rows, :rows]
+    zn_own = dot_over_pairs(zn_scaled[...], own_stack)[:rows, :rows]
+
+    def first(kept):
+        kept[pl.ds(0, rows), :] = own_own
+        kept[pl.ds(rows, rows), :] = xp_own
+        kept[pl.ds(2 * rows, half), :] = zn_own[:half]
+
+    def second(kept):
+        kept[pl.ds(0, half), :] = zn_own[half:]
+        kept[pl.ds(half, 2 * rows), :] = jnp.zeros((2 * rows, rows), jnp.float32)
+
+    @pl.when(c == 0)
+    def _():
+        first(mine)
+        second(theirs)
+
+    @pl.when(c == 1)
+    def _():
+        first(theirs)
+        second(mine)
+
+
+def far_kernel(weight, own, far, far_own):
+    far_own[...] = tile_of(far[...], own[...] * weight[...])
+
+
+def far_kernel(far, own_scaled, far_own):
+    rows = far_own.shape[0]
+    far_own[...] = dot_over_pairs(far[...], own_scaled[...])[:rows, :rows]
+
+
+def finish_kernel(mine, theirs, far_own, far_own2, tile, half_tile, response):
+    even, x, c = place()
+    rows = tile.shape[0]
+    half = rows // 2
+    response[...] = mine[...] + theirs[...]
+
+    @pl.when((c == 0) & (x == 1))
+    def _():
+        response[pl.ds(rows, rows), :] = tile[...]
+
+    @pl.when(c == 1)
+    def _():
+        response[pl.ds(half, rows), :] = tile[...]
+        response[pl.ds(half + rows, rows), :] = far_own[...] + far_own2[...]
+
+    @pl.when((c == 0) & ~even)
+    def _():
+        response[pl.ds(2 * rows, half), :] = half_tile[...]
+
+    @pl.when((c == 1) & ~even)
+    def _():
+        response[pl.ds(0, half), :] = half_tile[...]
+
+
+def in_vmem(kernel, outs, *operands, flops=1000):
+    whole = pl.BlockSpec(memory_space=pltpu.VMEM)
+    return pl.pallas_call(
+        kernel,
+        out_shape=[jax.ShapeDtypeStruct(*out) for out in outs],
+        in_specs=[whole] * len(operands),
+        out_specs=[whole] * len(outs),
+        compiler_params=pltpu.CompilerParams(vmem_limit_bytes=32 * 1024 * 1024),
+        cost_estimate=pl.CostEstimate(flops=flops, bytes_accessed=1000, transcendentals=0),
+    )(*operands)
+
+
+def octet_shards(pair_tensor, occ_energy, vir_energy, frequency):
+    own = pair_tensor.T
+    pairs, rows = own.shape
+    weight = jnp.broadcast_to(
+        pair_weights(occ_energy, vir_energy, frequency)[:, None], (pairs, rows)
+    )
+    stack = ((3 * pairs, 128), jnp.bfloat16)
+    plain = functools.partial(stack_kernel, (0, 1, 0))
+    far = sent(own, far_chip)
+    xp = sent(own, other_x)
+    zn = sent(own, next_chip)
+    (far_stack,) = in_vmem(plain, [stack], far, flops=10**11)
+    (zn_scaled,) = in_vmem(scaled_kernel, [stack], weight, zn)
+    xp, zn_scaled = lax.optimization_barrier((xp, zn_scaled))
+    (xp_stack,) = in_vmem(plain, [stack], xp)
+    (xp_scaled,) = in_vmem(scaled_kernel, [stack], weight, xp)
+    parts = ((3 * rows // 2, rows), jnp.float32)
+    mine, theirs = in_vmem(
+        meet_kernel, [parts] * 2, far_stack, xp_stack, xp_scaled, zn_scaled
+    )
+    square, half_square = ((rows, rows), jnp.float32), ((rows // 2, rows), jnp.float32)
+    tile, half_tile = in_vmem(
+        sum_kernel, [square, half_square], mine, sent(theirs, other_core)
+    )
+    tile = sent(tile, tile_chip)
+    half_tile = sent(half_tile, half_tile_chip)
+    (own_stack,) = in_vmem(plain, [stack], own)
+    (own_scaled,) = in_vmem(scaled_kernel, [stack], weight, own)
+    kept = ((5 * rows // 2, rows), jnp.float32)
+    mine, theirs = in_vmem(
+        local_kernel, [kept] * 2, own_stack, own_scaled, xp_stack, zn_scaled
+    )
+    (far_own,) = in_vmem(far_kernel, [square], far_stack, own_scaled)
+    (response,) = in_vmem(
+        finish_kernel,
+        [kept],
+        mine,
+        sent(theirs, other_core),
+        far_own,
+        sent(far_own, other_core),
+        tile,
+        half_tile,
+    )
+    return response.T
+
+
 def solution(mesh):
     in_specs = (P(("parts", "aux"), "pair"), P(("parts", "pair")), P("parts"), P("parts"))
     out_specs = P(("parts", "aux"), "pair")
+    octet = mesh.shape["aux"] == 8 and mesh.shape["pair"] == 2
+    shards = octet_shards if octet else ring_shards
     return jax.shard_map(shards, mesh=mesh, in_specs=in_specs, out_specs=out_specs, check_vma=False)

time: 41 us -> 23.6 us (0.58)
  waiting for transfers between devices: 14.1 us -> 7.2 us
  matrix products: 4.67 us -> 0 us
  local copies, waits for them, and re-layouts: 4.26 us -> 0.2 us
  blocking collectives: 3.17 us -> 0 us
  Pallas kernels: 0 us -> 2.31 us
  starting transfers between devices: 13 us -> 12.2 us
  other arithmetic: 0.08 us -> 0.76 us
  between operations: 1.44 us -> 0.78 us
    ppermute x4 -> x8, waiting for transfers between devices: 14.1 us -> 7.2 us  [sent(): return lax.ppermute(value, ('aux', 'pair'), pairs)]
    dot_general x5 -> x0, matrix products: 4.67 us -> none  [product_tile(): lax.dot_general(scaled_rows, block_rows, (((1,), (1,)), ((), ())), precis...]
    unnamed x1 -> x0, blocking collectives: 3.17 us -> none
    unnamed x12 -> x2, local copies, waits for them, and re-layouts: 2.45 us -> 0.01 us
    pallas_call x0 -> x11, Pallas kernels: none -> 2.31 us  [in_vmem(): pl.pallas_call(kernel, out_shape=[jax.ShapeDtypeStruct(*out) for out in o...]
    unnamed x1 -> x0, starting transfers between devices: 2.27 us -> none
    dynamic_update_slice x4 -> x0, local copies, waits for them, and re-layouts: 1.73 us -> none  [write_block(): return lax.dynamic_update_slice_in_dim(collected, values, column, 1)]
    ppermute x4 -> x8, starting transfers between devices: 10.8 us -> 12.2 us  [sent(): return lax.ppermute(value, ('aux', 'pair'), pairs)]
  transfers between devices with their start and end apart: 5 -> 8, of which waited for: 4 -> 2; matrix products, arithmetic and copies ran while one was open for 14% -> 4% of each run, Pallas kernels for 0% -> 4%
where the time goes in v3:
time: 23.6 us; the launch traced here: 23.5 us
  starting transfers between devices  12.2 us (52%)
  waiting for transfers between devices  7.2 us (31%)
  Pallas kernels  2.31 us (10%)
  between operations  0.78 us (3%)
  other arithmetic  0.76 us (3%)
    ppermute x8, starting transfers between devices, sent(): return lax.ppermute(value, ('aux', 'pair'), pairs)  12.2 us
    ppermute x8, waiting for transfers between devices, sent(): return lax.ppermute(value, ('aux', 'pair'), pairs)  7.2 us
    pallas_call x11, Pallas kernels, in_vmem(): pl.pallas_call(kernel, out_shape=[jax.ShapeDtypeStruct(*out) for out in o...  2.31 us
    div x1, other arithmetic, pair_weights(): 4.0 * energy_gap / (energy_gap * energy_gap + frequency[0] * frequency[0])  0.76 us
  transfers between devices with their start and end apart: 8, of which 2 were waited for; matrix products, arithmetic and copies ran while one was open for 4% of the time, Pallas kernels for 4%

profile of v3, /device:TPU:0, one launch (start us, length us, event | category | flops | bytes accessed | tf_op | source)
XLA Modules:
  0.0 23.5 jit_solution(7123268989124164045)
XLA Ops:
  0.0 0.0 copy-start
  0.0 4.0 %collective-permute-start.3 = (f32[400,126]{1,0:T(8,128)}, f32[400,126]{1,0:T(8,128)S(1)}, u32[]{:S(2)}, u32[]{:S(2)}) collective-permute-start(f32[400,126]{1,0:T(8,128)} %bitcast.3), channel_id=1, source_target_pairs={{0,8},{1,9},{2,10},{3,11},{4,12},{5,13},{6,14},{7,15},{8,0},{9,1},... | collective-permute-start | bytes 604808 | tf_op jit(solution)/shard_map/ppermute | solution.py:75
  4.0 2.5 %collective-permute-start.1 = (f32[400,126]{1,0:T(8,128)}, f32[400,126]{1,0:T(8,128)S(1)}, u32[]{:S(2)}, u32[]{:S(2)}) collective-permute-start(f32[400,126]{1,0:T(8,128)} %bitcast.4), channel_id=1, source_target_pairs={{0,6},{1,7},{2,4},{3,5},{4,0},{5,1},{6,2},{7,3},{8,14},{9,15},{10,... | collective-permute-start | bytes 604808 | tf_op jit(solution)/shard_map/ppermute | solution.py:75
  6.5 0.5 %collective-permute-start = (f32[400,126]{1,0:T(8,128)}, f32[400,126]{1,0:T(8,128)S(1)}, u32[]{:S(2)}, u32[]{:S(2)}) collective-permute-start(f32[400,126]{1,0:T(8,128)} %bitcast.5), channel_id=1, source_target_pairs={{0,2},{1,3},{2,0},{3,1},{4,6},{5,7},{6,4},{7,5},{8,10},{9,11},{10,... | collective-permute-start | bytes 604808 | tf_op jit(solution)/shard_map/ppermute | solution.py:75
  7.7 0.8 %fusion = f32[2,200]{1,0:T(2,128)S(1)} fusion(f32[]{:T(128)} %bitcast.1, f32[200]{0:T(256)} %param.6, f32[2]{0:T(128)} %param.5), kind=kLoop, calls=%fused_computation.2 | loop fusion | flops 2000 | bytes 2412 | tf_op jit(solution)/shard_map/div | solution.py:18
  8.5 0.1 div.11
  8.6 0.1 broadcast_in_dim.2.weight
  8.7 0.0 copy-done
  8.7 0.1 shard_map.47.own_scaled
  8.8 5.3 %collective-permute-done.1.block = f32[400,126]{1,0:T(8,128)S(1)} collective-permute-done((f32[400,126]{1,0:T(8,128)}, f32[400,126]{1,0:T(8,128)S(1)}, u32[]{:S(2)}, u32[]{:S(2)}) %collective-permute-start.1) | collective-permute-done | bytes 201632 | tf_op jit(solution)/shard_map/ppermute | solution.py:75
  14.1 0.0 collective-permute-done.block
  14.1 0.1 shard_map.49.xp
  14.2 0.1 shard_map.53.xp_scaled
  14.2 0.0 collective-permute-done.3.block
  14.3 0.1 shard_map.51.far
  14.3 0.5 %shard_map.54 = (f32[189,126]{1,0:T(8,128)S(1)}, f32[189,126]{1,0:T(8,128)S(1)}) custom-call(bf16[1200,128]{1,0:T(8,128)(2,1)S(1)} %shard_map.51.far, bf16[1200,128]{1,0:T(8,128)(2,1)S(1)} %shard_map.49.xp, bf16[1200,128]{1,0:T(8,128)(2,1)S(1)} %shard_map.53.xp_scaled, bf16[1200,128]{1,0:T(8,128)(2,1)S(1)} %shard_map.48.zn_scaled), custom_call_target="tpu_custom_call" | custom-call | flops 1000 | bytes 1000 | tf_op jit(solution)/shard_map/pallas_call | solution.py:256
  14.8 0.1 collective-permute-start.5
  14.9 0.1 shard_map.46.own
  15.0 0.5 %shard_map.50 = (f32[315,126]{1,0:T(8,128)S(1)}, f32[315,126]{1,0:T(8,128)S(1)}) custom-call(bf16[1200,128]{1,0:T(8,128)(2,1)S(1)} %shard_map.46.own, bf16[1200,128]{1,0:T(8,128)(2,1)S(1)} %shard_map.47.own_scaled, bf16[1200,128]{1,0:T(8,128)(2,1)S(1)} %shard_map.49.xp, bf16[1200,128]{1,0:T(8,128)(2,1)S(1)} %shard_map.48.zn_scaled), custom_call_target="tpu_custom_call" | custom-call | flops 1000 | bytes 1000 | tf_op jit(solution)/shard_map/pallas_call | solution.py:256
  15.5 0.6 %collective-permute-start.2 = (f32[315,126]{1,0:T(8,128)S(1)}, f32[315,126]{1,0:T(8,128)S(1)}, u32[]{:S(2)}, u32[]{:S(2)}) collective-permute-start(f32[315,126]{1,0:T(8,128)S(1)} %get-tuple-element.16), channel_id=1, source_target_pairs={{0,1},{1,0},{2,3},{3,2},{4,5},{5,4},{6,7},{7,6},{8,9},{9,8},{10,11... | collective-permute-start | bytes 476288 | tf_op jit(solution)/shard_map/ppermute | solution.py:75
  16.0 0.3 %shard_map.52.far_own = f32[126,126]{1,0:T(8,128)S(1)} custom-call(bf16[1200,128]{1,0:T(8,128)(2,1)S(1)} %shard_map.51.far, bf16[1200,128]{1,0:T(8,128)(2,1)S(1)} %shard_map.47.own_scaled), custom_call_target="tpu_custom_call" | custom-call | flops 1000 | bytes 1000 | tf_op jit(solution)/shard_map/pallas_call | solution.py:256
  16.3 0.1 collective-permute-start.4
  16.4 0.0 collective-permute-done.5.theirs
  16.4 1.5 %collective-permute-start.6 = (f32[126,126]{1,0:T(8,128)S(1)}, f32[126,126]{1,0:T(8,128)S(1)}, u32[]{:S(2)}, u32[]{:S(2)}) collective-permute-start(f32[126,126]{1,0:T(8,128)S(1)} %get-tuple-element.19), channel_id=1, source_target_pairs={{0,2},{1,3},{2,0},{3,1},{4,7},{5,13},{6,14},{7,4},{8,10},{9,11},{1... | collective-permute-start | bytes 190520 | tf_op jit(solution)/shard_map/ppermute | solution.py:75
  18.0 2.9 %collective-permute-start.7 = (f32[63,126]{1,0:T(8,128)S(1)}, f32[63,126]{1,0:T(8,128)S(1)}, u32[]{:S(2)}, u32[]{:S(2)}) collective-permute-start(f32[63,126]{1,0:T(8,128)S(1)} %get-tuple-element.20), channel_id=1, source_target_pairs={{0,4},{1,5},{2,6},{3,7},{4,0},{5,1},{6,2},{7,3},{8,12},{9,13},{10,... | collective-permute-start | bytes 95264 | tf_op jit(solution)/shard_map/ppermute | solution.py:75
  20.9 0.0 collective-permute-done.4.far_own2
  20.9 1.9 %collective-permute-done.7.half_tile = f32[63,126]{1,0:T(8,128)S(1)} collective-permute-done((f32[63,126]{1,0:T(8,128)S(1)}, f32[63,126]{1,0:T(8,128)S(1)}, u32[]{:S(2)}, u32[]{:S(2)}) %collective-permute-start.7) | collective-permute-done | bytes 31784 | tf_op jit(solution)/shard_map/ppermute | solution.py:75
  22.8 0.0 collective-permute-done.2.theirs
  22.8 0.0 collective-permute-done.6.tile
  22.8 0.7 %shard_map.56 = f32[315,126]{1,0:T(8,128)} custom-call(f32[315,126]{1,0:T(8,128)S(1)} %get-tuple-element.15.mine, f32[315,126]{1,0:T(8,128)S(1)} %collective-permute-done.2.theirs, f32[126,126]{1,0:T(8,128)S(1)} %shard_map.52.far_own, f32[126,126]{1,0:T(8,128)S(1)} %collective-permute-done.4.far_own2, f32[126,126]{1,0:T(8,128)S(1)} %collective-permute-done.6.tile, ...), custom_call_target="tpu_custom_call" | custom-call | flops 1000 | bytes 1000 | tf_op jit(solution)/shard_map/pallas_call | solution.py:256
  (2 shorter events, 0.1 us)
Async XLA Ops:
  0.0 8.7 %copy-start = (f32[126,400]{0,1:T(8,128)S(1)}, f32[126,400]{0,1:T(8,128)}, u32[]{:S(2)}) copy-start(f32[126,400]{0,1:T(8,128)} %param.4) | copy-start | bytes 604804
  0.0 14.2 %collective-permute-start.3 = (f32[400,126]{1,0:T(8,128)}, f32[400,126]{1,0:T(8,128)S(1)}, u32[]{:S(2)}, u32[]{:S(2)}) collective-permute-start(f32[400,126]{1,0:T(8,128)} %bitcast.3), channel_id=1, source_target_pairs={{0,8},{1,9},{2,10},{3,11},{4,12},{5,13},{6,14},{7,15},{8,0},{9,1},... | collective-permute-start | bytes 604808 | tf_op jit(solution)/shard_map/ppermute | solution.py:75
  4.0 10.0 %collective-permute-start.1 = (f32[400,126]{1,0:T(8,128)}, f32[400,126]{1,0:T(8,128)S(1)}, u32[]{:S(2)}, u32[]{:S(2)}) collective-permute-start(f32[400,126]{1,0:T(8,128)} %bitcast.4), channel_id=1, source_target_pairs={{0,6},{1,7},{2,4},{3,5},{4,0},{5,1},{6,2},{7,3},{8,14},{9,15},{10,... | collective-permute-start | bytes 604808 | tf_op jit(solution)/shard_map/ppermute | solution.py:75
  6.5 7.6 %collective-permute-start = (f32[400,126]{1,0:T(8,128)}, f32[400,126]{1,0:T(8,128)S(1)}, u32[]{:S(2)}, u32[]{:S(2)}) collective-permute-start(f32[400,126]{1,0:T(8,128)} %bitcast.5), channel_id=1, source_target_pairs={{0,2},{1,3},{2,0},{3,1},{4,6},{5,7},{6,4},{7,5},{8,10},{9,11},{10,... | collective-permute-start | bytes 604808 | tf_op jit(solution)/shard_map/ppermute | solution.py:75
  14.8 1.6 %collective-permute-start.5 = (f32[189,126]{1,0:T(8,128)S(1)}, f32[189,126]{1,0:T(8,128)S(1)}, u32[]{:S(2)}, u32[]{:S(2)}) collective-permute-start(f32[189,126]{1,0:T(8,128)S(1)} %get-tuple-element.18), channel_id=1, source_target_pairs={{0,1},{1,0},{2,3},{3,2},{4,5},{5,4},{6,7},{7,6},{8,9},{9,8},{10,11... | collective-permute-start | bytes 285776 | tf_op jit(solution)/shard_map/ppermute | solution.py:75
  15.5 7.3 %collective-permute-start.2 = (f32[315,126]{1,0:T(8,128)S(1)}, f32[315,126]{1,0:T(8,128)S(1)}, u32[]{:S(2)}, u32[]{:S(2)}) collective-permute-start(f32[315,126]{1,0:T(8,128)S(1)} %get-tuple-element.16), channel_id=1, source_target_pairs={{0,1},{1,0},{2,3},{3,2},{4,5},{5,4},{6,7},{7,6},{8,9},{9,8},{10,11... | collective-permute-start | bytes 476288 | tf_op jit(solution)/shard_map/ppermute | solution.py:75
  16.3 4.5 %collective-permute-start.4 = (f32[126,126]{1,0:T(8,128)S(1)}, f32[126,126]{1,0:T(8,128)S(1)}, u32[]{:S(2)}, u32[]{:S(2)}) collective-permute-start(f32[126,126]{1,0:T(8,128)S(1)} %shard_map.52.far_own), channel_id=1, source_target_pairs={{0,1},{1,0},{2,3},{3,2},{4,5},{5,4},{6,7},{7,6},{8,9},{9,8},{10,11... | collective-permute-start | bytes 190520 | tf_op jit(solution)/shard_map/ppermute | solution.py:75
  16.4 6.3 %collective-permute-start.6 = (f32[126,126]{1,0:T(8,128)S(1)}, f32[126,126]{1,0:T(8,128)S(1)}, u32[]{:S(2)}, u32[]{:S(2)}) collective-permute-start(f32[126,126]{1,0:T(8,128)S(1)} %get-tuple-element.19), channel_id=1, source_target_pairs={{0,2},{1,3},{2,0},{3,1},{4,7},{5,13},{6,14},{7,4},{8,10},{9,11},{1... | collective-permute-start | bytes 190520 | tf_op jit(solution)/shard_map/ppermute | solution.py:75
  18.0 4.8 %collective-permute-start.7 = (f32[63,126]{1,0:T(8,128)S(1)}, f32[63,126]{1,0:T(8,128)S(1)}, u32[]{:S(2)}, u32[]{:S(2)}) collective-permute-start(f32[63,126]{1,0:T(8,128)S(1)} %get-tuple-element.20), channel_id=1, source_target_pairs={{0,4},{1,5},{2,6},{3,7},{4,0},{5,1},{6,2},{7,3},{8,12},{9,13},{10,... | collective-permute-start | bytes 95264 | tf_op jit(solution)/shard_map/ppermute | solution.py:75

commit v4 on v3

--- a/solution.py
+++ b/solution.py
@@ -125,6 +125,17 @@
         stack[pl.ds(i * pairs, pairs), pl.ds(0, rows)] = parts[part]
 
 
+def both_kernel(weight, block, stack, scaled):
+    stack_kernel((0, 1, 0), block, stack)
+    scaled_kernel(weight, block, scaled)
+
+
+def three_kernel(weight, block, far, stack, scaled, far_stack):
+    stack_kernel((0, 1, 0), block, stack)
+    stack_kernel((0, 1, 0), far, far_stack)
+    scaled_kernel(weight, block, scaled)
+
+
 def meet_kernel(far, xp, xp_scaled, zn_scaled, mine, theirs):
     even, x, c = place()
     rows = mine.shape[1]
@@ -189,17 +200,54 @@
     )
 
 
-def local_kernel(own, own_scaled, xp, zn_scaled, mine, theirs):
-    even, x, c = place()
+def own_kernel(own, own_scaled, own_own):
+    rows = own_own.shape[0]
+    own_own[...] = dot_over_pairs(own[...], own_scaled[...])[:rows, :rows]
+
+
+def far_kernel(far, own_scaled, far_own):
+    rows = far_own.shape[0]
+    far_own[...] = dot_over_pairs(far[...], own_scaled[...])[:rows, :rows]
+
+
+def local_kernel(own, own_scaled, own_own, far, xp, zn_scaled, mine, theirs):
+    _, _, c = place()
     rows = mine.shape[1]
     half = rows // 2
-    own_stack = own[...]
-    by_own = dot_over_pairs(jnp.concatenate([own_stack, xp[...]], 1), own_scaled[...])
-    own_own, xp_own = by_own[:rows, :rows], by_own[128 : 128 + rows, :rows]
-    zn_own = dot_over_pairs(zn_scaled[...], own_stack)[:rows, :rows]
+    by_own = dot_over_pairs(jnp.concatenate([far[...], xp[...]], 1), own_scaled[...])
+    far_own, xp_own = by_own[:rows, :rows], by_own[128 : 128 + rows, :rows]
+    zn_own = dot_over_pairs(zn_scaled[...], own[...])[:rows, :rows]
 
     def first(kept):
-        kept[pl.ds(0, rows), :] = own_own
+        kept[pl.ds(0, rows), :] = own_own[...]
+        kept[pl.ds(rows, rows), :] = xp_own
+        kept[pl.ds(2 * rows, half), :] = zn_own[:half]
+
+    def second(kept):
+        kept[pl.ds(0, half), :] = zn_own[half:]
+        kept[pl.ds(half, rows), :] = jnp.zeros((rows, rows), jnp.float32)
+        kept[pl.ds(half + rows, rows), :] = far_own
+
+    @pl.when(c == 0)
+    def _():
+        first(mine)
+        second(theirs)
+
+    @pl.when(c == 1)
+    def _():
+        first(theirs)
+        second(mine)
+
+
+def local2_kernel(own, own_scaled, own_own, xp, zn_scaled, mine, theirs):
+    _, _, c = place()
+    rows = mine.shape[1]
+    half = rows // 2
+    xp_own = dot_over_pairs(xp[...], own_scaled[...])[:rows, :rows]
+    zn_own = dot_over_pairs(zn_scaled[...], own[...])[:rows, :rows]
+
+    def first(kept):
+        kept[pl.ds(0, rows), :] = own_own[...]
         kept[pl.ds(rows, rows), :] = xp_own
         kept[pl.ds(2 * rows, half), :] = zn_own[:half]
 
@@ -218,16 +266,30 @@
         second(mine)
 
 
-def far_kernel(weight, own, far, far_own):
-    far_own[...] = tile_of(far[...], own[...] * weight[...])
-
-
-def far_kernel(far, own_scaled, far_own):
-    rows = far_own.shape[0]
-    far_own[...] = dot_over_pairs(far[...], own_scaled[...])[:rows, :rows]
-
-
-def finish_kernel(mine, theirs, far_own, far_own2, tile, half_tile, response):
+def finish_kernel(mine, theirs, tile, half_tile, response):
+    even, x, c = place()
+    rows = tile.shape[0]
+    half = rows // 2
+    response[...] = mine[...] + theirs[...]
+
+    @pl.when((c == 0) & (x == 1))
+    def _():
+        response[pl.ds(rows, rows), :] = tile[...]
+
+    @pl.when(c == 1)
+    def _():
+        response[pl.ds(half, rows), :] = tile[...]
+
+    @pl.when((c == 0) & ~even)
+    def _():
+        response[pl.ds(2 * rows, half), :] = half_tile[...]
+
+    @pl.when((c == 1) & ~even)
+    def _():
+        response[pl.ds(0, half), :] = half_tile[...]
+
+
+def finish2_kernel(mine, theirs, far_own, far_own2, tile, half_tile, response):
     even, x, c = place()
     rows = tile.shape[0]
     half = rows // 2
@@ -270,41 +332,32 @@
         pair_weights(occ_energy, vir_energy, frequency)[:, None], (pairs, rows)
     )
     stack = ((3 * pairs, 128), jnp.bfloat16)
+    square, half_square = ((rows, rows), jnp.float32), ((rows // 2, rows), jnp.float32)
     plain = functools.partial(stack_kernel, (0, 1, 0))
     far = sent(own, far_chip)
     xp = sent(own, other_x)
     zn = sent(own, next_chip)
-    (far_stack,) = in_vmem(plain, [stack], far, flops=10**11)
+    xp_stack, xp_scaled, far_stack = in_vmem(three_kernel, [stack] * 3, weight, xp, far)
+    zn, xp_scaled = lax.optimization_barrier((zn, xp_scaled))
     (zn_scaled,) = in_vmem(scaled_kernel, [stack], weight, zn)
-    xp, zn_scaled = lax.optimization_barrier((xp, zn_scaled))
-    (xp_stack,) = in_vmem(plain, [stack], xp)
-    (xp_scaled,) = in_vmem(scaled_kernel, [stack], weight, xp)
+    (own_stack,) = in_vmem(plain, [stack], own)
+    (own_scaled,) = in_vmem(scaled_kernel, [stack], weight, own)
+    (own_own,) = in_vmem(own_kernel, [square], own_stack, own_scaled)
     parts = ((3 * rows // 2, rows), jnp.float32)
     mine, theirs = in_vmem(
-        meet_kernel, [parts] * 2, far_stack, xp_stack, xp_scaled, zn_scaled
-    )
-    square, half_square = ((rows, rows), jnp.float32), ((rows // 2, rows), jnp.float32)
+        meet_kernel, [parts] * 2, far_stack, xp_stack, xp_scaled, zn_scaled, flops=1000
+    )
     tile, half_tile = in_vmem(
         sum_kernel, [square, half_square], mine, sent(theirs, other_core)
     )
     tile = sent(tile, tile_chip)
     half_tile = sent(half_tile, half_tile_chip)
-    (own_stack,) = in_vmem(plain, [stack], own)
-    (own_scaled,) = in_vmem(scaled_kernel, [stack], weight, own)
     kept = ((5 * rows // 2, rows), jnp.float32)
     mine, theirs = in_vmem(
-        local_kernel, [kept] * 2, own_stack, own_scaled, xp_stack, zn_scaled
-    )
-    (far_own,) = in_vmem(far_kernel, [square], far_stack, own_scaled)
+        local_kernel, [kept] * 2, own_stack, own_scaled, own_own, far_stack, xp_stack, zn_scaled, flops=1000
+    )
     (response,) = in_vmem(
-        finish_kernel,
-        [kept],
-        mine,
-        sent(theirs, other_core),
-        far_own,
-        sent(far_own, other_core),
-        tile,
-        half_tile,
+        finish_kernel, [kept], mine, sent(theirs, other_core), tile, half_tile
     )
     return response.T
 

time: 23.6 us -> 22.7 us (0.962)
  starting transfers between devices: 12.2 us -> 10.4 us
  local copies, waits for them, and re-layouts: 0.2 us -> 1.18 us
  other arithmetic: 0.76 us -> 0.08 us
  waiting for transfers between devices: 7.2 us -> 7.83 us
    ppermute x8 -> x7, starting transfers between devices: 12.2 us -> 10.4 us  [sent(): return lax.ppermute(value, ('aux', 'pair'), pairs)]
    unnamed x2 -> x8, local copies, waits for them, and re-layouts: 0.01 us -> 0.98 us
    div x1, other arithmetic: 0.76 us -> 0.08 us  [pair_weights(): 4.0 * energy_gap / (energy_gap * energy_gap + frequency[0] * frequency[0])]
    ppermute x8 -> x7, waiting for transfers between devices: 7.2 us -> 7.83 us  [sent(): return lax.ppermute(value, ('aux', 'pair'), pairs)]
    pallas_call x11 -> x9, Pallas kernels: 2.31 us -> 2.31 us  [in_vmem(): pl.pallas_call(kernel, out_shape=[jax.ShapeDtypeStruct(*out) for out in o...]
  transfers between devices with their start and end apart: 8 -> 7, of which waited for: 2 -> 2; matrix products, arithmetic and copies ran while one was open for 4% -> 1% of each run, Pallas kernels for 4% -> 5%
where the time goes in v4:
time: 22.7 us; the launch traced here: 22.5 us
  starting transfers between devices  10.4 us (46%)
  waiting for transfers between devices  7.83 us (34%)
  Pallas kernels  2.31 us (10%)
  local copies, waits for them, and re-layouts  1.18 us (5%)
  between operations  0.8 us (4%)
    ppermute x7, starting transfers between devices, sent(): return lax.ppermute(value, ('aux', 'pair'), pairs)  10.4 us
    ppermute x7, waiting for transfers between devices, sent(): return lax.ppermute(value, ('aux', 'pair'), pairs)  7.83 us
    pallas_call x9, Pallas kernels, in_vmem(): pl.pallas_call(kernel, out_shape=[jax.ShapeDtypeStruct(*out) for out in o...  2.31 us
    unnamed x8, local copies, waits for them, and re-layouts  0.98 us
  transfers between devices with their start and end apart: 7, of which 2 were waited for; matrix products, arithmetic and copies ran while one was open for 1% of the time, Pallas kernels for 5%

profile of v4, /device:TPU:0, one launch (start us, length us, event | category | flops | bytes accessed | tf_op | source)
XLA Modules:
  0.0 22.5 jit_solution(7843889498490841337)
XLA Ops:
  0.0 2.9 %collective-permute-start = (f32[400,126]{1,0:T(8,128)}, f32[400,126]{1,0:T(8,128)S(1)}, u32[]{:S(2)}, u32[]{:S(2)}) collective-permute-start(f32[400,126]{1,0:T(8,128)} %bitcast.3), channel_id=1, source_target_pairs={{0,2},{1,3},{2,0},{3,1},{4,6},{5,7},{6,4},{7,5},{8,10},{9,11},{10,... | collective-permute-start | bytes 604808 | tf_op jit(solution)/shard_map/ppermute | solution.py:75
  2.9 2.6 %collective-permute-start.1 = (f32[400,126]{1,0:T(8,128)}, f32[400,126]{1,0:T(8,128)S(1)}, u32[]{:S(2)}, u32[]{:S(2)}) collective-permute-start(f32[400,126]{1,0:T(8,128)} %bitcast.4), channel_id=1, source_target_pairs={{0,8},{1,9},{2,10},{3,11},{4,12},{5,13},{6,14},{7,15},{8,0},{9,1},... | collective-permute-start | bytes 604808 | tf_op jit(solution)/shard_map/ppermute | solution.py:75
  5.5 1.5 %collective-permute-start.2 = (f32[400,126]{1,0:T(8,128)}, f32[400,126]{1,0:T(8,128)S(1)}, u32[]{:S(2)}, u32[]{:S(2)}) collective-permute-start(f32[400,126]{1,0:T(8,128)} %bitcast.5), channel_id=1, source_target_pairs={{0,6},{1,7},{2,4},{3,5},{4,0},{5,1},{6,2},{7,3},{8,14},{9,15},{10,... | collective-permute-start | bytes 604808 | tf_op jit(solution)/shard_map/ppermute | solution.py:75
  7.1 0.0 copy-start
  7.1 1.0 %copy-done = f32[126,400]{0,1:T(8,128)S(1)} copy-done((f32[126,400]{0,1:T(8,128)S(1)}, f32[126,400]{0,1:T(8,128)}, u32[]{:S(2)}) %copy-start) | copy-done | bytes 201624
  8.0 0.0 copy-start.2
  8.0 0.0 copy-start.3
  8.0 0.1 shard_map.46.own
  8.1 0.0 copy-start.1
  8.8 0.0 copy-done.2
  8.8 0.0 copy-done.3
  8.8 0.1 fusion
  8.9 0.1 div.11
  9.0 0.1 broadcast_in_dim.2.weight
  9.1 0.0 copy-done.1
  9.1 0.1 shard_map.47.own_scaled
  9.2 0.0 collective-permute-done.block
  9.2 5.9 %collective-permute-done.1.far = f32[400,126]{1,0:T(8,128)S(1)} collective-permute-done((f32[400,126]{1,0:T(8,128)}, f32[400,126]{1,0:T(8,128)S(1)}, u32[]{:S(2)}, u32[]{:S(2)}) %collective-permute-start.1) | collective-permute-done | bytes 201632 | tf_op jit(solution)/shard_map/ppermute | solution.py:75
  15.1 0.2 shard_map.49
  15.3 0.0 collective-permute-done.2.block
  15.3 0.5 %shard_map.52 = (f32[189,126]{1,0:T(8,128)S(1)}, f32[189,126]{1,0:T(8,128)S(1)}) custom-call(bf16[1200,128]{1,0:T(8,128)(2,1)S(1)} %get-tuple-element.16.far, bf16[1200,128]{1,0:T(8,128)(2,1)S(1)} %get-tuple-element.17.xp, bf16[1200,128]{1,0:T(8,128)(2,1)S(1)} %get-tuple-element.22.xp_scaled, bf16[1200,128]{1,0:T(8,128)(2,1)S(1)} %shard_map.50.zn_scaled), custom_call_target="tpu_custom_call" | custom-call | flops 1000 | bytes 1000 | tf_op jit(solution)/shard_map/pallas_call | solution.py:318
  15.8 0.1 collective-permute-start.4
  15.9 0.3 %shard_map.48.own_own = f32[126,126]{1,0:T(8,128)S(1)} custom-call(bf16[1200,128]{1,0:T(8,128)(2,1)S(1)} %shard_map.46.own, bf16[1200,128]{1,0:T(8,128)(2,1)S(1)} %shard_map.47.own_scaled), custom_call_target="tpu_custom_call" | custom-call | flops 1000 | bytes 1000 | tf_op jit(solution)/shard_map/pallas_call | solution.py:318
  16.2 0.5 %shard_map.51 = (f32[315,126]{1,0:T(8,128)S(1)}, f32[315,126]{1,0:T(8,128)S(1)}) custom-call(bf16[1200,128]{1,0:T(8,128)(2,1)S(1)} %shard_map.46.own, bf16[1200,128]{1,0:T(8,128)(2,1)S(1)} %shard_map.47.own_scaled, f32[126,126]{1,0:T(8,128)S(1)} %shard_map.48.own_own, bf16[1200,128]{1,0:T(8,128)(2,1)S(1)} %get-tuple-element.16.far, ...), custom_call_target="tpu_custom_call" | custom-call | flops 1000 | bytes 1000 | tf_op jit(solution)/shard_map/pallas_call | solution.py:318
  16.7 0.6 %collective-permute-start.3 = (f32[315,126]{1,0:T(8,128)S(1)}, f32[315,126]{1,0:T(8,128)S(1)}, u32[]{:S(2)}, u32[]{:S(2)}) collective-permute-start(f32[315,126]{1,0:T(8,128)S(1)} %get-tuple-element.21), channel_id=1, source_target_pairs={{0,1},{1,0},{2,3},{3,2},{4,5},{5,4},{6,7},{7,6},{8,9},{9,8},{10,11... | collective-permute-start | bytes 476288 | tf_op jit(solution)/shard_map/ppermute | solution.py:75
  17.3 0.0 collective-permute-done.4.theirs
  17.3 0.6 %collective-permute-start.5 = (f32[126,126]{1,0:T(8,128)S(1)}, f32[126,126]{1,0:T(8,128)S(1)}, u32[]{:S(2)}, u32[]{:S(2)}) collective-permute-start(f32[126,126]{1,0:T(8,128)S(1)} %get-tuple-element.25), channel_id=1, source_target_pairs={{0,2},{1,3},{2,0},{3,1},{4,7},{5,13},{6,14},{7,4},{8,10},{9,11},{1... | collective-permute-start | bytes 190520 | tf_op jit(solution)/shard_map/ppermute | solution.py:75
  17.9 2.1 %collective-permute-start.6 = (f32[63,126]{1,0:T(8,128)S(1)}, f32[63,126]{1,0:T(8,128)S(1)}, u32[]{:S(2)}, u32[]{:S(2)}) collective-permute-start(f32[63,126]{1,0:T(8,128)S(1)} %get-tuple-element.26), channel_id=1, source_target_pairs={{0,4},{1,5},{2,6},{3,7},{4,0},{5,1},{6,2},{7,3},{8,12},{9,13},{10,... | collective-permute-start | bytes 95264 | tf_op jit(solution)/shard_map/ppermute | solution.py:75
  20.0 1.9 %collective-permute-done.6.half_tile = f32[63,126]{1,0:T(8,128)S(1)} collective-permute-done((f32[63,126]{1,0:T(8,128)S(1)}, f32[63,126]{1,0:T(8,128)S(1)}, u32[]{:S(2)}, u32[]{:S(2)}) %collective-permute-start.6) | collective-permute-done | bytes 31784 | tf_op jit(solution)/shard_map/ppermute | solution.py:75
  21.8 0.0 collective-permute-done.3.theirs
  21.8 0.0 collective-permute-done.5.tile
  21.9 0.7 %shard_map.54 = f32[315,126]{1,0:T(8,128)} custom-call(f32[315,126]{1,0:T(8,128)S(1)} %get-tuple-element.20.mine, f32[315,126]{1,0:T(8,128)S(1)} %collective-permute-done.3.theirs, f32[126,126]{1,0:T(8,128)S(1)} %collective-permute-done.5.tile, f32[63,126]{1,0:T(8,128)S(1)} %collective-permute-done.6.half_tile), custom_call_target="tpu_custom_call" | custom-call | flops 1000 | bytes 1000 | tf_op jit(solution)/shard_map/pallas_call | solution.py:318
  (2 shorter events, 0.1 us)
Async XLA Ops:
  0.0 9.2 %collective-permute-start = (f32[400,126]{1,0:T(8,128)}, f32[400,126]{1,0:T(8,128)S(1)}, u32[]{:S(2)}, u32[]{:S(2)}) collective-permute-start(f32[400,126]{1,0:T(8,128)} %bitcast.3), channel_id=1, source_target_pairs={{0,2},{1,3},{2,0},{3,1},{4,6},{5,7},{6,4},{7,5},{8,10},{9,11},{10,... | collective-permute-start | bytes 604808 | tf_op jit(solution)/shard_map/ppermute | solution.py:75
  2.9 12.2 %collective-permute-start.1 = (f32[400,126]{1,0:T(8,128)}, f32[400,126]{1,0:T(8,128)S(1)}, u32[]{:S(2)}, u32[]{:S(2)}) collective-permute-start(f32[400,126]{1,0:T(8,128)} %bitcast.4), channel_id=1, source_target_pairs={{0,8},{1,9},{2,10},{3,11},{4,12},{5,13},{6,14},{7,15},{8,0},{9,1},... | collective-permute-start | bytes 604808 | tf_op jit(solution)/shard_map/ppermute | solution.py:75
  5.5 9.7 %collective-permute-start.2 = (f32[400,126]{1,0:T(8,128)}, f32[400,126]{1,0:T(8,128)S(1)}, u32[]{:S(2)}, u32[]{:S(2)}) collective-permute-start(f32[400,126]{1,0:T(8,128)} %bitcast.5), channel_id=1, source_target_pairs={{0,6},{1,7},{2,4},{3,5},{4,0},{5,1},{6,2},{7,3},{8,14},{9,15},{10,... | collective-permute-start | bytes 604808 | tf_op jit(solution)/shard_map/ppermute | solution.py:75
  7.1 1.0 %copy-start = (f32[126,400]{0,1:T(8,128)S(1)}, f32[126,400]{0,1:T(8,128)}, u32[]{:S(2)}) copy-start(f32[126,400]{0,1:T(8,128)} %param.4) | copy-start | bytes 604804
  8.0 0.8 %copy-start.2 = (f32[200]{0:T(256)S(1)}, f32[200]{0:T(256)}, u32[]{:S(2)}) copy-start(f32[200]{0:T(256)} %param.6) | copy-start | bytes 2404
  8.0 0.8 %copy-start.3 = (f32[2]{0:T(128)S(1)}, f32[2]{0:T(128)}, u32[]{:S(2)}) copy-start(f32[2]{0:T(128)} %param.5) | copy-start | bytes 28
  8.1 1.0 %copy-start.1 = (f32[126,400]{0,1:T(8,128)S(1)}, f32[126,400]{0,1:T(8,128)}, u32[]{:S(2)}) copy-start(f32[126,400]{0,1:T(8,128)} %param.4) | copy-start | bytes 604804
  15.8 1.5 %collective-permute-start.4 = (f32[189,126]{1,0:T(8,128)S(1)}, f32[189,126]{1,0:T(8,128)S(1)}, u32[]{:S(2)}, u32[]{:S(2)}) collective-permute-start(f32[189,126]{1,0:T(8,128)S(1)} %get-tuple-element.24), channel_id=1, source_target_pairs={{0,1},{1,0},{2,3},{3,2},{4,5},{5,4},{6,7},{7,6},{8,9},{9,8},{10,11... | collective-permute-start | bytes 285776 | tf_op jit(solution)/shard_map/ppermute | solution.py:75
  16.7 5.1 %collective-permute-start.3 = (f32[315,126]{1,0:T(8,128)S(1)}, f32[315,126]{1,0:T(8,128)S(1)}, u32[]{:S(2)}, u32[]{:S(2)}) collective-permute-start(f32[315,126]{1,0:T(8,128)S(1)} %get-tuple-element.21), channel_id=1, source_target_pairs={{0,1},{1,0},{2,3},{3,2},{4,5},{5,4},{6,7},{7,6},{8,9},{9,8},{10,11... | collective-permute-start | bytes 476288 | tf_op jit(solution)/shard_map/ppermute | solution.py:75
  17.3 4.5 %collective-permute-start.5 = (f32[126,126]{1,0:T(8,128)S(1)}, f32[126,126]{1,0:T(8,128)S(1)}, u32[]{:S(2)}, u32[]{:S(2)}) collective-permute-start(f32[126,126]{1,0:T(8,128)S(1)} %get-tuple-element.25), channel_id=1, source_target_pairs={{0,2},{1,3},{2,0},{3,1},{4,7},{5,13},{6,14},{7,4},{8,10},{9,11},{1... | collective-permute-start | bytes 190520 | tf_op jit(solution)/shard_map/ppermute | solution.py:75
  17.9 4.0 %collective-permute-start.6 = (f32[63,126]{1,0:T(8,128)S(1)}, f32[63,126]{1,0:T(8,128)S(1)}, u32[]{:S(2)}, u32[]{:S(2)}) collective-permute-start(f32[63,126]{1,0:T(8,128)S(1)} %get-tuple-element.26), channel_id=1, source_target_pairs={{0,4},{1,5},{2,6},{3,7},{4,0},{5,1},{6,2},{7,3},{8,12},{9,13},{10,... | collective-permute-start | bytes 95264 | tf_op jit(solution)/shard_map/ppermute | solution.py:75

commit v5 on v3

--- a/solution.py
+++ b/solution.py
@@ -79,6 +79,9 @@
     return (z, x, 1 - c)
 
 
+ORDERS = (("xp", "zn", "far"), ("far", "zn", "xp"))
+
+
 def far_chip(z, x, c):
     return (z ^ 2, x, c)
 
@@ -111,32 +114,44 @@
     return high, (value - high.astype(jnp.float32)).astype(jnp.bfloat16)
 
 
-def stack_kernel(order, block, stack):
-    pairs, rows = block.shape
-    parts = halves(block[...])
-    for i, part in enumerate(order):
-        stack[pl.ds(i * pairs, pairs), pl.ds(0, rows)] = parts[part]
-
-
-def scaled_kernel(weight, block, stack):
-    pairs, rows = block.shape
-    parts = halves(block[...] * weight[...])
-    for i, part in enumerate((0, 0, 1)):
-        stack[pl.ds(i * pairs, pairs), pl.ds(0, rows)] = parts[part]
+def product(left, right):
+    return (
+        jnp.dot(left[0], right[0], preferred_element_type=jnp.float32)
+        + jnp.dot(left[1], right[0], preferred_element_type=jnp.float32)
+        + jnp.dot(left[0], right[1], preferred_element_type=jnp.float32)
+    )
+
+
+def left_kernel(block, left):
+    left[0], left[1] = halves(block[...].T)
+
+
+def right_kernel(weight, block, right):
+    columns = pl.ds(0, block.shape[1])
+    right[0, :, columns], right[1, :, columns] = halves(block[...] * weight[...])
+
+
+def ready_kernel(orders, weight, *refs):
+    blocks, (far_left, xp_left, xp_right, zn_right) = refs[:3], refs[3:]
+    _, _, c = place()
+    for core, order in enumerate(orders):
+
+        @pl.when(c == core)
+        def _():
+            left_kernel(blocks[order.index("far")], far_left)
+            left_kernel(blocks[order.index("xp")], xp_left)
+            right_kernel(weight, blocks[order.index("xp")], xp_right)
+            right_kernel(weight, blocks[order.index("zn")], zn_right)
 
 
 def meet_kernel(far, xp, xp_scaled, zn_scaled, mine, theirs):
     even, x, c = place()
     rows = mine.shape[1]
     half = rows // 2
-    tiles = lax.dot_general(
-        jnp.concatenate([far[...], xp[...]], 1),
-        jnp.concatenate([zn_scaled[...], xp_scaled[...]], 1),
-        (((0,), (0,)), ((), ())),
-        preferred_element_type=jnp.float32,
-    )
-    far_zn, far_xp = tiles[:rows, :rows], tiles[:rows, 128 : 128 + rows]
-    xp_zn = tiles[128 : 128 + rows, :rows]
+    scaled = [jnp.concatenate([zn_scaled[i], xp_scaled[i]], 1) for i in range(2)]
+    by_far = product(far, scaled)
+    far_zn, far_xp = by_far[:, :rows], by_far[:, 128 : 128 + rows]
+    xp_zn = product(xp, zn_scaled)[:, :rows]
 
     def put(core, row, values):
         @pl.when(c == core)
@@ -183,29 +198,27 @@
     half_tile[...] = mine[pl.ds(rows, half), :] + theirs[pl.ds(rows, half), :]
 
 
-def dot_over_pairs(left, right):
-    return lax.dot_general(
-        left, right, (((0,), (0,)), ((), ())), preferred_element_type=jnp.float32
-    )
-
-
-def local_kernel(own, own_scaled, xp, zn_scaled, mine, theirs):
-    even, x, c = place()
+def own_kernel(own, own_scaled, own_own):
+    own_own[...] = product(own, own_scaled)[:, : own_own.shape[1]]
+
+
+def local_kernel(own, own_scaled, own_own, far, xp, zn_scaled, mine, theirs):
+    _, _, c = place()
     rows = mine.shape[1]
     half = rows // 2
-    own_stack = own[...]
-    by_own = dot_over_pairs(jnp.concatenate([own_stack, xp[...]], 1), own_scaled[...])
-    own_own, xp_own = by_own[:rows, :rows], by_own[128 : 128 + rows, :rows]
-    zn_own = dot_over_pairs(zn_scaled[...], own_stack)[:rows, :rows]
+    far_own = product(far, own_scaled)[:, :rows]
+    xp_own = product(xp, own_scaled)[:, :rows]
+    zn_own = product(own, zn_scaled)[:, :rows].T
 
     def first(kept):
-        kept[pl.ds(0, rows), :] = own_own
+        kept[pl.ds(0, rows), :] = own_own[...]
         kept[pl.ds(rows, rows), :] = xp_own
         kept[pl.ds(2 * rows, half), :] = zn_own[:half]
 
     def second(kept):
         kept[pl.ds(0, half), :] = zn_own[half:]
-        kept[pl.ds(half, 2 * rows), :] = jnp.zeros((2 * rows, rows), jnp.float32)
+        kept[pl.ds(half, rows), :] = jnp.zeros((rows, rows), jnp.float32)
+        kept[pl.ds(half + rows, rows), :] = far_own
 
     @pl.when(c == 0)
     def _():
@@ -218,16 +231,7 @@
         second(mine)
 
 
-def far_kernel(weight, own, far, far_own):
-    far_own[...] = tile_of(far[...], own[...] * weight[...])
-
-
-def far_kernel(far, own_scaled, far_own):
-    rows = far_own.shape[0]
-    far_own[...] = dot_over_pairs(far[...], own_scaled[...])[:rows, :rows]
-
-
-def finish_kernel(mine, theirs, far_own, far_own2, tile, half_tile, response):
+def finish_kernel(mine, theirs, tile, half_tile, response):
     even, x, c = place()
     rows = tile.shape[0]
     half = rows // 2
@@ -240,7 +244,6 @@
     @pl.when(c == 1)
     def _():
         response[pl.ds(half, rows), :] = tile[...]
-        response[pl.ds(half + rows, rows), :] = far_own[...] + far_own2[...]
 
     @pl.when((c == 0) & ~even)
     def _():
@@ -269,42 +272,31 @@
     weight = jnp.broadcast_to(
         pair_weights(occ_energy, vir_energy, frequency)[:, None], (pairs, rows)
     )
-    stack = ((3 * pairs, 128), jnp.bfloat16)
-    plain = functools.partial(stack_kernel, (0, 1, 0))
-    far = sent(own, far_chip)
-    xp = sent(own, other_x)
-    zn = sent(own, next_chip)
-    (far_stack,) = in_vmem(plain, [stack], far, flops=10**11)
-    (zn_scaled,) = in_vmem(scaled_kernel, [stack], weight, zn)
-    xp, zn_scaled = lax.optimization_barrier((xp, zn_scaled))
-    (xp_stack,) = in_vmem(plain, [stack], xp)
-    (xp_scaled,) = in_vmem(scaled_kernel, [stack], weight, xp)
+    left, right = ((2, rows, pairs), jnp.bfloat16), ((2, pairs, 128), jnp.bfloat16)
+    square, half_square = ((rows, rows), jnp.float32), ((rows // 2, rows), jnp.float32)
+    routes = {"far": far_chip, "xp": other_x, "zn": next_chip}
+    blocks = [
+        sent(own, lambda z, x, c, slot=slot: routes[ORDERS[c][slot]](z, x, c)) for slot in range(3)
+    ]
+    far_left, xp_left, xp_right, zn_right = in_vmem(
+        functools.partial(ready_kernel, ORDERS), [left, left, right, right], weight, *blocks
+    )
+    (own_left,) = in_vmem(left_kernel, [left], own)
+    (own_right,) = in_vmem(right_kernel, [right], weight, own)
+    (own_own,) = in_vmem(own_kernel, [square], own_left, own_right)
     parts = ((3 * rows // 2, rows), jnp.float32)
-    mine, theirs = in_vmem(
-        meet_kernel, [parts] * 2, far_stack, xp_stack, xp_scaled, zn_scaled
-    )
-    square, half_square = ((rows, rows), jnp.float32), ((rows // 2, rows), jnp.float32)
+    mine, theirs = in_vmem(meet_kernel, [parts] * 2, far_left, xp_left, xp_right, zn_right)
     tile, half_tile = in_vmem(
         sum_kernel, [square, half_square], mine, sent(theirs, other_core)
     )
     tile = sent(tile, tile_chip)
     half_tile = sent(half_tile, half_tile_chip)
-    (own_stack,) = in_vmem(plain, [stack], own)
-    (own_scaled,) = in_vmem(scaled_kernel, [stack], weight, own)
     kept = ((5 * rows // 2, rows), jnp.float32)
     mine, theirs = in_vmem(
-        local_kernel, [kept] * 2, own_stack, own_scaled, xp_stack, zn_scaled
-    )
-    (far_own,) = in_vmem(far_kernel, [square], far_stack, own_scaled)
+        local_kernel, [kept] * 2, own_left, own_right, own_own, far_left, xp_left, zn_right
+    )
     (response,) = in_vmem(
-        finish_kernel,
-        [kept],
-        mine,
-        sent(theirs, other_core),
-        far_own,
-        sent(far_own, other_core),
-        tile,
-        half_tile,
+        finish_kernel, [kept], mine, sent(theirs, other_core), tile, half_tile
     )
     return response.T
 

time: 23.6 us -> 22.1 us (0.936)
  starting transfers between devices: 12.2 us -> 10.4 us
  local copies, waits for them, and re-layouts: 0.2 us -> 1.18 us
  other arithmetic: 0.76 us -> 0.08 us
    ppermute x8 -> x7, starting transfers between devices: 12.2 us -> 10.4 us  [sent(): return lax.ppermute(value, ('aux', 'pair'), pairs)]
    unnamed x2 -> x8, local copies, waits for them, and re-layouts: 0.01 us -> 0.98 us
    div x1, other arithmetic: 0.76 us -> 0.08 us  [pair_weights(): 4.0 * energy_gap / (energy_gap * energy_gap + frequency[0] * frequency[0])]
    pallas_call x11 -> x8, Pallas kernels: 2.31 us -> 2.47 us  [in_vmem(): pl.pallas_call(kernel, out_shape=[jax.ShapeDtypeStruct(*out) for out in o...]
    ppermute x8 -> x7, waiting for transfers between devices: 7.2 us -> 7.05 us  [sent(): return lax.ppermute(value, ('aux', 'pair'), pairs)]
  transfers between devices with their start and end apart: 8 -> 7, of which waited for: 2 -> 2; matrix products, arithmetic and copies ran while one was open for 4% -> 1% of each run, Pallas kernels for 4% -> 4%
where the time goes in v5:
time: 22.1 us; the launch traced here: 21.9 us
  starting transfers between devices  10.4 us (47%)
  waiting for transfers between devices  7.05 us (32%)
  Pallas kernels  2.47 us (11%)
  local copies, waits for them, and re-layouts  1.18 us (5%)
  between operations  0.8 us (4%)
    ppermute x7, starting transfers between devices, sent(): return lax.ppermute(value, ('aux', 'pair'), pairs)  10.4 us
    ppermute x7, waiting for transfers between devices, sent(): return lax.ppermute(value, ('aux', 'pair'), pairs)  7.05 us
    pallas_call x8, Pallas kernels, in_vmem(): pl.pallas_call(kernel, out_shape=[jax.ShapeDtypeStruct(*out) for out in o...  2.47 us
    unnamed x8, local copies, waits for them, and re-layouts  0.98 us
  transfers between devices with their start and end apart: 7, of which 2 were waited for; matrix products, arithmetic and copies ran while one was open for 1% of the time, Pallas kernels for 4%

profile of v5, /device:TPU:0, one launch (start us, length us, event | category | flops | bytes accessed | tf_op | source)
XLA Modules:
  0.0 21.9 jit_solution(4180330701687543178)
XLA Ops:
  0.0 2.9 %collective-permute-start = (f32[400,126]{1,0:T(8,128)}, f32[400,126]{1,0:T(8,128)S(1)}, u32[]{:S(2)}, u32[]{:S(2)}) collective-permute-start(f32[400,126]{1,0:T(8,128)} %bitcast.3), channel_id=1, source_target_pairs={{0,2},{1,9},{2,0},{3,11},{4,6},{5,13},{6,4},{7,15},{8,10},{9,1},{1... | collective-permute-start | bytes 604808 | tf_op jit(solution)/shard_map/ppermute | solution.py:75
  2.9 1.5 %collective-permute-start.1 = (f32[400,126]{1,0:T(8,128)}, f32[400,126]{1,0:T(8,128)S(1)}, u32[]{:S(2)}, u32[]{:S(2)}) collective-permute-start(f32[400,126]{1,0:T(8,128)} %bitcast.4), channel_id=1, source_target_pairs={{0,6},{1,7},{2,4},{3,5},{4,0},{5,1},{6,2},{7,3},{8,14},{9,15},{10,... | collective-permute-start | bytes 604808 | tf_op jit(solution)/shard_map/ppermute | solution.py:75
  4.5 2.6 %collective-permute-start.2 = (f32[400,126]{1,0:T(8,128)}, f32[400,126]{1,0:T(8,128)S(1)}, u32[]{:S(2)}, u32[]{:S(2)}) collective-permute-start(f32[400,126]{1,0:T(8,128)} %bitcast.5), channel_id=1, source_target_pairs={{0,8},{1,3},{2,10},{3,1},{4,12},{5,7},{6,14},{7,5},{8,0},{9,11},{1... | collective-permute-start | bytes 604808 | tf_op jit(solution)/shard_map/ppermute | solution.py:75
  7.1 0.0 copy-start
  7.1 1.0 %copy-done = f32[126,400]{0,1:T(8,128)S(1)} copy-done((f32[126,400]{0,1:T(8,128)S(1)}, f32[126,400]{0,1:T(8,128)}, u32[]{:S(2)}) %copy-start) | copy-done | bytes 201624
  8.0 0.0 copy-start.2
  8.0 0.0 copy-start.3
  8.0 0.1 shard_map.46.own
  8.2 0.0 copy-start.1
  8.9 0.0 copy-done.2
  8.9 0.0 copy-done.3
  8.9 0.1 fusion
  9.0 0.1 div.11
  9.1 0.1 broadcast_in_dim.2.weight
  9.2 0.0 copy-done.1
  9.2 0.1 shard_map.47.own_scaled
  9.3 0.0 collective-permute-done.refs_0_
  9.3 4.7 %collective-permute-done.1.refs_1_ = f32[400,126]{1,0:T(8,128)S(1)} collective-permute-done((f32[400,126]{1,0:T(8,128)}, f32[400,126]{1,0:T(8,128)S(1)}, u32[]{:S(2)}, u32[]{:S(2)}) %collective-permute-start.1) | collective-permute-done | bytes 201632 | tf_op jit(solution)/shard_map/ppermute | solution.py:75
  14.0 0.0 collective-permute-done.2.refs_2_
  14.0 0.3 %shard_map.49 = (bf16[2,126,400]{2,1,0:T(8,128)(2,1)S(1)}, bf16[2,126,400]{2,1,0:T(8,128)(2,1)S(1)}, bf16[2,400,128]{2,1,0:T(8,128)(2,1)S(1)}, bf16[2,400,128]{2,1,0:T(8,128)(2,1)S(1)}) custom-call(f32[400,126]{1,0:T(8,128)S(1)} %broadcast_in_dim.2.weight, f32[400,126]{1,0:T(8,128)S(1)} %collective-permute-done.refs_0_, ...), custom_call_target="tpu_custom_call" | custom-call | flops 1000 | bytes 1000 | tf_op jit(solution)/shard_map/pallas_call | solution.py:259
  14.3 0.5 %shard_map.51 = (f32[189,126]{1,0:T(8,128)S(1)}, f32[189,126]{1,0:T(8,128)S(1)}) custom-call(bf16[2,126,400]{2,1,0:T(8,128)(2,1)S(1)} %get-tuple-element.15.far, bf16[2,126,400]{2,1,0:T(8,128)(2,1)S(1)} %get-tuple-element.16.xp, bf16[2,400,128]{2,1,0:T(8,128)(2,1)S(1)} %get-tuple-element.20.xp_scaled, bf16[2,400,128]{2,1,0:T(8,128)(2,1)S(1)} %get-tuple-element.17.zn_scaled), custom_call_target="tpu_custom_call" | custom-call | flops 1000 | bytes 1000 | tf_op jit(solution)/shard_map/pallas_call | solution.py:259
  14.8 0.1 collective-permute-start.4
  14.9 0.3 %shard_map.48.own_own = f32[126,126]{1,0:T(8,128)S(1)} custom-call(bf16[2,126,400]{2,1,0:T(8,128)(2,1)S(1)} %shard_map.46.own, bf16[2,400,128]{2,1,0:T(8,128)(2,1)S(1)} %shard_map.47.own_scaled), custom_call_target="tpu_custom_call" | custom-call | flops 1000 | bytes 1000 | tf_op jit(solution)/shard_map/pallas_call | solution.py:259
  15.1 0.5 %shard_map.50 = (f32[315,126]{1,0:T(8,128)S(1)}, f32[315,126]{1,0:T(8,128)S(1)}) custom-call(bf16[2,126,400]{2,1,0:T(8,128)(2,1)S(1)} %shard_map.46.own, bf16[2,400,128]{2,1,0:T(8,128)(2,1)S(1)} %shard_map.47.own_scaled, f32[126,126]{1,0:T(8,128)S(1)} %shard_map.48.own_own, bf16[2,126,400]{2,1,0:T(8,128)(2,1)S(1)} %get-tuple-element.15.far, ...), custom_call_target="tpu_custom_call" | custom-call | flops 1000 | bytes 1000 | tf_op jit(solution)/shard_map/pallas_call | solution.py:259
  15.7 0.6 %collective-permute-start.3 = (f32[315,126]{1,0:T(8,128)S(1)}, f32[315,126]{1,0:T(8,128)S(1)}, u32[]{:S(2)}, u32[]{:S(2)}) collective-permute-start(f32[315,126]{1,0:T(8,128)S(1)} %get-tuple-element.19), channel_id=1, source_target_pairs={{0,1},{1,0},{2,3},{3,2},{4,5},{5,4},{6,7},{7,6},{8,9},{9,8},{10,11... | collective-permute-start | bytes 476288 | tf_op jit(solution)/shard_map/ppermute | solution.py:75
  16.3 0.0 collective-permute-done.4.theirs
  16.3 1.0 %collective-permute-start.5 = (f32[126,126]{1,0:T(8,128)S(1)}, f32[126,126]{1,0:T(8,128)S(1)}, u32[]{:S(2)}, u32[]{:S(2)}) collective-permute-start(f32[126,126]{1,0:T(8,128)S(1)} %get-tuple-element.23), channel_id=1, source_target_pairs={{0,2},{1,3},{2,0},{3,1},{4,7},{5,13},{6,14},{7,4},{8,10},{9,11},{1... | collective-permute-start | bytes 190520 | tf_op jit(solution)/shard_map/ppermute | solution.py:75
  17.3 1.6 %collective-permute-start.6 = (f32[63,126]{1,0:T(8,128)S(1)}, f32[63,126]{1,0:T(8,128)S(1)}, u32[]{:S(2)}, u32[]{:S(2)}) collective-permute-start(f32[63,126]{1,0:T(8,128)S(1)} %get-tuple-element.24), channel_id=1, source_target_pairs={{0,4},{1,5},{2,6},{3,7},{4,0},{5,1},{6,2},{7,3},{8,12},{9,13},{10,... | collective-permute-start | bytes 95264 | tf_op jit(solution)/shard_map/ppermute | solution.py:75
  18.9 2.3 %collective-permute-done.6.half_tile = f32[63,126]{1,0:T(8,128)S(1)} collective-permute-done((f32[63,126]{1,0:T(8,128)S(1)}, f32[63,126]{1,0:T(8,128)S(1)}, u32[]{:S(2)}, u32[]{:S(2)}) %collective-permute-start.6) | collective-permute-done | bytes 31784 | tf_op jit(solution)/shard_map/ppermute | solution.py:75
  21.2 0.0 collective-permute-done.3.theirs
  21.2 0.0 collective-permute-done.5.tile
  21.2 0.7 %shard_map.53 = f32[315,126]{1,0:T(8,128)} custom-call(f32[315,126]{1,0:T(8,128)S(1)} %get-tuple-element.18.mine, f32[315,126]{1,0:T(8,128)S(1)} %collective-permute-done.3.theirs, f32[126,126]{1,0:T(8,128)S(1)} %collective-permute-done.5.tile, f32[63,126]{1,0:T(8,128)S(1)} %collective-permute-done.6.half_tile), custom_call_target="tpu_custom_call" | custom-call | flops 1000 | bytes 1000 | tf_op jit(solution)/shard_map/pallas_call | solution.py:259
  (1 shorter events, 0.0 us)
Async XLA Ops:
  0.0 9.3 %collective-permute-start = (f32[400,126]{1,0:T(8,128)}, f32[400,126]{1,0:T(8,128)S(1)}, u32[]{:S(2)}, u32[]{:S(2)}) collective-permute-start(f32[400,126]{1,0:T(8,128)} %bitcast.3), channel_id=1, source_target_pairs={{0,2},{1,9},{2,0},{3,11},{4,6},{5,13},{6,4},{7,15},{8,10},{9,1},{1... | collective-permute-start | bytes 604808 | tf_op jit(solution)/shard_map/ppermute | solution.py:75
  2.9 11.1 %collective-permute-start.1 = (f32[400,126]{1,0:T(8,128)}, f32[400,126]{1,0:T(8,128)S(1)}, u32[]{:S(2)}, u32[]{:S(2)}) collective-permute-start(f32[400,126]{1,0:T(8,128)} %bitcast.4), channel_id=1, source_target_pairs={{0,6},{1,7},{2,4},{3,5},{4,0},{5,1},{6,2},{7,3},{8,14},{9,15},{10,... | collective-permute-start | bytes 604808 | tf_op jit(solution)/shard_map/ppermute | solution.py:75
  4.5 9.5 %collective-permute-start.2 = (f32[400,126]{1,0:T(8,128)}, f32[400,126]{1,0:T(8,128)S(1)}, u32[]{:S(2)}, u32[]{:S(2)}) collective-permute-start(f32[400,126]{1,0:T(8,128)} %bitcast.5), channel_id=1, source_target_pairs={{0,8},{1,3},{2,10},{3,1},{4,12},{5,7},{6,14},{7,5},{8,0},{9,11},{1... | collective-permute-start | bytes 604808 | tf_op jit(solution)/shard_map/ppermute | solution.py:75
  7.1 1.0 %copy-start = (f32[126,400]{0,1:T(8,128)S(1)}, f32[126,400]{0,1:T(8,128)}, u32[]{:S(2)}) copy-start(f32[126,400]{0,1:T(8,128)} %param.4) | copy-start | bytes 604804
  8.0 0.8 %copy-start.2 = (f32[200]{0:T(256)S(1)}, f32[200]{0:T(256)}, u32[]{:S(2)}) copy-start(f32[200]{0:T(256)} %param.6) | copy-start | bytes 2404
  8.0 0.9 %copy-start.3 = (f32[2]{0:T(128)S(1)}, f32[2]{0:T(128)}, u32[]{:S(2)}) copy-start(f32[2]{0:T(128)} %param.5) | copy-start | bytes 28
  8.2 1.0 %copy-start.1 = (f32[126,400]{0,1:T(8,128)S(1)}, f32[126,400]{0,1:T(8,128)}, u32[]{:S(2)}) copy-start(f32[126,400]{0,1:T(8,128)} %param.4) | copy-start | bytes 604804
  14.8 1.5 %collective-permute-start.4 = (f32[189,126]{1,0:T(8,128)S(1)}, f32[189,126]{1,0:T(8,128)S(1)}, u32[]{:S(2)}, u32[]{:S(2)}) collective-permute-start(f32[189,126]{1,0:T(8,128)S(1)} %get-tuple-element.22), channel_id=1, source_target_pairs={{0,1},{1,0},{2,3},{3,2},{4,5},{5,4},{6,7},{7,6},{8,9},{9,8},{10,11... | collective-permute-start | bytes 285776 | tf_op jit(solution)/shard_map/ppermute | solution.py:75
  15.7 5.5 %collective-permute-start.3 = (f32[315,126]{1,0:T(8,128)S(1)}, f32[315,126]{1,0:T(8,128)S(1)}, u32[]{:S(2)}, u32[]{:S(2)}) collective-permute-start(f32[315,126]{1,0:T(8,128)S(1)} %get-tuple-element.19), channel_id=1, source_target_pairs={{0,1},{1,0},{2,3},{3,2},{4,5},{5,4},{6,7},{7,6},{8,9},{9,8},{10,11... | collective-permute-start | bytes 476288 | tf_op jit(solution)/shard_map/ppermute | solution.py:75
  16.3 4.9 %collective-permute-start.5 = (f32[126,126]{1,0:T(8,128)S(1)}, f32[126,126]{1,0:T(8,128)S(1)}, u32[]{:S(2)}, u32[]{:S(2)}) collective-permute-start(f32[126,126]{1,0:T(8,128)S(1)} %get-tuple-element.23), channel_id=1, source_target_pairs={{0,2},{1,3},{2,0},{3,1},{4,7},{5,13},{6,14},{7,4},{8,10},{9,11},{1... | collective-permute-start | bytes 190520 | tf_op jit(solution)/shard_map/ppermute | solution.py:75
  17.3 3.9 %collective-permute-start.6 = (f32[63,126]{1,0:T(8,128)S(1)}, f32[63,126]{1,0:T(8,128)S(1)}, u32[]{:S(2)}, u32[]{:S(2)}) collective-permute-start(f32[63,126]{1,0:T(8,128)S(1)} %get-tuple-element.24), channel_id=1, source_target_pairs={{0,4},{1,5},{2,6},{3,7},{4,0},{5,1},{6,2},{7,3},{8,12},{9,13},{10,... | collective-permute-start | bytes 95264 | tf_op jit(solution)/shard_map/ppermute | solution.py:75

commit v6 on v5

--- a/solution.py
+++ b/solution.py
@@ -95,9 +95,7 @@
 
 
 def tile_chip(z, x, c):
-    if z % 2 == 0:
-        return (z, 1 - x, c)
-    return (z ^ 2, x, c) if x != c else (z, 1 - x, 1 - c)
+    return (z ^ 2, x, c) if z % 2 and x != c else (z, 1 - x, 1 - c)
 
 
 def half_tile_chip(z, x, c):
@@ -168,15 +166,15 @@
     @pl.when(even)
     def _():
         zn_xp = xp_zn.T
-        put(0, 0, zn_xp)
+        put(1, 0, zn_xp)
 
         @pl.when(x == 0)
         def _():
-            put(1, 0, far_xp)
+            put(0, 0, far_xp)
 
         @pl.when(x == 1)
         def _():
-            put(1, 0, zn_xp)
+            put(0, 0, zn_xp)
 
     @pl.when(~even)
     def _():

time: 22.1 us -> 22.1 us (level)
  the two profiles are of different devices: /device:TPU:0 before, /device:TPU:10 now
where the time goes in v6:
time: 22.1 us; the launch traced here: 21.9 us
  waiting for transfers between devices  10.5 us (48%)
  starting transfers between devices  6.9 us (31%)
  Pallas kernels  2.46 us (11%)
  local copies, waits for them, and re-layouts  1.18 us (5%)
  between operations  0.78 us (4%)
    ppermute x7, waiting for transfers between devices, sent(): return lax.ppermute(value, ('aux', 'pair'), pairs)  10.5 us
    ppermute x7, starting transfers between devices, sent(): return lax.ppermute(value, ('aux', 'pair'), pairs)  6.9 us
    pallas_call x8, Pallas kernels, in_vmem(): pl.pallas_call(kernel, out_shape=[jax.ShapeDtypeStruct(*out) for out in o...  2.46 us
    unnamed x8, local copies, waits for them, and re-layouts  0.98 us
  transfers between devices with their start and end apart: 7, of which 3 were waited for; matrix products, arithmetic and copies ran while one was open for 1% of the time, Pallas kernels for 4%

profile of v6, /device:TPU:10, one launch (start us, length us, event | category | flops | bytes accessed | tf_op | source)
XLA Modules:
  0.0 21.9 jit_solution(8735335567894157861)
XLA Ops:
  0.0 0.5 %collective-permute-start = (f32[400,126]{1,0:T(8,128)}, f32[400,126]{1,0:T(8,128)S(1)}, u32[]{:S(2)}, u32[]{:S(2)}) collective-permute-start(f32[400,126]{1,0:T(8,128)} %bitcast.3), channel_id=1, source_target_pairs={{0,2},{1,9},{2,0},{3,11},{4,6},{5,13},{6,4},{7,15},{8,10},{9,1},{1... | collective-permute-start | bytes 604808 | tf_op jit(solution)/shard_map/ppermute | solution.py:75
  0.5 0.0 collective-permute-start.1
  0.5 3.0 %collective-permute-start.2 = (f32[400,126]{1,0:T(8,128)}, f32[400,126]{1,0:T(8,128)S(1)}, u32[]{:S(2)}, u32[]{:S(2)}) collective-permute-start(f32[400,126]{1,0:T(8,128)} %bitcast.5), channel_id=1, source_target_pairs={{0,8},{1,3},{2,10},{3,1},{4,12},{5,7},{6,14},{7,5},{8,0},{9,11},{1... | collective-permute-start | bytes 604808 | tf_op jit(solution)/shard_map/ppermute | solution.py:75
  3.6 0.0 copy-start
  3.6 1.0 %copy-done = f32[126,400]{0,1:T(8,128)S(1)} copy-done((f32[126,400]{0,1:T(8,128)S(1)}, f32[126,400]{0,1:T(8,128)}, u32[]{:S(2)}) %copy-start) | copy-done | bytes 201624
  4.5 0.0 copy-start.2
  4.5 0.0 copy-start.3
  4.5 0.1 shard_map.46.own
  4.7 0.0 copy-start.1
  5.4 0.0 copy-done.2
  5.4 0.0 copy-done.3
  5.4 0.1 fusion
  5.5 0.1 div.11
  5.6 0.1 broadcast_in_dim.2.weight
  5.7 0.0 copy-done.1
  5.7 0.1 shard_map.47.own_scaled
  5.8 5.4 %collective-permute-done.refs_0_ = f32[400,126]{1,0:T(8,128)S(1)} collective-permute-done((f32[400,126]{1,0:T(8,128)}, f32[400,126]{1,0:T(8,128)S(1)}, u32[]{:S(2)}, u32[]{:S(2)}) %collective-permute-start) | collective-permute-done | bytes 201632 | tf_op jit(solution)/shard_map/ppermute | solution.py:75
  11.2 0.0 collective-permute-done.1.refs_1_
  11.2 1.2 %collective-permute-done.2.refs_2_ = f32[400,126]{1,0:T(8,128)S(1)} collective-permute-done((f32[400,126]{1,0:T(8,128)}, f32[400,126]{1,0:T(8,128)S(1)}, u32[]{:S(2)}, u32[]{:S(2)}) %collective-permute-start.2) | collective-permute-done | bytes 201632 | tf_op jit(solution)/shard_map/ppermute | solution.py:75
  12.4 0.3 %shard_map.49 = (bf16[2,126,400]{2,1,0:T(8,128)(2,1)S(1)}, bf16[2,126,400]{2,1,0:T(8,128)(2,1)S(1)}, bf16[2,400,128]{2,1,0:T(8,128)(2,1)S(1)}, bf16[2,400,128]{2,1,0:T(8,128)(2,1)S(1)}) custom-call(f32[400,126]{1,0:T(8,128)S(1)} %broadcast_in_dim.2.weight, f32[400,126]{1,0:T(8,128)S(1)} %collective-permute-done.refs_0_, ...), custom_call_target="tpu_custom_call" | custom-call | flops 1000 | bytes 1000 | tf_op jit(solution)/shard_map/pallas_call | solution.py:257
  12.7 0.5 %shard_map.51 = (f32[189,126]{1,0:T(8,128)S(1)}, f32[189,126]{1,0:T(8,128)S(1)}) custom-call(bf16[2,126,400]{2,1,0:T(8,128)(2,1)S(1)} %get-tuple-element.15.far, bf16[2,126,400]{2,1,0:T(8,128)(2,1)S(1)} %get-tuple-element.16.xp, bf16[2,400,128]{2,1,0:T(8,128)(2,1)S(1)} %get-tuple-element.20.xp_scaled, bf16[2,400,128]{2,1,0:T(8,128)(2,1)S(1)} %get-tuple-element.17.zn_scaled), custom_call_target="tpu_custom_call" | custom-call | flops 1000 | bytes 1000 | tf_op jit(solution)/shard_map/pallas_call | solution.py:257
  13.2 0.2 collective-permute-start.4
  13.3 0.3 %shard_map.48.own_own = f32[126,126]{1,0:T(8,128)S(1)} custom-call(bf16[2,126,400]{2,1,0:T(8,128)(2,1)S(1)} %shard_map.46.own, bf16[2,400,128]{2,1,0:T(8,128)(2,1)S(1)} %shard_map.47.own_scaled), custom_call_target="tpu_custom_call" | custom-call | flops 1000 | bytes 1000 | tf_op jit(solution)/shard_map/pallas_call | solution.py:257
  13.6 0.5 %shard_map.50 = (f32[315,126]{1,0:T(8,128)S(1)}, f32[315,126]{1,0:T(8,128)S(1)}) custom-call(bf16[2,126,400]{2,1,0:T(8,128)(2,1)S(1)} %shard_map.46.own, bf16[2,400,128]{2,1,0:T(8,128)(2,1)S(1)} %shard_map.47.own_scaled, f32[126,126]{1,0:T(8,128)S(1)} %shard_map.48.own_own, bf16[2,126,400]{2,1,0:T(8,128)(2,1)S(1)} %get-tuple-element.15.far, ...), custom_call_target="tpu_custom_call" | custom-call | flops 1000 | bytes 1000 | tf_op jit(solution)/shard_map/pallas_call | solution.py:257
  14.1 0.5 %collective-permute-start.3 = (f32[315,126]{1,0:T(8,128)S(1)}, f32[315,126]{1,0:T(8,128)S(1)}, u32[]{:S(2)}, u32[]{:S(2)}) collective-permute-start(f32[315,126]{1,0:T(8,128)S(1)} %get-tuple-element.19), channel_id=1, source_target_pairs={{0,1},{1,0},{2,3},{3,2},{4,5},{5,4},{6,7},{7,6},{8,9},{9,8},{10,11... | collective-permute-start | bytes 476288 | tf_op jit(solution)/shard_map/ppermute | solution.py:75
  14.6 0.0 collective-permute-done.4.theirs
  14.6 2.7 %collective-permute-start.5 = (f32[126,126]{1,0:T(8,128)S(1)}, f32[126,126]{1,0:T(8,128)S(1)}, u32[]{:S(2)}, u32[]{:S(2)}) collective-permute-start(f32[126,126]{1,0:T(8,128)S(1)} %get-tuple-element.23), channel_id=1, source_target_pairs={{0,3},{1,2},{2,1},{3,0},{4,7},{5,13},{6,14},{7,4},{8,11},{9,10},{1... | collective-permute-start | bytes 190520 | tf_op jit(solution)/shard_map/ppermute | solution.py:75
  17.3 0.0 collective-permute-start.6
  17.3 3.9 %collective-permute-done.6.half_tile = f32[63,126]{1,0:T(8,128)S(1)} collective-permute-done((f32[63,126]{1,0:T(8,128)S(1)}, f32[63,126]{1,0:T(8,128)S(1)}, u32[]{:S(2)}, u32[]{:S(2)}) %collective-permute-start.6) | collective-permute-done | bytes 31784 | tf_op jit(solution)/shard_map/ppermute | solution.py:75
  21.2 0.0 collective-permute-done.3.theirs
  21.2 0.0 collective-permute-done.5.tile
  21.2 0.7 %shard_map.53 = f32[315,126]{1,0:T(8,128)} custom-call(f32[315,126]{1,0:T(8,128)S(1)} %get-tuple-element.18.mine, f32[315,126]{1,0:T(8,128)S(1)} %collective-permute-done.3.theirs, f32[126,126]{1,0:T(8,128)S(1)} %collective-permute-done.5.tile, f32[63,126]{1,0:T(8,128)S(1)} %collective-permute-done.6.half_tile), custom_call_target="tpu_custom_call" | custom-call | flops 1000 | bytes 1000 | tf_op jit(solution)/shard_map/pallas_call | solution.py:257
  (1 shorter events, 0.0 us)
Async XLA Ops:
  0.0 11.2 %collective-permute-start = (f32[400,126]{1,0:T(8,128)}, f32[400,126]{1,0:T(8,128)S(1)}, u32[]{:S(2)}, u32[]{:S(2)}) collective-permute-start(f32[400,126]{1,0:T(8,128)} %bitcast.3), channel_id=1, source_target_pairs={{0,2},{1,9},{2,0},{3,11},{4,6},{5,13},{6,4},{7,15},{8,10},{9,1},{1... | collective-permute-start | bytes 604808 | tf_op jit(solution)/shard_map/ppermute | solution.py:75
  0.5 10.6 %collective-permute-start.1 = (f32[400,126]{1,0:T(8,128)}, f32[400,126]{1,0:T(8,128)S(1)}, u32[]{:S(2)}, u32[]{:S(2)}) collective-permute-start(f32[400,126]{1,0:T(8,128)} %bitcast.4), channel_id=1, source_target_pairs={{0,6},{1,7},{2,4},{3,5},{4,0},{5,1},{6,2},{7,3},{8,14},{9,15},{10,... | collective-permute-start | bytes 604808 | tf_op jit(solution)/shard_map/ppermute | solution.py:75
  0.5 11.8 %collective-permute-start.2 = (f32[400,126]{1,0:T(8,128)}, f32[400,126]{1,0:T(8,128)S(1)}, u32[]{:S(2)}, u32[]{:S(2)}) collective-permute-start(f32[400,126]{1,0:T(8,128)} %bitcast.5), channel_id=1, source_target_pairs={{0,8},{1,3},{2,10},{3,1},{4,12},{5,7},{6,14},{7,5},{8,0},{9,11},{1... | collective-permute-start | bytes 604808 | tf_op jit(solution)/shard_map/ppermute | solution.py:75
  3.6 1.0 %copy-start = (f32[126,400]{0,1:T(8,128)S(1)}, f32[126,400]{0,1:T(8,128)}, u32[]{:S(2)}) copy-start(f32[126,400]{0,1:T(8,128)} %param.4) | copy-start | bytes 604804
  4.5 0.8 %copy-start.2 = (f32[200]{0:T(256)S(1)}, f32[200]{0:T(256)}, u32[]{:S(2)}) copy-start(f32[200]{0:T(256)} %param.6) | copy-start | bytes 2404
  4.5 0.9 %copy-start.3 = (f32[2]{0:T(128)S(1)}, f32[2]{0:T(128)}, u32[]{:S(2)}) copy-start(f32[2]{0:T(128)} %param.5) | copy-start | bytes 28
  4.7 1.0 %copy-start.1 = (f32[126,400]{0,1:T(8,128)S(1)}, f32[126,400]{0,1:T(8,128)}, u32[]{:S(2)}) copy-start(f32[126,400]{0,1:T(8,128)} %param.4) | copy-start | bytes 604804
  13.2 1.5 %collective-permute-start.4 = (f32[189,126]{1,0:T(8,128)S(1)}, f32[189,126]{1,0:T(8,128)S(1)}, u32[]{:S(2)}, u32[]{:S(2)}) collective-permute-start(f32[189,126]{1,0:T(8,128)S(1)} %get-tuple-element.22), channel_id=1, source_target_pairs={{0,1},{1,0},{2,3},{3,2},{4,5},{5,4},{6,7},{7,6},{8,9},{9,8},{10,11... | collective-permute-start | bytes 285776 | tf_op jit(solution)/shard_map/ppermute | solution.py:75
  14.1 7.1 %collective-permute-start.3 = (f32[315,126]{1,0:T(8,128)S(1)}, f32[315,126]{1,0:T(8,128)S(1)}, u32[]{:S(2)}, u32[]{:S(2)}) collective-permute-start(f32[315,126]{1,0:T(8,128)S(1)} %get-tuple-element.19), channel_id=1, source_target_pairs={{0,1},{1,0},{2,3},{3,2},{4,5},{5,4},{6,7},{7,6},{8,9},{9,8},{10,11... | collective-permute-start | bytes 476288 | tf_op jit(solution)/shard_map/ppermute | solution.py:75
  14.6 6.6 %collective-permute-start.5 = (f32[126,126]{1,0:T(8,128)S(1)}, f32[126,126]{1,0:T(8,128)S(1)}, u32[]{:S(2)}, u32[]{:S(2)}) collective-permute-start(f32[126,126]{1,0:T(8,128)S(1)} %get-tuple-element.23), channel_id=1, source_target_pairs={{0,3},{1,2},{2,1},{3,0},{4,7},{5,13},{6,14},{7,4},{8,11},{9,10},{1... | collective-permute-start | bytes 190520 | tf_op jit(solution)/shard_map/ppermute | solution.py:75
  17.3 3.9 %collective-permute-start.6 = (f32[63,126]{1,0:T(8,128)S(1)}, f32[63,126]{1,0:T(8,128)S(1)}, u32[]{:S(2)}, u32[]{:S(2)}) collective-permute-start(f32[63,126]{1,0:T(8,128)S(1)} %get-tuple-element.24), channel_id=1, source_target_pairs={{0,4},{1,5},{2,6},{3,7},{4,0},{5,1},{6,2},{7,3},{8,12},{9,13},{10,... | collective-permute-start | bytes 95264 | tf_op jit(solution)/shard_map/ppermute | solution.py:75

commit v7 on v6

--- a/solution.py
+++ b/solution.py
@@ -131,15 +131,23 @@
 
 def ready_kernel(orders, weight, *refs):
     blocks, (far_left, xp_left, xp_right, zn_right) = refs[:3], refs[3:]
-    _, _, c = place()
+    even, x, c = place()
     for core, order in enumerate(orders):
 
         @pl.when(c == core)
         def _():
             left_kernel(blocks[order.index("far")], far_left)
-            left_kernel(blocks[order.index("xp")], xp_left)
-            right_kernel(weight, blocks[order.index("xp")], xp_right)
             right_kernel(weight, blocks[order.index("zn")], zn_right)
+
+            @pl.when(even | (x == 0))
+            def _():
+                left_kernel(blocks[order.index("xp")], xp_left)
+                right_kernel(weight, blocks[order.index("xp")], xp_right)
+
+            @pl.when(~even & (x == 1))
+            def _():
+                xp_left[...] = jnp.zeros_like(xp_left)
+                xp_right[...] = jnp.zeros_like(xp_right)
 
 
 def meet_kernel(far, xp, xp_scaled, zn_scaled, mine, theirs):
@@ -149,7 +157,6 @@
     scaled = [jnp.concatenate([zn_scaled[i], xp_scaled[i]], 1) for i in range(2)]
     by_far = product(far, scaled)
     far_zn, far_xp = by_far[:, :rows], by_far[:, 128 : 128 + rows]
-    xp_zn = product(xp, zn_scaled)[:, :rows]
 
     def put(core, row, values):
         @pl.when(c == core)
@@ -165,7 +172,7 @@
 
     @pl.when(even)
     def _():
-        zn_xp = xp_zn.T
+        zn_xp = product(xp, zn_scaled)[:, :rows].T
         put(1, 0, zn_xp)
 
         @pl.when(x == 0)

time: 22.1 us -> 21.9 us (level)
  the two profiles are of different devices: /device:TPU:10 before, /device:TPU:0 now
where the time goes in v7:
time: 21.9 us; the launch traced here: 21.8 us
  starting transfers between devices  10 us (46%)
  waiting for transfers between devices  7.09 us (32%)
  Pallas kernels  2.6 us (12%)
  local copies, waits for them, and re-layouts  1.18 us (5%)
  between operations  0.8 us (4%)
    ppermute x7, starting transfers between devices, sent(): return lax.ppermute(value, ('aux', 'pair'), pairs)  10 us
    ppermute x7, waiting for transfers between devices, sent(): return lax.ppermute(value, ('aux', 'pair'), pairs)  7.09 us
    pallas_call x8, Pallas kernels, in_vmem(): pl.pallas_call(kernel, out_shape=[jax.ShapeDtypeStruct(*out) for out in o...  2.6 us
    unnamed x8, local copies, waits for them, and re-layouts  0.98 us
  transfers between devices with their start and end apart: 7, of which 2 were waited for; matrix products, arithmetic and copies ran while one was open for 1% of the time, Pallas kernels for 4%

profile of v7, /device:TPU:0, one launch (start us, length us, event | category | flops | bytes accessed | tf_op | source)
XLA Modules:
  0.0 21.8 jit_solution(240650639582169005)
XLA Ops:
  0.0 2.9 %collective-permute-start = (f32[400,126]{1,0:T(8,128)}, f32[400,126]{1,0:T(8,128)S(1)}, u32[]{:S(2)}, u32[]{:S(2)}) collective-permute-start(f32[400,126]{1,0:T(8,128)} %bitcast.3), channel_id=1, source_target_pairs={{0,2},{1,9},{2,0},{3,11},{4,6},{5,13},{6,4},{7,15},{8,10},{9,1},{1... | collective-permute-start | bytes 604808 | tf_op jit(solution)/shard_map/ppermute | solution.py:75
  2.9 1.5 %collective-permute-start.1 = (f32[400,126]{1,0:T(8,128)}, f32[400,126]{1,0:T(8,128)S(1)}, u32[]{:S(2)}, u32[]{:S(2)}) collective-permute-start(f32[400,126]{1,0:T(8,128)} %bitcast.4), channel_id=1, source_target_pairs={{0,6},{1,7},{2,4},{3,5},{4,0},{5,1},{6,2},{7,3},{8,14},{9,15},{10,... | collective-permute-start | bytes 604808 | tf_op jit(solution)/shard_map/ppermute | solution.py:75
  4.5 2.6 %collective-permute-start.2 = (f32[400,126]{1,0:T(8,128)}, f32[400,126]{1,0:T(8,128)S(1)}, u32[]{:S(2)}, u32[]{:S(2)}) collective-permute-start(f32[400,126]{1,0:T(8,128)} %bitcast.5), channel_id=1, source_target_pairs={{0,8},{1,3},{2,10},{3,1},{4,12},{5,7},{6,14},{7,5},{8,0},{9,11},{1... | collective-permute-start | bytes 604808 | tf_op jit(solution)/shard_map/ppermute | solution.py:75
  7.1 0.0 copy-start
  7.1 1.0 %copy-done = f32[126,400]{0,1:T(8,128)S(1)} copy-done((f32[126,400]{0,1:T(8,128)S(1)}, f32[126,400]{0,1:T(8,128)}, u32[]{:S(2)}) %copy-start) | copy-done | bytes 201624
  8.0 0.0 copy-start.2
  8.0 0.0 copy-start.3
  8.0 0.1 shard_map.46.own
  8.2 0.0 copy-start.1
  8.9 0.0 copy-done.2
  8.9 0.0 copy-done.3
  8.9 0.1 fusion
  9.0 0.1 div.11
  9.1 0.1 broadcast_in_dim.2.weight
  9.2 0.0 copy-done.1
  9.2 0.1 shard_map.47.own_scaled
  9.3 0.0 collective-permute-done.refs_0_
  9.3 4.7 %collective-permute-done.1.refs_1_ = f32[400,126]{1,0:T(8,128)S(1)} collective-permute-done((f32[400,126]{1,0:T(8,128)}, f32[400,126]{1,0:T(8,128)S(1)}, u32[]{:S(2)}, u32[]{:S(2)}) %collective-permute-start.1) | collective-permute-done | bytes 201632 | tf_op jit(solution)/shard_map/ppermute | solution.py:75
  14.0 0.0 collective-permute-done.2.refs_2_
  14.0 0.3 %shard_map.49 = (bf16[2,126,400]{2,1,0:T(8,128)(2,1)S(1)}, bf16[2,126,400]{2,1,0:T(8,128)(2,1)S(1)}, bf16[2,400,128]{2,1,0:T(8,128)(2,1)S(1)}, bf16[2,400,128]{2,1,0:T(8,128)(2,1)S(1)}) custom-call(f32[400,126]{1,0:T(8,128)S(1)} %broadcast_in_dim.2.weight, f32[400,126]{1,0:T(8,128)S(1)} %collective-permute-done.refs_0_, ...), custom_call_target="tpu_custom_call" | custom-call | flops 1000 | bytes 1000 | tf_op jit(solution)/shard_map/pallas_call | solution.py:264
  14.3 0.6 %shard_map.51 = (f32[189,126]{1,0:T(8,128)S(1)}, f32[189,126]{1,0:T(8,128)S(1)}) custom-call(bf16[2,126,400]{2,1,0:T(8,128)(2,1)S(1)} %get-tuple-element.15.far, bf16[2,126,400]{2,1,0:T(8,128)(2,1)S(1)} %get-tuple-element.16.xp, bf16[2,400,128]{2,1,0:T(8,128)(2,1)S(1)} %get-tuple-element.20.xp_scaled, bf16[2,400,128]{2,1,0:T(8,128)(2,1)S(1)} %get-tuple-element.17.zn_scaled), custom_call_target="tpu_custom_call" | custom-call | flops 1000 | bytes 1000 | tf_op jit(solution)/shard_map/pallas_call | solution.py:264
  15.0 0.1 collective-permute-start.4
  15.0 0.2 %shard_map.48.own_own = f32[126,126]{1,0:T(8,128)S(1)} custom-call(bf16[2,126,400]{2,1,0:T(8,128)(2,1)S(1)} %shard_map.46.own, bf16[2,400,128]{2,1,0:T(8,128)(2,1)S(1)} %shard_map.47.own_scaled), custom_call_target="tpu_custom_call" | custom-call | flops 1000 | bytes 1000 | tf_op jit(solution)/shard_map/pallas_call | solution.py:264
  15.3 0.5 %shard_map.50 = (f32[315,126]{1,0:T(8,128)S(1)}, f32[315,126]{1,0:T(8,128)S(1)}) custom-call(bf16[2,126,400]{2,1,0:T(8,128)(2,1)S(1)} %shard_map.46.own, bf16[2,400,128]{2,1,0:T(8,128)(2,1)S(1)} %shard_map.47.own_scaled, f32[126,126]{1,0:T(8,128)S(1)} %shard_map.48.own_own, bf16[2,126,400]{2,1,0:T(8,128)(2,1)S(1)} %get-tuple-element.15.far, ...), custom_call_target="tpu_custom_call" | custom-call | flops 1000 | bytes 1000 | tf_op jit(solution)/shard_map/pallas_call | solution.py:264
  15.8 0.6 %collective-permute-start.3 = (f32[315,126]{1,0:T(8,128)S(1)}, f32[315,126]{1,0:T(8,128)S(1)}, u32[]{:S(2)}, u32[]{:S(2)}) collective-permute-start(f32[315,126]{1,0:T(8,128)S(1)} %get-tuple-element.19), channel_id=1, source_target_pairs={{0,1},{1,0},{2,3},{3,2},{4,5},{5,4},{6,7},{7,6},{8,9},{9,8},{10,11... | collective-permute-start | bytes 476288 | tf_op jit(solution)/shard_map/ppermute | solution.py:75
  16.4 0.0 collective-permute-done.4.theirs
  16.4 0.7 %collective-permute-start.5 = (f32[126,126]{1,0:T(8,128)S(1)}, f32[126,126]{1,0:T(8,128)S(1)}, u32[]{:S(2)}, u32[]{:S(2)}) collective-permute-start(f32[126,126]{1,0:T(8,128)S(1)} %get-tuple-element.23), channel_id=1, source_target_pairs={{0,3},{1,2},{2,1},{3,0},{4,7},{5,13},{6,14},{7,4},{8,11},{9,10},{1... | collective-permute-start | bytes 190520 | tf_op jit(solution)/shard_map/ppermute | solution.py:75
  17.1 1.6 %collective-permute-start.6 = (f32[63,126]{1,0:T(8,128)S(1)}, f32[63,126]{1,0:T(8,128)S(1)}, u32[]{:S(2)}, u32[]{:S(2)}) collective-permute-start(f32[63,126]{1,0:T(8,128)S(1)} %get-tuple-element.24), channel_id=1, source_target_pairs={{0,4},{1,5},{2,6},{3,7},{4,0},{5,1},{6,2},{7,3},{8,12},{9,13},{10,... | collective-permute-start | bytes 95264 | tf_op jit(solution)/shard_map/ppermute | solution.py:75
  18.7 2.3 %collective-permute-done.6.half_tile = f32[63,126]{1,0:T(8,128)S(1)} collective-permute-done((f32[63,126]{1,0:T(8,128)S(1)}, f32[63,126]{1,0:T(8,128)S(1)}, u32[]{:S(2)}, u32[]{:S(2)}) %collective-permute-start.6) | collective-permute-done | bytes 31784 | tf_op jit(solution)/shard_map/ppermute | solution.py:75
  21.0 0.0 collective-permute-done.3.theirs
  21.0 0.0 collective-permute-done.5.tile
  21.1 0.7 %shard_map.53 = f32[315,126]{1,0:T(8,128)} custom-call(f32[315,126]{1,0:T(8,128)S(1)} %get-tuple-element.18.mine, f32[315,126]{1,0:T(8,128)S(1)} %collective-permute-done.3.theirs, f32[126,126]{1,0:T(8,128)S(1)} %collective-permute-done.5.tile, f32[63,126]{1,0:T(8,128)S(1)} %collective-permute-done.6.half_tile), custom_call_target="tpu_custom_call" | custom-call | flops 1000 | bytes 1000 | tf_op jit(solution)/shard_map/pallas_call | solution.py:264
  (1 shorter events, 0.0 us)
Async XLA Ops:
  0.0 9.3 %collective-permute-start = (f32[400,126]{1,0:T(8,128)}, f32[400,126]{1,0:T(8,128)S(1)}, u32[]{:S(2)}, u32[]{:S(2)}) collective-permute-start(f32[400,126]{1,0:T(8,128)} %bitcast.3), channel_id=1, source_target_pairs={{0,2},{1,9},{2,0},{3,11},{4,6},{5,13},{6,4},{7,15},{8,10},{9,1},{1... | collective-permute-start | bytes 604808 | tf_op jit(solution)/shard_map/ppermute | solution.py:75
  2.9 11.1 %collective-permute-start.1 = (f32[400,126]{1,0:T(8,128)}, f32[400,126]{1,0:T(8,128)S(1)}, u32[]{:S(2)}, u32[]{:S(2)}) collective-permute-start(f32[400,126]{1,0:T(8,128)} %bitcast.4), channel_id=1, source_target_pairs={{0,6},{1,7},{2,4},{3,5},{4,0},{5,1},{6,2},{7,3},{8,14},{9,15},{10,... | collective-permute-start | bytes 604808 | tf_op jit(solution)/shard_map/ppermute | solution.py:75
  4.5 9.5 %collective-permute-start.2 = (f32[400,126]{1,0:T(8,128)}, f32[400,126]{1,0:T(8,128)S(1)}, u32[]{:S(2)}, u32[]{:S(2)}) collective-permute-start(f32[400,126]{1,0:T(8,128)} %bitcast.5), channel_id=1, source_target_pairs={{0,8},{1,3},{2,10},{3,1},{4,12},{5,7},{6,14},{7,5},{8,0},{9,11},{1... | collective-permute-start | bytes 604808 | tf_op jit(solution)/shard_map/ppermute | solution.py:75
  7.1 1.0 %copy-start = (f32[126,400]{0,1:T(8,128)S(1)}, f32[126,400]{0,1:T(8,128)}, u32[]{:S(2)}) copy-start(f32[126,400]{0,1:T(8,128)} %param.4) | copy-start | bytes 604804
  8.0 0.8 %copy-start.2 = (f32[200]{0:T(256)S(1)}, f32[200]{0:T(256)}, u32[]{:S(2)}) copy-start(f32[200]{0:T(256)} %param.6) | copy-start | bytes 2404
  8.0 0.9 %copy-start.3 = (f32[2]{0:T(128)S(1)}, f32[2]{0:T(128)}, u32[]{:S(2)}) copy-start(f32[2]{0:T(128)} %param.5) | copy-start | bytes 28
  8.2 1.0 %copy-start.1 = (f32[126,400]{0,1:T(8,128)S(1)}, f32[126,400]{0,1:T(8,128)}, u32[]{:S(2)}) copy-start(f32[126,400]{0,1:T(8,128)} %param.4) | copy-start | bytes 604804
  15.0 1.5 %collective-permute-start.4 = (f32[189,126]{1,0:T(8,128)S(1)}, f32[189,126]{1,0:T(8,128)S(1)}, u32[]{:S(2)}, u32[]{:S(2)}) collective-permute-start(f32[189,126]{1,0:T(8,128)S(1)} %get-tuple-element.22), channel_id=1, source_target_pairs={{0,1},{1,0},{2,3},{3,2},{4,5},{5,4},{6,7},{7,6},{8,9},{9,8},{10,11... | collective-permute-start | bytes 285776 | tf_op jit(solution)/shard_map/ppermute | solution.py:75
  15.8 5.2 %collective-permute-start.3 = (f32[315,126]{1,0:T(8,128)S(1)}, f32[315,126]{1,0:T(8,128)S(1)}, u32[]{:S(2)}, u32[]{:S(2)}) collective-permute-start(f32[315,126]{1,0:T(8,128)S(1)} %get-tuple-element.19), channel_id=1, source_target_pairs={{0,1},{1,0},{2,3},{3,2},{4,5},{5,4},{6,7},{7,6},{8,9},{9,8},{10,11... | collective-permute-start | bytes 476288 | tf_op jit(solution)/shard_map/ppermute | solution.py:75
  16.4 4.6 %collective-permute-start.5 = (f32[126,126]{1,0:T(8,128)S(1)}, f32[126,126]{1,0:T(8,128)S(1)}, u32[]{:S(2)}, u32[]{:S(2)}) collective-permute-start(f32[126,126]{1,0:T(8,128)S(1)} %get-tuple-element.23), channel_id=1, source_target_pairs={{0,3},{1,2},{2,1},{3,0},{4,7},{5,13},{6,14},{7,4},{8,11},{9,10},{1... | collective-permute-start | bytes 190520 | tf_op jit(solution)/shard_map/ppermute | solution.py:75
  17.1 3.9 %collective-permute-start.6 = (f32[63,126]{1,0:T(8,128)S(1)}, f32[63,126]{1,0:T(8,128)S(1)}, u32[]{:S(2)}, u32[]{:S(2)}) collective-permute-start(f32[63,126]{1,0:T(8,128)S(1)} %get-tuple-element.24), channel_id=1, source_target_pairs={{0,4},{1,5},{2,6},{3,7},{4,0},{5,1},{6,2},{7,3},{8,12},{9,13},{10,... | collective-permute-start | bytes 95264 | tf_op jit(solution)/shard_map/ppermute | solution.py:75

commit v8 on v7

--- a/solution.py
+++ b/solution.py
@@ -79,7 +79,7 @@
     return (z, x, 1 - c)
 
 
-ORDERS = (("xp", "zn", "far"), ("far", "zn", "xp"))
+ORDERS = (("zn", "xp", "far"), ("far", "zn", "xp"))
 
 
 def far_chip(z, x, c):

time: 21.9 us -> 21.9 us (level)
  starting transfers between devices: 10 us -> 11.3 us
  waiting for transfers between devices: 7.09 us -> 5.86 us
    ppermute x7, starting transfers between devices: 10 us -> 11.3 us  [sent(): return lax.ppermute(value, ('aux', 'pair'), pairs)]
    ppermute x7, waiting for transfers between devices: 7.09 us -> 5.86 us  [sent(): return lax.ppermute(value, ('aux', 'pair'), pairs)]
  transfers between devices with their start and end apart: 7 -> 7, of which waited for: 2 -> 3; matrix products, arithmetic and copies ran while one was open for 1% -> 1% of each run, Pallas kernels for 4% -> 4%
where the time goes in v8:
time: 21.9 us; the launch traced here: 21.8 us
  starting transfers between devices  11.3 us (52%)
  waiting for transfers between devices  5.86 us (27%)
  Pallas kernels  2.59 us (12%)
  local copies, waits for them, and re-layouts  1.18 us (5%)
  between operations  0.78 us (4%)
    ppermute x7, starting transfers between devices, sent(): return lax.ppermute(value, ('aux', 'pair'), pairs)  11.3 us
    ppermute x7, waiting for transfers between devices, sent(): return lax.ppermute(value, ('aux', 'pair'), pairs)  5.86 us
    pallas_call x8, Pallas kernels, in_vmem(): pl.pallas_call(kernel, out_shape=[jax.ShapeDtypeStruct(*out) for out in o...  2.59 us
    unnamed x8, local copies, waits for them, and re-layouts  0.98 us
  transfers between devices with their start and end apart: 7, of which 3 were waited for; matrix products, arithmetic and copies ran while one was open for 1% of the time, Pallas kernels for 4%

profile of v8, /device:TPU:0, one launch (start us, length us, event | category | flops | bytes accessed | tf_op | source)
XLA Modules:
  0.0 21.8 jit_solution(9679375488740821694)
XLA Ops:
  0.0 4.0 %collective-permute-start = (f32[400,126]{1,0:T(8,128)}, f32[400,126]{1,0:T(8,128)S(1)}, u32[]{:S(2)}, u32[]{:S(2)}) collective-permute-start(f32[400,126]{1,0:T(8,128)} %bitcast.3), channel_id=1, source_target_pairs={{0,6},{1,9},{2,4},{3,11},{4,0},{5,13},{6,2},{7,15},{8,14},{9,1},{1... | collective-permute-start | bytes 604808 | tf_op jit(solution)/shard_map/ppermute | solution.py:75
  4.0 0.5 %collective-permute-start.1 = (f32[400,126]{1,0:T(8,128)}, f32[400,126]{1,0:T(8,128)S(1)}, u32[]{:S(2)}, u32[]{:S(2)}) collective-permute-start(f32[400,126]{1,0:T(8,128)} %bitcast.4), channel_id=1, source_target_pairs={{0,2},{1,7},{2,0},{3,5},{4,6},{5,1},{6,4},{7,3},{8,10},{9,15},{10,... | collective-permute-start | bytes 604808 | tf_op jit(solution)/shard_map/ppermute | solution.py:75
  4.5 2.6 %collective-permute-start.2 = (f32[400,126]{1,0:T(8,128)}, f32[400,126]{1,0:T(8,128)S(1)}, u32[]{:S(2)}, u32[]{:S(2)}) collective-permute-start(f32[400,126]{1,0:T(8,128)} %bitcast.5), channel_id=1, source_target_pairs={{0,8},{1,3},{2,10},{3,1},{4,12},{5,7},{6,14},{7,5},{8,0},{9,11},{1... | collective-permute-start | bytes 604808 | tf_op jit(solution)/shard_map/ppermute | solution.py:75
  7.1 0.0 copy-start
  7.1 1.0 %copy-done = f32[126,400]{0,1:T(8,128)S(1)} copy-done((f32[126,400]{0,1:T(8,128)S(1)}, f32[126,400]{0,1:T(8,128)}, u32[]{:S(2)}) %copy-start) | copy-done | bytes 201624
  8.0 0.0 copy-start.2
  8.0 0.0 copy-start.3
  8.0 0.1 shard_map.46.own
  8.2 0.0 copy-start.1
  8.9 0.0 copy-done.2
  8.9 0.0 copy-done.3
  8.9 0.1 fusion
  9.0 0.1 div.11
  9.1 0.1 broadcast_in_dim.2.weight
  9.2 0.0 copy-done.1
  9.2 0.1 shard_map.47.own_scaled
  9.3 3.7 %collective-permute-done.refs_0_ = f32[400,126]{1,0:T(8,128)S(1)} collective-permute-done((f32[400,126]{1,0:T(8,128)}, f32[400,126]{1,0:T(8,128)S(1)}, u32[]{:S(2)}, u32[]{:S(2)}) %collective-permute-start) | collective-permute-done | bytes 201632 | tf_op jit(solution)/shard_map/ppermute | solution.py:75
  13.0 0.0 collective-permute-done.1.refs_1_
  13.0 0.1 collective-permute-done.2.refs_2_
  13.1 0.3 %shard_map.49 = (bf16[2,126,400]{2,1,0:T(8,128)(2,1)S(1)}, bf16[2,126,400]{2,1,0:T(8,128)(2,1)S(1)}, bf16[2,400,128]{2,1,0:T(8,128)(2,1)S(1)}, bf16[2,400,128]{2,1,0:T(8,128)(2,1)S(1)}) custom-call(f32[400,126]{1,0:T(8,128)S(1)} %broadcast_in_dim.2.weight, f32[400,126]{1,0:T(8,128)S(1)} %collective-permute-done.refs_0_, ...), custom_call_target="tpu_custom_call" | custom-call | flops 1000 | bytes 1000 | tf_op jit(solution)/shard_map/pallas_call | solution.py:264
  13.4 0.6 %shard_map.51 = (f32[189,126]{1,0:T(8,128)S(1)}, f32[189,126]{1,0:T(8,128)S(1)}) custom-call(bf16[2,126,400]{2,1,0:T(8,128)(2,1)S(1)} %get-tuple-element.15.far, bf16[2,126,400]{2,1,0:T(8,128)(2,1)S(1)} %get-tuple-element.16.xp, bf16[2,400,128]{2,1,0:T(8,128)(2,1)S(1)} %get-tuple-element.20.xp_scaled, bf16[2,400,128]{2,1,0:T(8,128)(2,1)S(1)} %get-tuple-element.17.zn_scaled), custom_call_target="tpu_custom_call" | custom-call | flops 1000 | bytes 1000 | tf_op jit(solution)/shard_map/pallas_call | solution.py:264
  14.1 0.3 %collective-permute-start.4 = (f32[189,126]{1,0:T(8,128)S(1)}, f32[189,126]{1,0:T(8,128)S(1)}, u32[]{:S(2)}, u32[]{:S(2)}) collective-permute-start(f32[189,126]{1,0:T(8,128)S(1)} %get-tuple-element.22), channel_id=1, source_target_pairs={{0,1},{1,0},{2,3},{3,2},{4,5},{5,4},{6,7},{7,6},{8,9},{9,8},{10,11... | collective-permute-start | bytes 285776 | tf_op jit(solution)/shard_map/ppermute | solution.py:75
  14.4 0.2 %shard_map.48.own_own = f32[126,126]{1,0:T(8,128)S(1)} custom-call(bf16[2,126,400]{2,1,0:T(8,128)(2,1)S(1)} %shard_map.46.own, bf16[2,400,128]{2,1,0:T(8,128)(2,1)S(1)} %shard_map.47.own_scaled), custom_call_target="tpu_custom_call" | custom-call | flops 1000 | bytes 1000 | tf_op jit(solution)/shard_map/pallas_call | solution.py:264
  14.6 0.5 %shard_map.50 = (f32[315,126]{1,0:T(8,128)S(1)}, f32[315,126]{1,0:T(8,128)S(1)}) custom-call(bf16[2,126,400]{2,1,0:T(8,128)(2,1)S(1)} %shard_map.46.own, bf16[2,400,128]{2,1,0:T(8,128)(2,1)S(1)} %shard_map.47.own_scaled, f32[126,126]{1,0:T(8,128)S(1)} %shard_map.48.own_own, bf16[2,126,400]{2,1,0:T(8,128)(2,1)S(1)} %get-tuple-element.15.far, ...), custom_call_target="tpu_custom_call" | custom-call | flops 1000 | bytes 1000 | tf_op jit(solution)/shard_map/pallas_call | solution.py:264
  15.2 0.4 %collective-permute-start.3 = (f32[315,126]{1,0:T(8,128)S(1)}, f32[315,126]{1,0:T(8,128)S(1)}, u32[]{:S(2)}, u32[]{:S(2)}) collective-permute-start(f32[315,126]{1,0:T(8,128)S(1)} %get-tuple-element.19), channel_id=1, source_target_pairs={{0,1},{1,0},{2,3},{3,2},{4,5},{5,4},{6,7},{7,6},{8,9},{9,8},{10,11... | collective-permute-start | bytes 476288 | tf_op jit(solution)/shard_map/ppermute | solution.py:75
  15.5 0.0 collective-permute-done.4.theirs
  15.5 1.6 %collective-permute-start.5 = (f32[126,126]{1,0:T(8,128)S(1)}, f32[126,126]{1,0:T(8,128)S(1)}, u32[]{:S(2)}, u32[]{:S(2)}) collective-permute-start(f32[126,126]{1,0:T(8,128)S(1)} %get-tuple-element.23), channel_id=1, source_target_pairs={{0,3},{1,2},{2,1},{3,0},{4,7},{5,13},{6,14},{7,4},{8,11},{9,10},{1... | collective-permute-start | bytes 190520 | tf_op jit(solution)/shard_map/ppermute | solution.py:75
  17.1 1.9 %collective-permute-start.6 = (f32[63,126]{1,0:T(8,128)S(1)}, f32[63,126]{1,0:T(8,128)S(1)}, u32[]{:S(2)}, u32[]{:S(2)}) collective-permute-start(f32[63,126]{1,0:T(8,128)S(1)} %get-tuple-element.24), channel_id=1, source_target_pairs={{0,4},{1,5},{2,6},{3,7},{4,0},{5,1},{6,2},{7,3},{8,12},{9,13},{10,... | collective-permute-start | bytes 95264 | tf_op jit(solution)/shard_map/ppermute | solution.py:75
  19.1 2.0 %collective-permute-done.6.half_tile = f32[63,126]{1,0:T(8,128)S(1)} collective-permute-done((f32[63,126]{1,0:T(8,128)S(1)}, f32[63,126]{1,0:T(8,128)S(1)}, u32[]{:S(2)}, u32[]{:S(2)}) %collective-permute-start.6) | collective-permute-done | bytes 31784 | tf_op jit(solution)/shard_map/ppermute | solution.py:75
  21.0 0.0 collective-permute-done.3.theirs
  21.0 0.0 collective-permute-done.5.tile
  21.1 0.7 %shard_map.53 = f32[315,126]{1,0:T(8,128)} custom-call(f32[315,126]{1,0:T(8,128)S(1)} %get-tuple-element.18.mine, f32[315,126]{1,0:T(8,128)S(1)} %collective-permute-done.3.theirs, f32[126,126]{1,0:T(8,128)S(1)} %collective-permute-done.5.tile, f32[63,126]{1,0:T(8,128)S(1)} %collective-permute-done.6.half_tile), custom_call_target="tpu_custom_call" | custom-call | flops 1000 | bytes 1000 | tf_op jit(solution)/shard_map/pallas_call | solution.py:264
  (1 shorter events, 0.0 us)
Async XLA Ops:
  0.0 13.0 %collective-permute-start = (f32[400,126]{1,0:T(8,128)}, f32[400,126]{1,0:T(8,128)S(1)}, u32[]{:S(2)}, u32[]{:S(2)}) collective-permute-start(f32[400,126]{1,0:T(8,128)} %bitcast.3), channel_id=1, source_target_pairs={{0,6},{1,9},{2,4},{3,11},{4,0},{5,13},{6,2},{7,15},{8,14},{9,1},{1... | collective-permute-start | bytes 604808 | tf_op jit(solution)/shard_map/ppermute | solution.py:75
  4.0 9.0 %collective-permute-start.1 = (f32[400,126]{1,0:T(8,128)}, f32[400,126]{1,0:T(8,128)S(1)}, u32[]{:S(2)}, u32[]{:S(2)}) collective-permute-start(f32[400,126]{1,0:T(8,128)} %bitcast.4), channel_id=1, source_target_pairs={{0,2},{1,7},{2,0},{3,5},{4,6},{5,1},{6,4},{7,3},{8,10},{9,15},{10,... | collective-permute-start | bytes 604808 | tf_op jit(solution)/shard_map/ppermute | solution.py:75
  4.5 8.6 %collective-permute-start.2 = (f32[400,126]{1,0:T(8,128)}, f32[400,126]{1,0:T(8,128)S(1)}, u32[]{:S(2)}, u32[]{:S(2)}) collective-permute-start(f32[400,126]{1,0:T(8,128)} %bitcast.5), channel_id=1, source_target_pairs={{0,8},{1,3},{2,10},{3,1},{4,12},{5,7},{6,14},{7,5},{8,0},{9,11},{1... | collective-permute-start | bytes 604808 | tf_op jit(solution)/shard_map/ppermute | solution.py:75
  7.1 1.0 %copy-start = (f32[126,400]{0,1:T(8,128)S(1)}, f32[126,400]{0,1:T(8,128)}, u32[]{:S(2)}) copy-start(f32[126,400]{0,1:T(8,128)} %param.4) | copy-start | bytes 604804
  8.0 0.8 %copy-start.2 = (f32[200]{0:T(256)S(1)}, f32[200]{0:T(256)}, u32[]{:S(2)}) copy-start(f32[200]{0:T(256)} %param.6) | copy-start | bytes 2404
  8.0 0.9 %copy-start.3 = (f32[2]{0:T(128)S(1)}, f32[2]{0:T(128)}, u32[]{:S(2)}) copy-start(f32[2]{0:T(128)} %param.5) | copy-start | bytes 28
  8.2 1.0 %copy-start.1 = (f32[126,400]{0,1:T(8,128)S(1)}, f32[126,400]{0,1:T(8,128)}, u32[]{:S(2)}) copy-start(f32[126,400]{0,1:T(8,128)} %param.4) | copy-start | bytes 604804
  14.1 1.5 %collective-permute-start.4 = (f32[189,126]{1,0:T(8,128)S(1)}, f32[189,126]{1,0:T(8,128)S(1)}, u32[]{:S(2)}, u32[]{:S(2)}) collective-permute-start(f32[189,126]{1,0:T(8,128)S(1)} %get-tuple-element.22), channel_id=1, source_target_pairs={{0,1},{1,0},{2,3},{3,2},{4,5},{5,4},{6,7},{7,6},{8,9},{9,8},{10,11... | collective-permute-start | bytes 285776 | tf_op jit(solution)/shard_map/ppermute | solution.py:75
  15.2 5.9 %collective-permute-start.3 = (f32[315,126]{1,0:T(8,128)S(1)}, f32[315,126]{1,0:T(8,128)S(1)}, u32[]{:S(2)}, u32[]{:S(2)}) collective-permute-start(f32[315,126]{1,0:T(8,128)S(1)} %get-tuple-element.19), channel_id=1, source_target_pairs={{0,1},{1,0},{2,3},{3,2},{4,5},{5,4},{6,7},{7,6},{8,9},{9,8},{10,11... | collective-permute-start | bytes 476288 | tf_op jit(solution)/shard_map/ppermute | solution.py:75
  15.5 5.5 %collective-permute-start.5 = (f32[126,126]{1,0:T(8,128)S(1)}, f32[126,126]{1,0:T(8,128)S(1)}, u32[]{:S(2)}, u32[]{:S(2)}) collective-permute-start(f32[126,126]{1,0:T(8,128)S(1)} %get-tuple-element.23), channel_id=1, source_target_pairs={{0,3},{1,2},{2,1},{3,0},{4,7},{5,13},{6,14},{7,4},{8,11},{9,10},{1... | collective-permute-start | bytes 190520 | tf_op jit(solution)/shard_map/ppermute | solution.py:75
  17.1 3.9 %collective-permute-start.6 = (f32[63,126]{1,0:T(8,128)S(1)}, f32[63,126]{1,0:T(8,128)S(1)}, u32[]{:S(2)}, u32[]{:S(2)}) collective-permute-start(f32[63,126]{1,0:T(8,128)S(1)} %get-tuple-element.24), channel_id=1, source_target_pairs={{0,4},{1,5},{2,6},{3,7},{4,0},{5,1},{6,2},{7,3},{8,12},{9,13},{10,... | collective-permute-start | bytes 95264 | tf_op jit(solution)/shard_map/ppermute | solution.py:75

commit v9 on v8

--- a/solution.py
+++ b/solution.py
@@ -150,13 +150,20 @@
                 xp_right[...] = jnp.zeros_like(xp_right)
 
 
-def meet_kernel(far, xp, xp_scaled, zn_scaled, mine, theirs):
+def meet_kernel(far, xp, xp_scaled, zn_scaled, mine, theirs, by_far):
     even, x, c = place()
     rows = mine.shape[1]
     half = rows // 2
-    scaled = [jnp.concatenate([zn_scaled[i], xp_scaled[i]], 1) for i in range(2)]
-    by_far = product(far, scaled)
-    far_zn, far_xp = by_far[:, :rows], by_far[:, 128 : 128 + rows]
+    @pl.when(x == 0)
+    def _():
+        scaled = [jnp.concatenate([zn_scaled[i], xp_scaled[i]], 1) for i in range(2)]
+        by_far[...] = product(far, scaled)
+
+    @pl.when(x == 1)
+    def _():
+        by_far[:, pl.ds(0, 128)] = product(far, zn_scaled)
+
+    far_zn = by_far[:, pl.ds(0, rows)]
 
     def put(core, row, values):
         @pl.when(c == core)
@@ -177,7 +184,7 @@
 
         @pl.when(x == 0)
         def _():
-            put(0, 0, far_xp)
+            put(0, 0, by_far[:, pl.ds(128, rows)])
 
         @pl.when(x == 1)
         def _():
@@ -190,7 +197,7 @@
 
         @pl.when(x == 0)
         def _():
-            put(0, 0, far_xp)
+            put(0, 0, by_far[:, pl.ds(128, rows)])
 
         @pl.when(x == 1)
         def _():
@@ -259,15 +266,16 @@
         response[pl.ds(0, half), :] = half_tile[...]
 
 
-def in_vmem(kernel, outs, *operands, flops=1000):
+def in_vmem(kernel, outs, *operands, scratch=()):
     whole = pl.BlockSpec(memory_space=pltpu.VMEM)
     return pl.pallas_call(
         kernel,
         out_shape=[jax.ShapeDtypeStruct(*out) for out in outs],
         in_specs=[whole] * len(operands),
         out_specs=[whole] * len(outs),
+        scratch_shapes=[pltpu.VMEM(shape, jnp.float32) for shape in scratch],
         compiler_params=pltpu.CompilerParams(vmem_limit_bytes=32 * 1024 * 1024),
-        cost_estimate=pl.CostEstimate(flops=flops, bytes_accessed=1000, transcendentals=0),
+        cost_estimate=pl.CostEstimate(flops=1000, bytes_accessed=1000, transcendentals=0),
     )(*operands)
 
 
@@ -290,7 +298,15 @@
     (own_right,) = in_vmem(right_kernel, [right], weight, own)
     (own_own,) = in_vmem(own_kernel, [square], own_left, own_right)
     parts = ((3 * rows // 2, rows), jnp.float32)
-    mine, theirs = in_vmem(meet_kernel, [parts] * 2, far_left, xp_left, xp_right, zn_right)
+    mine, theirs = in_vmem(
+        meet_kernel,
+        [parts] * 2,
+        far_left,
+        xp_left,
+        xp_right,
+        zn_right,
+        scratch=[(rows, 256)],
+    )
     tile, half_tile = in_vmem(
         sum_kernel, [square, half_square], mine, sent(theirs, other_core)
     )

time: 21.9 us -> 21.9 us (level)
  no operation moved by 1% of the time
where the time goes in v9:
time: 21.9 us; the launch traced here: 21.8 us
  starting transfers between devices  11.3 us (52%)
  waiting for transfers between devices  5.87 us (27%)
  Pallas kernels  2.62 us (12%)
  local copies, waits for them, and re-layouts  1.18 us (5%)
  between operations  0.78 us (4%)
    ppermute x7, starting transfers between devices, sent(): return lax.ppermute(value, ('aux', 'pair'), pairs)  11.3 us
    ppermute x7, waiting for transfers between devices, sent(): return lax.ppermute(value, ('aux', 'pair'), pairs)  5.87 us
    pallas_call x8, Pallas kernels, in_vmem(): pl.pallas_call(kernel, out_shape=[jax.ShapeDtypeStruct(*out) for out in o...  2.62 us
    unnamed x8, local copies, waits for them, and re-layouts  0.98 us
  transfers between devices with their start and end apart: 7, of which 3 were waited for; matrix products, arithmetic and copies ran while one was open for 1% of the time, Pallas kernels for 4%

profile of v9, /device:TPU:0, one launch (start us, length us, event | category | flops | bytes accessed | tf_op | source)
XLA Modules:
  0.0 21.8 jit_solution(399236214776474837)
XLA Ops:
  0.0 4.0 %collective-permute-start = (f32[400,126]{1,0:T(8,128)}, f32[400,126]{1,0:T(8,128)S(1)}, u32[]{:S(2)}, u32[]{:S(2)}) collective-permute-start(f32[400,126]{1,0:T(8,128)} %bitcast.3), channel_id=1, source_target_pairs={{0,6},{1,9},{2,4},{3,11},{4,0},{5,13},{6,2},{7,15},{8,14},{9,1},{1... | collective-permute-start | bytes 604808 | tf_op jit(solution)/shard_map/ppermute | solution.py:75
  4.0 0.5 %collective-permute-start.1 = (f32[400,126]{1,0:T(8,128)}, f32[400,126]{1,0:T(8,128)S(1)}, u32[]{:S(2)}, u32[]{:S(2)}) collective-permute-start(f32[400,126]{1,0:T(8,128)} %bitcast.4), channel_id=1, source_target_pairs={{0,2},{1,7},{2,0},{3,5},{4,6},{5,1},{6,4},{7,3},{8,10},{9,15},{10,... | collective-permute-start | bytes 604808 | tf_op jit(solution)/shard_map/ppermute | solution.py:75
  4.5 2.6 %collective-permute-start.2 = (f32[400,126]{1,0:T(8,128)}, f32[400,126]{1,0:T(8,128)S(1)}, u32[]{:S(2)}, u32[]{:S(2)}) collective-permute-start(f32[400,126]{1,0:T(8,128)} %bitcast.5), channel_id=1, source_target_pairs={{0,8},{1,3},{2,10},{3,1},{4,12},{5,7},{6,14},{7,5},{8,0},{9,11},{1... | collective-permute-start | bytes 604808 | tf_op jit(solution)/shard_map/ppermute | solution.py:75
  7.1 0.0 copy-start
  7.1 1.0 %copy-done = f32[126,400]{0,1:T(8,128)S(1)} copy-done((f32[126,400]{0,1:T(8,128)S(1)}, f32[126,400]{0,1:T(8,128)}, u32[]{:S(2)}) %copy-start) | copy-done | bytes 201624
  8.0 0.0 copy-start.2
  8.0 0.0 copy-start.3
  8.0 0.1 shard_map.46.own
  8.2 0.0 copy-start.1
  8.9 0.0 copy-done.2
  8.9 0.0 copy-done.3
  8.9 0.1 fusion
  9.0 0.1 div.11
  9.1 0.1 broadcast_in_dim.2.weight
  9.2 0.0 copy-done.1
  9.2 0.1 shard_map.47.own_scaled
  9.3 3.7 %collective-permute-done.refs_0_ = f32[400,126]{1,0:T(8,128)S(1)} collective-permute-done((f32[400,126]{1,0:T(8,128)}, f32[400,126]{1,0:T(8,128)S(1)}, u32[]{:S(2)}, u32[]{:S(2)}) %collective-permute-start) | collective-permute-done | bytes 201632 | tf_op jit(solution)/shard_map/ppermute | solution.py:75
  13.0 0.0 collective-permute-done.1.refs_1_
  13.0 0.1 collective-permute-done.2.refs_2_
  13.1 0.3 %shard_map.49 = (bf16[2,126,400]{2,1,0:T(8,128)(2,1)S(1)}, bf16[2,126,400]{2,1,0:T(8,128)(2,1)S(1)}, bf16[2,400,128]{2,1,0:T(8,128)(2,1)S(1)}, bf16[2,400,128]{2,1,0:T(8,128)(2,1)S(1)}) custom-call(f32[400,126]{1,0:T(8,128)S(1)} %broadcast_in_dim.2.weight, f32[400,126]{1,0:T(8,128)S(1)} %collective-permute-done.refs_0_, ...), custom_call_target="tpu_custom_call" | custom-call | flops 1000 | bytes 1000 | tf_op jit(solution)/shard_map/pallas_call | solution.py:271
  13.4 0.6 %shard_map.51 = (f32[189,126]{1,0:T(8,128)S(1)}, f32[189,126]{1,0:T(8,128)S(1)}) custom-call(bf16[2,126,400]{2,1,0:T(8,128)(2,1)S(1)} %get-tuple-element.15.far, bf16[2,126,400]{2,1,0:T(8,128)(2,1)S(1)} %get-tuple-element.16.xp, bf16[2,400,128]{2,1,0:T(8,128)(2,1)S(1)} %get-tuple-element.20.xp_scaled, bf16[2,400,128]{2,1,0:T(8,128)(2,1)S(1)} %get-tuple-element.17.zn_scaled), custom_call_target="tpu_custom_call" | custom-call | flops 1000 | bytes 1000 | tf_op jit(solution)/shard_map/pallas_call | solution.py:271
  14.1 0.3 %collective-permute-start.4 = (f32[189,126]{1,0:T(8,128)S(1)}, f32[189,126]{1,0:T(8,128)S(1)}, u32[]{:S(2)}, u32[]{:S(2)}) collective-permute-start(f32[189,126]{1,0:T(8,128)S(1)} %get-tuple-element.22), channel_id=1, source_target_pairs={{0,1},{1,0},{2,3},{3,2},{4,5},{5,4},{6,7},{7,6},{8,9},{9,8},{10,11... | collective-permute-start | bytes 285776 | tf_op jit(solution)/shard_map/ppermute | solution.py:75
  14.4 0.2 %shard_map.48.own_own = f32[126,126]{1,0:T(8,128)S(1)} custom-call(bf16[2,126,400]{2,1,0:T(8,128)(2,1)S(1)} %shard_map.46.own, bf16[2,400,128]{2,1,0:T(8,128)(2,1)S(1)} %shard_map.47.own_scaled), custom_call_target="tpu_custom_call" | custom-call | flops 1000 | bytes 1000 | tf_op jit(solution)/shard_map/pallas_call | solution.py:271
  14.6 0.5 %shard_map.50 = (f32[315,126]{1,0:T(8,128)S(1)}, f32[315,126]{1,0:T(8,128)S(1)}) custom-call(bf16[2,126,400]{2,1,0:T(8,128)(2,1)S(1)} %shard_map.46.own, bf16[2,400,128]{2,1,0:T(8,128)(2,1)S(1)} %shard_map.47.own_scaled, f32[126,126]{1,0:T(8,128)S(1)} %shard_map.48.own_own, bf16[2,126,400]{2,1,0:T(8,128)(2,1)S(1)} %get-tuple-element.15.far, ...), custom_call_target="tpu_custom_call" | custom-call | flops 1000 | bytes 1000 | tf_op jit(solution)/shard_map/pallas_call | solution.py:271
  15.2 0.4 %collective-permute-start.3 = (f32[315,126]{1,0:T(8,128)S(1)}, f32[315,126]{1,0:T(8,128)S(1)}, u32[]{:S(2)}, u32[]{:S(2)}) collective-permute-start(f32[315,126]{1,0:T(8,128)S(1)} %get-tuple-element.19), channel_id=1, source_target_pairs={{0,1},{1,0},{2,3},{3,2},{4,5},{5,4},{6,7},{7,6},{8,9},{9,8},{10,11... | collective-permute-start | bytes 476288 | tf_op jit(solution)/shard_map/ppermute | solution.py:75
  15.5 0.0 collective-permute-done.4.theirs
  15.6 1.6 %collective-permute-start.5 = (f32[126,126]{1,0:T(8,128)S(1)}, f32[126,126]{1,0:T(8,128)S(1)}, u32[]{:S(2)}, u32[]{:S(2)}) collective-permute-start(f32[126,126]{1,0:T(8,128)S(1)} %get-tuple-element.23), channel_id=1, source_target_pairs={{0,3},{1,2},{2,1},{3,0},{4,7},{5,13},{6,14},{7,4},{8,11},{9,10},{1... | collective-permute-start | bytes 190520 | tf_op jit(solution)/shard_map/ppermute | solution.py:75
  17.2 1.9 %collective-permute-start.6 = (f32[63,126]{1,0:T(8,128)S(1)}, f32[63,126]{1,0:T(8,128)S(1)}, u32[]{:S(2)}, u32[]{:S(2)}) collective-permute-start(f32[63,126]{1,0:T(8,128)S(1)} %get-tuple-element.24), channel_id=1, source_target_pairs={{0,4},{1,5},{2,6},{3,7},{4,0},{5,1},{6,2},{7,3},{8,12},{9,13},{10,... | collective-permute-start | bytes 95264 | tf_op jit(solution)/shard_map/ppermute | solution.py:75
  19.1 2.0 %collective-permute-done.6.half_tile = f32[63,126]{1,0:T(8,128)S(1)} collective-permute-done((f32[63,126]{1,0:T(8,128)S(1)}, f32[63,126]{1,0:T(8,128)S(1)}, u32[]{:S(2)}, u32[]{:S(2)}) %collective-permute-start.6) | collective-permute-done | bytes 31784 | tf_op jit(solution)/shard_map/ppermute | solution.py:75
  21.1 0.0 collective-permute-done.3.theirs
  21.1 0.0 collective-permute-done.5.tile
  21.1 0.7 %shard_map.53 = f32[315,126]{1,0:T(8,128)} custom-call(f32[315,126]{1,0:T(8,128)S(1)} %get-tuple-element.18.mine, f32[315,126]{1,0:T(8,128)S(1)} %collective-permute-done.3.theirs, f32[126,126]{1,0:T(8,128)S(1)} %collective-permute-done.5.tile, f32[63,126]{1,0:T(8,128)S(1)} %collective-permute-done.6.half_tile), custom_call_target="tpu_custom_call" | custom-call | flops 1000 | bytes 1000 | tf_op jit(solution)/shard_map/pallas_call | solution.py:271
  (1 shorter events, 0.0 us)
Async XLA Ops:
  0.0 13.0 %collective-permute-start = (f32[400,126]{1,0:T(8,128)}, f32[400,126]{1,0:T(8,128)S(1)}, u32[]{:S(2)}, u32[]{:S(2)}) collective-permute-start(f32[400,126]{1,0:T(8,128)} %bitcast.3), channel_id=1, source_target_pairs={{0,6},{1,9},{2,4},{3,11},{4,0},{5,13},{6,2},{7,15},{8,14},{9,1},{1... | collective-permute-start | bytes 604808 | tf_op jit(solution)/shard_map/ppermute | solution.py:75
  4.0 9.0 %collective-permute-start.1 = (f32[400,126]{1,0:T(8,128)}, f32[400,126]{1,0:T(8,128)S(1)}, u32[]{:S(2)}, u32[]{:S(2)}) collective-permute-start(f32[400,126]{1,0:T(8,128)} %bitcast.4), channel_id=1, source_target_pairs={{0,2},{1,7},{2,0},{3,5},{4,6},{5,1},{6,4},{7,3},{8,10},{9,15},{10,... | collective-permute-start | bytes 604808 | tf_op jit(solution)/shard_map/ppermute | solution.py:75
  4.5 8.6 %collective-permute-start.2 = (f32[400,126]{1,0:T(8,128)}, f32[400,126]{1,0:T(8,128)S(1)}, u32[]{:S(2)}, u32[]{:S(2)}) collective-permute-start(f32[400,126]{1,0:T(8,128)} %bitcast.5), channel_id=1, source_target_pairs={{0,8},{1,3},{2,10},{3,1},{4,12},{5,7},{6,14},{7,5},{8,0},{9,11},{1... | collective-permute-start | bytes 604808 | tf_op jit(solution)/shard_map/ppermute | solution.py:75
  7.1 1.0 %copy-start = (f32[126,400]{0,1:T(8,128)S(1)}, f32[126,400]{0,1:T(8,128)}, u32[]{:S(2)}) copy-start(f32[126,400]{0,1:T(8,128)} %param.4) | copy-start | bytes 604804
  8.0 0.8 %copy-start.2 = (f32[200]{0:T(256)S(1)}, f32[200]{0:T(256)}, u32[]{:S(2)}) copy-start(f32[200]{0:T(256)} %param.6) | copy-start | bytes 2404
  8.0 0.9 %copy-start.3 = (f32[2]{0:T(128)S(1)}, f32[2]{0:T(128)}, u32[]{:S(2)}) copy-start(f32[2]{0:T(128)} %param.5) | copy-start | bytes 28
  8.2 1.0 %copy-start.1 = (f32[126,400]{0,1:T(8,128)S(1)}, f32[126,400]{0,1:T(8,128)}, u32[]{:S(2)}) copy-start(f32[126,400]{0,1:T(8,128)} %param.4) | copy-start | bytes 604804
  14.1 1.5 %collective-permute-start.4 = (f32[189,126]{1,0:T(8,128)S(1)}, f32[189,126]{1,0:T(8,128)S(1)}, u32[]{:S(2)}, u32[]{:S(2)}) collective-permute-start(f32[189,126]{1,0:T(8,128)S(1)} %get-tuple-element.22), channel_id=1, source_target_pairs={{0,1},{1,0},{2,3},{3,2},{4,5},{5,4},{6,7},{7,6},{8,9},{9,8},{10,11... | collective-permute-start | bytes 285776 | tf_op jit(solution)/shard_map/ppermute | solution.py:75
  15.2 5.9 %collective-permute-start.3 = (f32[315,126]{1,0:T(8,128)S(1)}, f32[315,126]{1,0:T(8,128)S(1)}, u32[]{:S(2)}, u32[]{:S(2)}) collective-permute-start(f32[315,126]{1,0:T(8,128)S(1)} %get-tuple-element.19), channel_id=1, source_target_pairs={{0,1},{1,0},{2,3},{3,2},{4,5},{5,4},{6,7},{7,6},{8,9},{9,8},{10,11... | collective-permute-start | bytes 476288 | tf_op jit(solution)/shard_map/ppermute | solution.py:75
  15.6 5.5 %collective-permute-start.5 = (f32[126,126]{1,0:T(8,128)S(1)}, f32[126,126]{1,0:T(8,128)S(1)}, u32[]{:S(2)}, u32[]{:S(2)}) collective-permute-start(f32[126,126]{1,0:T(8,128)S(1)} %get-tuple-element.23), channel_id=1, source_target_pairs={{0,3},{1,2},{2,1},{3,0},{4,7},{5,13},{6,14},{7,4},{8,11},{9,10},{1... | collective-permute-start | bytes 190520 | tf_op jit(solution)/shard_map/ppermute | solution.py:75
  17.2 3.9 %collective-permute-start.6 = (f32[63,126]{1,0:T(8,128)S(1)}, f32[63,126]{1,0:T(8,128)S(1)}, u32[]{:S(2)}, u32[]{:S(2)}) collective-permute-start(f32[63,126]{1,0:T(8,128)S(1)} %get-tuple-element.24), channel_id=1, source_target_pairs={{0,4},{1,5},{2,6},{3,7},{4,0},{5,1},{6,2},{7,3},{8,12},{9,13},{10,... | collective-permute-start | bytes 95264 | tf_op jit(solution)/shard_map/ppermute | solution.py:75

commit v10 on v8

--- a/solution.py
+++ b/solution.py
@@ -79,7 +79,7 @@
     return (z, x, 1 - c)
 
 
-ORDERS = (("zn", "xp", "far"), ("far", "zn", "xp"))
+ORDERS = (("far", "xp", "zn"), ("xp", "zn", "far"))
 
 
 def far_chip(z, x, c):
@@ -283,12 +283,13 @@
     blocks = [
         sent(own, lambda z, x, c, slot=slot: routes[ORDERS[c][slot]](z, x, c)) for slot in range(3)
     ]
-    far_left, xp_left, xp_right, zn_right = in_vmem(
-        functools.partial(ready_kernel, ORDERS), [left, left, right, right], weight, *blocks
-    )
     (own_left,) = in_vmem(left_kernel, [left], own)
     (own_right,) = in_vmem(right_kernel, [right], weight, own)
     (own_own,) = in_vmem(own_kernel, [square], own_left, own_right)
+    weight, own_own = lax.optimization_barrier((weight, own_own))
+    far_left, xp_left, xp_right, zn_right = in_vmem(
+        functools.partial(ready_kernel, ORDERS), [left, left, right, right], weight, *blocks
+    )
     parts = ((3 * rows // 2, rows), jnp.float32)
     mine, theirs = in_vmem(meet_kernel, [parts] * 2, far_left, xp_left, xp_right, zn_right)
     tile, half_tile = in_vmem(

time: 21.9 us -> 21.9 us (level)
  transfers between devices with their start and end apart: 7 -> 7, of which waited for: 3 -> 4; matrix products, arithmetic and copies ran while one was open for 1% -> 1% of each run, Pallas kernels for 4% -> 4%
where the time goes in v10:
time: 21.9 us; the launch traced here: 21.7 us
  starting transfers between devices  11.3 us (52%)
  waiting for transfers between devices  5.81 us (27%)
  Pallas kernels  2.59 us (12%)
  local copies, waits for them, and re-layouts  1.18 us (5%)
  between operations  0.78 us (4%)
    ppermute x7, starting transfers between devices, sent(): return lax.ppermute(value, ('aux', 'pair'), pairs)  11.3 us
    ppermute x7, waiting for transfers between devices, sent(): return lax.ppermute(value, ('aux', 'pair'), pairs)  5.81 us
    pallas_call x8, Pallas kernels, in_vmem(): pl.pallas_call(kernel, out_shape=[jax.ShapeDtypeStruct(*out) for out in o...  2.59 us
    unnamed x8, local copies, waits for them, and re-layouts  0.98 us
  transfers between devices with their start and end apart: 7, of which 4 were waited for; matrix products, arithmetic and copies ran while one was open for 1% of the time, Pallas kernels for 4%

profile of v10, /device:TPU:0, one launch (start us, length us, event | category | flops | bytes accessed | tf_op | source)
XLA Modules:
  0.0 21.7 jit_solution(12690546686539143452)
XLA Ops:
  0.0 4.0 %collective-permute-start.2 = (f32[400,126]{1,0:T(8,128)}, f32[400,126]{1,0:T(8,128)S(1)}, u32[]{:S(2)}, u32[]{:S(2)}) collective-permute-start(f32[400,126]{1,0:T(8,128)} %bitcast.3), channel_id=1, source_target_pairs={{0,6},{1,9},{2,4},{3,11},{4,0},{5,13},{6,2},{7,15},{8,14},{9,1},{1... | collective-permute-start | bytes 604808 | tf_op jit(solution)/shard_map/ppermute | solution.py:75
  4.0 0.5 %collective-permute-start.1 = (f32[400,126]{1,0:T(8,128)}, f32[400,126]{1,0:T(8,128)S(1)}, u32[]{:S(2)}, u32[]{:S(2)}) collective-permute-start(f32[400,126]{1,0:T(8,128)} %bitcast.4), channel_id=1, source_target_pairs={{0,2},{1,7},{2,0},{3,5},{4,6},{5,1},{6,4},{7,3},{8,10},{9,15},{10,... | collective-permute-start | bytes 604808 | tf_op jit(solution)/shard_map/ppermute | solution.py:75
  4.5 2.6 %collective-permute-start = (f32[400,126]{1,0:T(8,128)}, f32[400,126]{1,0:T(8,128)S(1)}, u32[]{:S(2)}, u32[]{:S(2)}) collective-permute-start(f32[400,126]{1,0:T(8,128)} %bitcast.5), channel_id=1, source_target_pairs={{0,8},{1,3},{2,10},{3,1},{4,12},{5,7},{6,14},{7,5},{8,0},{9,11},{1... | collective-permute-start | bytes 604808 | tf_op jit(solution)/shard_map/ppermute | solution.py:75
  7.1 0.0 copy-start
  7.1 1.0 %copy-done = f32[126,400]{0,1:T(8,128)S(1)} copy-done((f32[126,400]{0,1:T(8,128)S(1)}, f32[126,400]{0,1:T(8,128)}, u32[]{:S(2)}) %copy-start) | copy-done | bytes 201624
  8.0 0.0 copy-start.2
  8.0 0.0 copy-start.3
  8.0 0.1 shard_map.46.own
  8.2 0.0 copy-start.1
  8.9 0.0 copy-done.2
  8.9 0.0 copy-done.3
  8.9 0.1 fusion
  9.0 0.1 div.11
  9.1 0.1 broadcast_in_dim.2.weight
  9.2 0.0 copy-done.1
  9.2 0.1 shard_map.47.own_scaled
  9.3 0.3 %shard_map.48.own_own = f32[126,126]{1,0:T(8,128)S(1)} custom-call(bf16[2,126,400]{2,1,0:T(8,128)(2,1)S(1)} %shard_map.46.own, bf16[2,400,128]{2,1,0:T(8,128)(2,1)S(1)} %shard_map.47.own_scaled), custom_call_target="tpu_custom_call" | custom-call | flops 1000 | bytes 1000 | tf_op jit(solution)/shard_map/pallas_call | solution.py:264
  9.5 3.5 %collective-permute-done.2.refs_2_ = f32[400,126]{1,0:T(8,128)S(1)} collective-permute-done((f32[400,126]{1,0:T(8,128)}, f32[400,126]{1,0:T(8,128)S(1)}, u32[]{:S(2)}, u32[]{:S(2)}) %collective-permute-start.2) | collective-permute-done | bytes 201632 | tf_op jit(solution)/shard_map/ppermute | solution.py:75
  13.0 0.0 collective-permute-done.1.refs_1_
  13.0 0.1 collective-permute-done.refs_0_
  13.1 0.3 %shard_map.49 = (bf16[2,126,400]{2,1,0:T(8,128)(2,1)S(1)}, bf16[2,126,400]{2,1,0:T(8,128)(2,1)S(1)}, bf16[2,400,128]{2,1,0:T(8,128)(2,1)S(1)}, bf16[2,400,128]{2,1,0:T(8,128)(2,1)S(1)}) custom-call(f32[400,126]{1,0:T(8,128)S(1)} %broadcast_in_dim.2.weight, f32[400,126]{1,0:T(8,128)S(1)} %collective-permute-done.refs_0_, ...), custom_call_target="tpu_custom_call" | custom-call | flops 1000 | bytes 1000 | tf_op jit(solution)/shard_map/pallas_call | solution.py:264
  13.4 0.6 %shard_map.51 = (f32[189,126]{1,0:T(8,128)S(1)}, f32[189,126]{1,0:T(8,128)S(1)}) custom-call(bf16[2,126,400]{2,1,0:T(8,128)(2,1)S(1)} %get-tuple-element.19.far, bf16[2,126,400]{2,1,0:T(8,128)(2,1)S(1)} %get-tuple-element.20.xp, bf16[2,400,128]{2,1,0:T(8,128)(2,1)S(1)} %get-tuple-element.24.xp_scaled, bf16[2,400,128]{2,1,0:T(8,128)(2,1)S(1)} %get-tuple-element.21.zn_scaled), custom_call_target="tpu_custom_call" | custom-call | flops 1000 | bytes 1000 | tf_op jit(solution)/shard_map/pallas_call | solution.py:264
  14.1 0.3 %collective-permute-start.4 = (f32[189,126]{1,0:T(8,128)S(1)}, f32[189,126]{1,0:T(8,128)S(1)}, u32[]{:S(2)}, u32[]{:S(2)}) collective-permute-start(f32[189,126]{1,0:T(8,128)S(1)} %get-tuple-element.26), channel_id=1, source_target_pairs={{0,1},{1,0},{2,3},{3,2},{4,5},{5,4},{6,7},{7,6},{8,9},{9,8},{10,11... | collective-permute-start | bytes 285776 | tf_op jit(solution)/shard_map/ppermute | solution.py:75
  14.4 0.5 %shard_map.50 = (f32[315,126]{1,0:T(8,128)S(1)}, f32[315,126]{1,0:T(8,128)S(1)}) custom-call(bf16[2,126,400]{2,1,0:T(8,128)(2,1)S(1)} %shard_map.46.own, bf16[2,400,128]{2,1,0:T(8,128)(2,1)S(1)} %shard_map.47.own_scaled, f32[126,126]{1,0:T(8,128)S(1)} %shard_map.48.own_own, bf16[2,126,400]{2,1,0:T(8,128)(2,1)S(1)} %get-tuple-element.19.far, ...), custom_call_target="tpu_custom_call" | custom-call | flops 1000 | bytes 1000 | tf_op jit(solution)/shard_map/pallas_call | solution.py:264
  14.9 0.4 %collective-permute-start.3 = (f32[315,126]{1,0:T(8,128)S(1)}, f32[315,126]{1,0:T(8,128)S(1)}, u32[]{:S(2)}, u32[]{:S(2)}) collective-permute-start(f32[315,126]{1,0:T(8,128)S(1)} %get-tuple-element.23), channel_id=1, source_target_pairs={{0,1},{1,0},{2,3},{3,2},{4,5},{5,4},{6,7},{7,6},{8,9},{9,8},{10,11... | collective-permute-start | bytes 476288 | tf_op jit(solution)/shard_map/ppermute | solution.py:75
  15.3 0.2 collective-permute-done.4.theirs
  15.4 1.7 %collective-permute-start.5 = (f32[126,126]{1,0:T(8,128)S(1)}, f32[126,126]{1,0:T(8,128)S(1)}, u32[]{:S(2)}, u32[]{:S(2)}) collective-permute-start(f32[126,126]{1,0:T(8,128)S(1)} %get-tuple-element.27), channel_id=1, source_target_pairs={{0,3},{1,2},{2,1},{3,0},{4,7},{5,13},{6,14},{7,4},{8,11},{9,10},{1... | collective-permute-start | bytes 190520 | tf_op jit(solution)/shard_map/ppermute | solution.py:75
  17.1 1.9 %collective-permute-start.6 = (f32[63,126]{1,0:T(8,128)S(1)}, f32[63,126]{1,0:T(8,128)S(1)}, u32[]{:S(2)}, u32[]{:S(2)}) collective-permute-start(f32[63,126]{1,0:T(8,128)S(1)} %get-tuple-element.28), channel_id=1, source_target_pairs={{0,4},{1,5},{2,6},{3,7},{4,0},{5,1},{6,2},{7,3},{8,12},{9,13},{10,... | collective-permute-start | bytes 95264 | tf_op jit(solution)/shard_map/ppermute | solution.py:75
  19.0 2.0 %collective-permute-done.6.half_tile = f32[63,126]{1,0:T(8,128)S(1)} collective-permute-done((f32[63,126]{1,0:T(8,128)S(1)}, f32[63,126]{1,0:T(8,128)S(1)}, u32[]{:S(2)}, u32[]{:S(2)}) %collective-permute-start.6) | collective-permute-done | bytes 31784 | tf_op jit(solution)/shard_map/ppermute | solution.py:75
  21.0 0.0 collective-permute-done.3.theirs
  21.0 0.0 collective-permute-done.5.tile
  21.0 0.7 %shard_map.53 = f32[315,126]{1,0:T(8,128)} custom-call(f32[315,126]{1,0:T(8,128)S(1)} %get-tuple-element.22.mine, f32[315,126]{1,0:T(8,128)S(1)} %collective-permute-done.3.theirs, f32[126,126]{1,0:T(8,128)S(1)} %collective-permute-done.5.tile, f32[63,126]{1,0:T(8,128)S(1)} %collective-permute-done.6.half_tile), custom_call_target="tpu_custom_call" | custom-call | flops 1000 | bytes 1000 | tf_op jit(solution)/shard_map/pallas_call | solution.py:264
  (1 shorter events, 0.0 us)
Async XLA Ops:
  0.0 13.0 %collective-permute-start.2 = (f32[400,126]{1,0:T(8,128)}, f32[400,126]{1,0:T(8,128)S(1)}, u32[]{:S(2)}, u32[]{:S(2)}) collective-permute-start(f32[400,126]{1,0:T(8,128)} %bitcast.3), channel_id=1, source_target_pairs={{0,6},{1,9},{2,4},{3,11},{4,0},{5,13},{6,2},{7,15},{8,14},{9,1},{1... | collective-permute-start | bytes 604808 | tf_op jit(solution)/shard_map/ppermute | solution.py:75
  4.0 9.0 %collective-permute-start.1 = (f32[400,126]{1,0:T(8,128)}, f32[400,126]{1,0:T(8,128)S(1)}, u32[]{:S(2)}, u32[]{:S(2)}) collective-permute-start(f32[400,126]{1,0:T(8,128)} %bitcast.4), channel_id=1, source_target_pairs={{0,2},{1,7},{2,0},{3,5},{4,6},{5,1},{6,4},{7,3},{8,10},{9,15},{10,... | collective-permute-start | bytes 604808 | tf_op jit(solution)/shard_map/ppermute | solution.py:75
  4.5 8.6 %collective-permute-start = (f32[400,126]{1,0:T(8,128)}, f32[400,126]{1,0:T(8,128)S(1)}, u32[]{:S(2)}, u32[]{:S(2)}) collective-permute-start(f32[400,126]{1,0:T(8,128)} %bitcast.5), channel_id=1, source_target_pairs={{0,8},{1,3},{2,10},{3,1},{4,12},{5,7},{6,14},{7,5},{8,0},{9,11},{1... | collective-permute-start | bytes 604808 | tf_op jit(solution)/shard_map/ppermute | solution.py:75
  7.1 1.0 %copy-start = (f32[126,400]{0,1:T(8,128)S(1)}, f32[126,400]{0,1:T(8,128)}, u32[]{:S(2)}) copy-start(f32[126,400]{0,1:T(8,128)} %param.4) | copy-start | bytes 604804
  8.0 0.8 %copy-start.2 = (f32[200]{0:T(256)S(1)}, f32[200]{0:T(256)}, u32[]{:S(2)}) copy-start(f32[200]{0:T(256)} %param.6) | copy-start | bytes 2404
  8.0 0.9 %copy-start.3 = (f32[2]{0:T(128)S(1)}, f32[2]{0:T(128)}, u32[]{:S(2)}) copy-start(f32[2]{0:T(128)} %param.5) | copy-start | bytes 28
  8.2 1.0 %copy-start.1 = (f32[126,400]{0,1:T(8,128)S(1)}, f32[126,400]{0,1:T(8,128)}, u32[]{:S(2)}) copy-start(f32[126,400]{0,1:T(8,128)} %param.4) | copy-start | bytes 604804
  14.1 1.4 %collective-permute-start.4 = (f32[189,126]{1,0:T(8,128)S(1)}, f32[189,126]{1,0:T(8,128)S(1)}, u32[]{:S(2)}, u32[]{:S(2)}) collective-permute-start(f32[189,126]{1,0:T(8,128)S(1)} %get-tuple-element.26), channel_id=1, source_target_pairs={{0,1},{1,0},{2,3},{3,2},{4,5},{5,4},{6,7},{7,6},{8,9},{9,8},{10,11... | collective-permute-start | bytes 285776 | tf_op jit(solution)/shard_map/ppermute | solution.py:75
  14.9 6.1 %collective-permute-start.3 = (f32[315,126]{1,0:T(8,128)S(1)}, f32[315,126]{1,0:T(8,128)S(1)}, u32[]{:S(2)}, u32[]{:S(2)}) collective-permute-start(f32[315,126]{1,0:T(8,128)S(1)} %get-tuple-element.23), channel_id=1, source_target_pairs={{0,1},{1,0},{2,3},{3,2},{4,5},{5,4},{6,7},{7,6},{8,9},{9,8},{10,11... | collective-permute-start | bytes 476288 | tf_op jit(solution)/shard_map/ppermute | solution.py:75
  15.4 5.6 %collective-permute-start.5 = (f32[126,126]{1,0:T(8,128)S(1)}, f32[126,126]{1,0:T(8,128)S(1)}, u32[]{:S(2)}, u32[]{:S(2)}) collective-permute-start(f32[126,126]{1,0:T(8,128)S(1)} %get-tuple-element.27), channel_id=1, source_target_pairs={{0,3},{1,2},{2,1},{3,0},{4,7},{5,13},{6,14},{7,4},{8,11},{9,10},{1... | collective-permute-start | bytes 190520 | tf_op jit(solution)/shard_map/ppermute | solution.py:75
  17.1 3.9 %collective-permute-start.6 = (f32[63,126]{1,0:T(8,128)S(1)}, f32[63,126]{1,0:T(8,128)S(1)}, u32[]{:S(2)}, u32[]{:S(2)}) collective-permute-start(f32[63,126]{1,0:T(8,128)S(1)} %get-tuple-element.28), channel_id=1, source_target_pairs={{0,4},{1,5},{2,6},{3,7},{4,0},{5,1},{6,2},{7,3},{8,12},{9,13},{10,... | collective-permute-start | bytes 95264 | tf_op jit(solution)/shard_map/ppermute | solution.py:75
